TPU v7x, 32 devices: a whole 2x2x4 slice. The times are simulated.
32 devices in a mesh: grp: 2 (over x), exp: 16 (over z, y, core).
Axes of the slice: x: 2, y: 2, z: 4, core: 2. Of those that a mesh axis runs over, the one named last changes fastest.
Arguments:
- tokens: bfloat16 [4096, 4096], P(('grp', 'exp')), parts along dimension 0, may hold values from -6 to 6
- upstream: bfloat16 [4096, 4096], P(('grp', 'exp')), parts along dimension 0, may hold values from -6 to 6
- expert_ids: int32 [4096, 8], P(('grp', 'exp')), parts along dimension 0, may hold values from 0 to 127, as said below
- gate_values: float32 [4096, 8], P(('grp', 'exp')), parts along dimension 0, may hold values from 0.05 to 1
- w_gate: bfloat16 [16, 192, 4096], P('exp'), may hold values from -0.09375 to 0.09375
- w_up: bfloat16 [16, 192, 4096], P('exp'), may hold values from -0.09375 to 0.09375
- w_down: bfloat16 [16, 192, 4096], P('exp'), may hold values from -0.15625 to 0.15625
Outputs:
- d_tokens: bfloat16 [4096, 4096], P(('grp', 'exp')), parts along dimension 0
- grad_gate: bfloat16 [32, 192, 4096], P(('grp', 'exp')), parts along dimension 0
- grad_up: bfloat16 [32, 192, 4096], P(('grp', 'exp')), parts along dimension 0
- grad_down: bfloat16 [32, 192, 4096], P(('grp', 'exp')), parts along dimension 0
There are 2 independent parts, one for each index of `grp`. A program takes and returns all parts, laid end to end along the dimension named above; an argument that names none is the same for every part. Nothing has to cross between parts.
Inputs may be any that keep to these rules, and one draw needn't show every extreme that they name: `expert_ids`: each token names 8 different experts, at most one of them below 2. Among one device's 128 tokens at most 16 name any one expert below 2, and some expert below 2 is named by exactly 16 tokens on every device.
All inputs are finite; a program needn't handle non-finite values.
Results may differ from a plain program's by a relative error of at most 0.0064.
Values may be sent and summed in bfloat16 or wider, within the bound.
No kernel may reach another device: no remote copies, remote signals or barrier semaphores. Data moves between devices by JAX's collectives and lax.ppermute only.
A program may use at most 128 MiB of HBM per device.

v0:
```python
import jax
import jax.numpy as jnp
from jax import lax
from jax.sharding import PartitionSpec as P

TILES = 8
CAP = 16


def contract(left, right, left_dim, right_dim):
    return lax.dot_general(
        left, right, (((left_dim,), (right_dim,)), ((), ())), preferred_element_type=jnp.float32
    )


def on_device(tokens, upstream, expert_ids, gate_values, w_gate, w_up, w_down):
    tiles = TILES
    window = lax.axis_size("exp") // tiles
    width = tokens.shape[1]
    inside = expert_ids < window
    chosen = jnp.sum(jnp.where(inside, expert_ids, 0), axis=1)
    has_slot = jnp.any(inside, axis=1)
    weight = jnp.sum(jnp.where(inside, gate_values, 0.0), axis=1)
    scaled = (upstream.astype(jnp.float32) * weight[:, None]).astype(jnp.bfloat16)
    member = (chosen[:, None] == jnp.arange(window)[None, :]) & has_slot[:, None]
    ranking = jnp.cumsum(member.astype(jnp.int32), axis=0) - 1
    rank = jnp.sum(jnp.where(member, ranking, 0), axis=1)
    slot = jnp.where(has_slot, chosen * CAP + rank, -1)
    select = (slot[None, :] == jnp.arange(window * CAP)[:, None]).astype(jnp.bfloat16)
    packed_x = jnp.dot(select, tokens, preferred_element_type=jnp.float32).astype(jnp.bfloat16)
    packed_z = jnp.dot(select, scaled, preferred_element_type=jnp.float32).astype(jnp.bfloat16)
    total_rows = window * tiles * CAP

    def spread(packed):
        return jnp.broadcast_to(
            packed.reshape(window, 1, CAP, width), (window, tiles, CAP, width)
        ).reshape(total_rows, width)

    row_x, row_z = (
        lax.all_to_all(spread(packed_x), "exp", split_axis=0, concat_axis=0, tiled=True),
        lax.all_to_all(spread(packed_z), "exp", split_axis=0, concat_axis=0, tiled=True),
    )
    gate_tile = w_gate[0]
    up_tile = w_up[0]
    down_tile = w_down[0]
    pre_gate = contract(row_x, gate_tile, 1, 1)
    pre_up = contract(row_x, up_tile, 1, 1)
    sigma = jax.nn.sigmoid(pre_gate)
    active = pre_gate * sigma
    hidden = (active * pre_up).astype(jnp.bfloat16)
    d_hidden = contract(row_z, down_tile, 1, 1)
    d_gate = (d_hidden * pre_up * sigma * (1.0 + pre_gate * (1.0 - sigma))).astype(jnp.bfloat16)
    d_up = (d_hidden * active).astype(jnp.bfloat16)
    grad_gate = contract(d_gate, row_x, 0, 0).astype(jnp.bfloat16)
    grad_up = contract(d_up, row_x, 0, 0).astype(jnp.bfloat16)
    grad_down = contract(hidden, row_z, 0, 0).astype(jnp.bfloat16)
    partial_value = jnp.dot(d_gate, gate_tile, preferred_element_type=jnp.float32)
    partial_value = (
        partial_value + jnp.dot(d_up, up_tile, preferred_element_type=jnp.float32)
    ).astype(jnp.bfloat16)
    returned = lax.all_to_all(partial_value, "exp", split_axis=0, concat_axis=0, tiled=True)
    summed = jnp.sum(returned.reshape(window, tiles, CAP, width).astype(jnp.float32), axis=1)
    summed = summed.astype(jnp.bfloat16).reshape(window * CAP, width)
    d_tokens = contract(select, summed, 0, 0).astype(jnp.bfloat16)
    return (d_tokens, grad_gate[None], grad_up[None], grad_down[None])


def solution(mesh):
    placed = (
        P(("grp", "exp"), None),
        P(("grp", "exp"), None),
        P(("grp", "exp"), None),
        P(("grp", "exp"), None),
        P("exp", None, None),
        P("exp", None, None),
        P("exp", None, None),
    )
    return jax.shard_map(
        on_device,
        mesh=mesh,
        in_specs=placed,
        out_specs=(
            P(("grp", "exp"), None),
            P(("grp", "exp"), None, None),
            P(("grp", "exp"), None, None),
            P(("grp", "exp"), None, None),
        ),
        check_vma=False,
    )
```

profile of v0, /device:TPU:13, one launch (start us, length us, event | category | flops | bytes accessed | tf_op | source)
XLA Modules:
  0.0 175.6 jit_solution(13059236022716602169)
XLA Ops:
  0.6 0.0 copy-start
  0.6 0.8 fusion.22
  1.5 0.7 select_reduce_fusion.2
  2.2 0.1 fusion.16
  2.3 0.2 reduce_window_sum.11
  2.5 0.2 select_reduce_fusion
  2.6 1.5 convolution_convert_fusion.4
  4.1 1.5 broadcast_in_dim.52
  5.7 6.7 %all-to-all-start.1 = ((bf16[16,16,4096]{2,1,0:T(8,128)(2,1)}), bf16[16,16,4096]{2,1,0:T(8,128)(2,1)}, u32[]{:S(2)}, u32[]{:S(2)}) async-start(bf16[16,16,4096]{2,1,0:T(8,128)(2,1)} %bitcast.43), calls=%async_computation.1 | async-start | bytes 4194304 | tf_op jit(solution)/shard_map/all_to_all | solution.py:40
  12.4 0.0 copy-done.7
  12.4 0.0 copy-done.8
  12.4 0.0 copy-done.2
  12.4 0.4 convolution_convert_fusion.5
  12.8 47.1 %all-to-all-done.1 = bf16[16,16,4096]{2,1,0:T(8,128)(2,1)} async-done(((bf16[16,16,4096]{2,1,0:T(8,128)(2,1)}), bf16[16,16,4096]{2,1,0:T(8,128)(2,1)}, u32[]{:S(2)}, u32[]{:S(2)}) %all-to-all-start.1) | async-done | bytes 2097184 | tf_op jit(solution)/shard_map/all_to_all | solution.py:40
  59.9 1.6 broadcast_in_dim.50
  61.5 4.9 %all-to-all-start = ((bf16[16,16,4096]{2,1,0:T(8,128)(2,1)}), bf16[16,16,4096]{2,1,0:T(8,128)(2,1)}, u32[]{:S(2)}, u32[]{:S(2)}) async-start(bf16[16,16,4096]{2,1,0:T(8,128)(2,1)} %bitcast.44), calls=%async_computation | async-start | bytes 4194304 | tf_op jit(solution)/shard_map/all_to_all | solution.py:41
  66.4 2.6 %fusion.6 = f32[256,192]{0,1:T(8,128)S(1)} fusion(bf16[256,4096]{1,0:T(8,128)(2,1)} %bitcast.6, bf16[1,192,4096]{2,1,0:T(8,128)(2,1)S(1)} %copy-done), kind=kOutput, calls=%fused_computation.15 | convolution fusion | flops 402653184 | bytes 3866624 | tf_op jit(solution)/shard_map/dot_general | solution.py:11
  69.0 2.5 %fusion.9 = f32[256,192]{0,1:T(8,128)S(1)} fusion(bf16[256,4096]{1,0:T(8,128)(2,1)} %bitcast.6, bf16[1,192,4096]{2,1,0:T(8,128)(2,1)S(1)} %copy-done.1), kind=kOutput, calls=%fused_computation.18 | convolution fusion | flops 402653184 | bytes 3866624 | tf_op jit(solution)/shard_map/dot_general | solution.py:11
  71.5 42.4 %all-to-all-done = bf16[16,16,4096]{2,1,0:T(8,128)(2,1)} async-done(((bf16[16,16,4096]{2,1,0:T(8,128)(2,1)}), bf16[16,16,4096]{2,1,0:T(8,128)(2,1)}, u32[]{:S(2)}, u32[]{:S(2)}) %all-to-all-start) | async-done | bytes 2097184 | tf_op jit(solution)/shard_map/all_to_all | solution.py:41
  113.9 2.9 %multiply_convert_fusion.3 = (bf16[256,192]{0,1:T(8,128)(2,1)S(1)}, bf16[256,192]{0,1:T(8,128)(2,1)S(1)}) fusion(f32[256,192]{0,1:T(8,128)S(1)} %fusion.6, f32[256,192]{0,1:T(8,128)S(1)} %fusion.9, bf16[256,4096]{1,0:T(8,128)(2,1)} %bitcast.2, bf16[1,192,4096]{2,1,0:T(8,128)(2,1)} %param.13), kind=kOutput, calls=%fused_computation.24 | convolution fusion | flops 403292160 | bytes 4259840 | tf_op jit(solution)/shard_map/dot_general | solution.py:11
  116.8 0.0 copy-start.5
  116.8 0.0 copy-start.3
  116.8 0.7 fusion.4
  117.6 2.1 %fusion = bf16[256,4096]{1,0:T(8,128)(2,1)} fusion(f32[256,4096]{1,0:T(8,128)S(1)} %fusion.4, bf16[256,192]{0,1:T(8,128)(2,1)S(1)} %get-tuple-element.4, bf16[1,192,4096]{2,1,0:T(8,128)(2,1)S(1)} %copy-done.1), kind=kOutput, calls=%fused_computation.1 | convolution fusion | flops 404750336 | bytes 7962624 | tf_op jit(solution)/shard_map/dot_general | solution.py:59
  119.7 5.0 %all-to-all-start.2 = ((bf16[16,16,4096]{2,1,0:T(8,128)(2,1)}), bf16[16,16,4096]{2,1,0:T(8,128)(2,1)}, u32[]{:S(2)}, u32[]{:S(2)}) async-start(bf16[16,16,4096]{2,1,0:T(8,128)(2,1)} %bitcast.45), calls=%async_computation.2 | async-start | bytes 4194304 | tf_op jit(solution)/shard_map/all_to_all | solution.py:61
  124.8 0.0 copy-start.4
  124.8 3.4 %fusion.1 = bf16[1,192,4096]{2,1,0:T(8,128)(2,1)} fusion(bf16[256,192]{0,1:T(8,128)(2,1)S(1)} %copy-done.6, bf16[256,4096]{1,0:T(8,128)(2,1)} %bitcast.6), kind=kOutput, calls=%fused_computation.6 | convolution fusion | flops 403439616 | bytes 3768320 | tf_op jit(solution)/shard_map/dot_general | solution.py:11
  128.1 3.3 %fusion.2 = bf16[1,192,4096]{2,1,0:T(8,128)(2,1)} fusion(bf16[256,192]{0,1:T(8,128)(2,1)S(1)} %copy-done.4, bf16[256,4096]{1,0:T(8,128)(2,1)} %bitcast.6), kind=kOutput, calls=%fused_computation.7 | convolution fusion | flops 403439616 | bytes 3768320 | tf_op jit(solution)/shard_map/dot_general | solution.py:11
  131.5 3.3 %fusion.3 = bf16[1,192,4096]{2,1,0:T(8,128)(2,1)} fusion(bf16[256,4096]{1,0:T(8,128)(2,1)} %bitcast.2, f32[256,192]{0,1:T(8,128)S(1)} %fusion.9, f32[256,192]{0,1:T(8,128)S(1)} %fusion.6), kind=kOutput, calls=%fused_computation.8 | convolution fusion | flops 403734528 | bytes 4063232 | tf_op jit(solution)/shard_map/dot_general | solution.py:11
  134.8 37.5 %all-to-all-done.2 = bf16[16,16,4096]{2,1,0:T(8,128)(2,1)} async-done(((bf16[16,16,4096]{2,1,0:T(8,128)(2,1)}), bf16[16,16,4096]{2,1,0:T(8,128)(2,1)}, u32[]{:S(2)}, u32[]{:S(2)}) %all-to-all-start.2) | async-done | bytes 2097184 | tf_op jit(solution)/shard_map/all_to_all | solution.py:61
  172.3 1.9 %bitcast_reduce_fusion = bf16[2,16,4096]{2,1,0:T(8,128)(2,1)S(1)} fusion(bf16[16,16,4096]{2,1,0:T(8,128)(2,1)} %all-to-all-done.2), kind=kLoop, calls=%fused_computation.11 | loop fusion | flops 917504 | bytes 2359296 | tf_op jit(solution)/shard_map/reduce_sum | solution.py:62
  174.2 1.5 convolution_convert_fusion.3
  (13 shorter events, 0.0 us)
Async XLA Ops:
  0.6 65.8 %copy-start = (bf16[1,192,4096]{2,1,0:T(8,128)(2,1)S(1)}, bf16[1,192,4096]{2,1,0:T(8,128)(2,1)}, u32[]{:S(2)}) copy-start(bf16[1,192,4096]{2,1,0:T(8,128)(2,1)} %param.11) | copy-start | bytes 4718596
  5.7 6.7 %copy-start.7 = (s32[128,8]{0,1:T(8,128)S(1)}, s32[128,8]{0,1:T(8,128)}, u32[]{:S(2)}) copy-start(s32[128,8]{0,1:T(8,128)} %param.9) | copy-start | bytes 12292
  5.7 6.7 %copy-start.8 = (f32[128,8]{0,1:T(8,128)S(1)}, f32[128,8]{0,1:T(8,128)}, u32[]{:S(2)}) copy-start(f32[128,8]{0,1:T(8,128)} %param.10) | copy-start | bytes 12292
  5.7 6.7 %copy-start.2 = (bf16[128,4096]{1,0:T(8,128)(2,1)S(1)}, bf16[128,4096]{1,0:T(8,128)(2,1)}, u32[]{:S(2)}) copy-start(bf16[128,4096]{1,0:T(8,128)(2,1)} %param.8) | copy-start | bytes 3145732
  5.7 54.2 %all-to-all-start.1 = ((bf16[16,16,4096]{2,1,0:T(8,128)(2,1)}), bf16[16,16,4096]{2,1,0:T(8,128)(2,1)}, u32[]{:S(2)}, u32[]{:S(2)}) async-start(bf16[16,16,4096]{2,1,0:T(8,128)(2,1)} %bitcast.43), calls=%async_computation.1 | async-start | bytes 4194304 | tf_op jit(solution)/shard_map/all_to_all | solution.py:40
  61.5 52.4 %all-to-all-start = ((bf16[16,16,4096]{2,1,0:T(8,128)(2,1)}), bf16[16,16,4096]{2,1,0:T(8,128)(2,1)}, u32[]{:S(2)}, u32[]{:S(2)}) async-start(bf16[16,16,4096]{2,1,0:T(8,128)(2,1)} %bitcast.44), calls=%async_computation | async-start | bytes 4194304 | tf_op jit(solution)/shard_map/all_to_all | solution.py:41
  66.4 2.6 %copy-start.1 = (bf16[1,192,4096]{2,1,0:T(8,128)(2,1)S(1)}, bf16[1,192,4096]{2,1,0:T(8,128)(2,1)}, u32[]{:S(2)}) copy-start(bf16[1,192,4096]{2,1,0:T(8,128)(2,1)} %param.12) | copy-start | bytes 4718596
  116.8 0.8 copy-start.5
  116.8 0.8 copy-start.3
  119.7 5.0 %copy-start.6 = (bf16[256,192]{0,1:T(8,128)(2,1)S(1)}, bf16[256,192]{0,1:T(8,128)(2,1)}, u32[]{:S(2)}) copy-start(bf16[256,192]{0,1:T(8,128)(2,1)} %copy-done.5) | copy-start | bytes 294916
  119.7 52.6 %all-to-all-start.2 = ((bf16[16,16,4096]{2,1,0:T(8,128)(2,1)}), bf16[16,16,4096]{2,1,0:T(8,128)(2,1)}, u32[]{:S(2)}, u32[]{:S(2)}) async-start(bf16[16,16,4096]{2,1,0:T(8,128)(2,1)} %bitcast.45), calls=%async_computation.2 | async-start | bytes 4194304 | tf_op jit(solution)/shard_map/all_to_all | solution.py:61
  124.8 3.4 %copy-start.4 = (bf16[256,192]{0,1:T(8,128)(2,1)S(1)}, bf16[256,192]{0,1:T(8,128)(2,1)}, u32[]{:S(2)}) copy-start(bf16[256,192]{0,1:T(8,128)(2,1)} %copy-done.3) | copy-start | bytes 294916
where the time goes:
time: 176 us
  waiting for transfers between devices  127 us (72%)
  matrix products  24.2 us (14%)
  starting transfers between devices  16.6 us (9%)
  other arithmetic  3.88 us (2%)
  local copies, waits for them, and re-layouts  3.15 us (2%)
    all_to_all x1, waiting for transfers between devices, on_device(): lax.all_to_all(spread(packed_x), 'exp', split_axis=0, concat_axis=0, tile...  47.1 us
    all_to_all x1, waiting for transfers between devices, on_device(): lax.all_to_all(spread(packed_z), 'exp', split_axis=0, concat_axis=0, tile...  42.4 us
    all_to_all x1, waiting for transfers between devices, on_device(): lax.all_to_all(partial_value, 'exp', split_axis=0, concat_axis=0, tiled=T...  37.5 us
    dot_general x7, matrix products, contract(): lax.dot_general(left, right, (((left_dim,), (right_dim,)), ((), ())), pre...  19.4 us
    all_to_all x1, starting transfers between devices, on_device(): lax.all_to_all(spread(packed_x), 'exp', split_axis=0, concat_axis=0, tile...  6.69 us
    all_to_all x1, starting transfers between devices, on_device(): lax.all_to_all(partial_value, 'exp', split_axis=0, concat_axis=0, tiled=T...  5.04 us
    all_to_all x1, starting transfers between devices, on_device(): lax.all_to_all(spread(packed_z), 'exp', split_axis=0, concat_axis=0, tile...  4.91 us
  transfers between devices with their start and end apart: 3, of which 3 were waited for; matrix products, arithmetic and copies ran while one was open for 9% of the time, Pallas kernels for 0%

commit v1 on v0

v1 whole, which is shorter than its diff:
```python
import functools

import jax
import jax.numpy as jnp
from jax import lax
from jax.experimental import pallas as pl
from jax.experimental.pallas import tpu as pltpu
from jax.sharding import PartitionSpec as P

TILES = 8
CAP = 16
BF = jnp.bfloat16
F32 = jnp.float32
VMEM = pl.BlockSpec(memory_space=pltpu.VMEM)
SMEM = pl.BlockSpec(memory_space=pltpu.SMEM)
PARAMS = pltpu.CompilerParams(vmem_limit_bytes=48 * 1024 * 1024)


def dot(left, right, left_dim, right_dim):
    return lax.dot_general(
        left, right, (((left_dim,), (right_dim,)), ((), ())), preferred_element_type=F32
    )


def pack_kernel(window, own_ref, ids_ref, gate_ref, tokens_ref, upstream_ref, *out):
    select_ref, blocks = out[0], out[1:]
    count, width = tokens_ref.shape
    ids = ids_ref[...]
    inside = ids < window
    chosen = jnp.sum(jnp.where(inside, ids, 0).astype(F32), axis=1, keepdims=True).astype(jnp.int32)
    has_slot = jnp.sum(inside.astype(F32), axis=1, keepdims=True) > 0.0
    weight = jnp.sum(jnp.where(inside, gate_ref[...], 0.0), axis=1, keepdims=True)
    shift = chosen - own_ref[0]
    shift = jnp.where(shift < 0, shift + window, shift)
    lanes = window * CAP
    lane = lax.broadcasted_iota(jnp.int32, (count, lanes), 1)
    first = shift * CAP
    member = ((lane >= first) & (lane < first + CAP) & has_slot).astype(F32)
    row = lax.broadcasted_iota(jnp.int32, (count, count), 0)
    col = lax.broadcasted_iota(jnp.int32, (count, count), 1)
    before = (col < row).astype(BF)
    earlier = dot(before, member.astype(BF), 1, 0)
    position = lane - first
    select = ((member > 0.0) & (position.astype(F32) == earlier)).astype(BF)
    select_ref[...] = select
    step = min(1024, width)
    for at in range(0, width, step):
        cols = pl.ds(at, step)
        x = dot(select, tokens_ref[:, cols], 0, 0).astype(BF)
        scaled = (upstream_ref[:, cols].astype(F32) * weight).astype(BF)
        z = dot(select, scaled, 0, 0).astype(BF)
        for k in range(window):
            part = slice(k * CAP, (k + 1) * CAP)
            blocks[k][:CAP, cols] = x[part]
            blocks[k][CAP:, cols] = z[part]


def expert_kernel(count, *refs):
    blocks, refs = refs[:count], refs[count:]
    gate_ref, up_ref, down_ref, x_ref, z_ref, dg_ref, du_ref, hidden_ref = refs[:8]
    parts = refs[8:]
    for j, block in enumerate(blocks):
        x_ref[j * CAP : (j + 1) * CAP, :] = block[:CAP, :]
        z_ref[j * CAP : (j + 1) * CAP, :] = block[CAP:, :]
    x = x_ref[...]
    pre_gate = dot(x, gate_ref[...], 1, 1)
    pre_up = dot(x, up_ref[...], 1, 1)
    d_hidden = dot(z_ref[...], down_ref[...], 1, 1)
    sigma = 1.0 / (1.0 + jnp.exp(-pre_gate))
    active = pre_gate * sigma
    hidden_ref[...] = (active * pre_up).astype(BF)
    d_gate = (d_hidden * pre_up * sigma * (1.0 + pre_gate * (1.0 - sigma))).astype(BF)
    d_up = (d_hidden * active).astype(BF)
    dg_ref[...] = d_gate
    du_ref[...] = d_up
    half = count * CAP // 2
    width = gate_ref.shape[1]
    step = min(1024, width)
    for at in range(0, width, step):
        cols = pl.ds(at, step)
        value = dot(d_gate, gate_ref[:, cols], 1, 0) + dot(d_up, up_ref[:, cols], 1, 0)
        value = value.astype(BF)
        parts[0][:, cols] = value[:half]
        parts[1][:, cols] = value[half:]


def grad_kernel(count, *refs):
    out = refs[-1]
    total = None
    for j in range(count):
        term = dot(refs[j][...], refs[count + j][...], 0, 0)
        total = term if total is None else total + term
    out[...] = total.astype(BF)


def sum_kernel(terms, *refs):
    outs = refs[terms:]
    rows = outs[0].shape[0]
    for j, out in enumerate(outs):
        total = refs[0][j * rows : (j + 1) * rows, :].astype(F32)
        for ref in refs[1:terms]:
            total = total + ref[j * rows : (j + 1) * rows, :].astype(F32)
        out[...] = total.astype(BF)


def unpack_kernel(count, select_ref, *refs):
    out = refs[-1]
    width = out.shape[1]
    step = min(1024, width)
    for at in range(0, width, step):
        cols = pl.ds(at, step)
        rows = jnp.concatenate([refs[k][:, cols] for k in range(count)], axis=0)
        out[:, cols] = dot(select_ref[...], rows, 1, 0).astype(BF)


def call(kernel, out_shape, *args, smem=0):
    return pl.pallas_call(
        kernel,
        out_shape=out_shape,
        in_specs=[SMEM] * smem + [VMEM] * (len(args) - smem),
        out_specs=jax.tree.map(lambda _: VMEM, out_shape),
        compiler_params=PARAMS,
    )(*args)


def shape(*dims):
    return jax.ShapeDtypeStruct(dims, BF)


def grads(lefts, rights):
    count = len(lefts)
    hidden, width = lefts[0].shape[1], rights[0].shape[1]
    step = min(1024, width)
    return pl.pallas_call(
        functools.partial(grad_kernel, count),
        grid=(width // step,),
        out_shape=shape(hidden, width),
        in_specs=[pl.BlockSpec(a.shape, lambda i: (0, 0)) for a in lefts]
        + [pl.BlockSpec((a.shape[0], step), lambda i: (0, i)) for a in rights],
        out_specs=pl.BlockSpec((hidden, step), lambda i: (0, i)),
        compiler_params=PARAMS,
    )(*lefts, *rights)


def on_device(tokens, upstream, expert_ids, gate_values, w_gate, w_up, w_down):
    devices = lax.axis_size("exp")
    window = devices // TILES
    count, width = tokens.shape
    hidden = w_gate.shape[1]
    own = lax.axis_index("exp") // TILES

    def swap(a, bits):
        return lax.ppermute(a, "exp", [(i, i ^ bits) for i in range(devices)])

    def turn(a, k):
        return lax.ppermute(a, "exp", [(i, (i + k * TILES) % devices) for i in range(devices)])

    packed = call(
        functools.partial(pack_kernel, window),
        [shape(count, window * CAP)] + [shape(2 * CAP, width)] * window,
        own.astype(jnp.int32)[None],
        expert_ids,
        gate_values,
        tokens,
        upstream,
        smem=1,
    )
    select, packed = packed[0], packed[1:]
    blocks = [packed[0]] + [turn(packed[k], k) for k in range(1, window)]
    done = []
    for block in blocks:
        near = [block] + [swap(block, bits) for bits in (2, 4, 6)]
        both = near + [swap(b, 1) for b in near]
        rows = len(both) * CAP
        done.append(
            call(
                functools.partial(expert_kernel, len(both)),
                [shape(rows, width)] * 2 + [shape(rows, hidden)] * 3 + [shape(rows // 2, width)] * 2,
                *both,
                w_gate[0],
                w_up[0],
                w_down[0],
            )
        )
    returned = []
    for k, result in enumerate(done):
        mine, other = result[5:]
        pieces = call(functools.partial(sum_kernel, 2), [shape(CAP, width)] * 4, mine, swap(other, 1))
        pieces = [pieces[0]] + [swap(pieces[j], 2 * j) for j in (1, 2, 3)]
        whole = call(functools.partial(sum_kernel, 4), [shape(CAP, width)], *pieces)[0]
        returned.append(whole if k == 0 else turn(whole, window - k))
    grad_gate = grads([r[2] for r in done], [r[0] for r in done])
    grad_up = grads([r[3] for r in done], [r[0] for r in done])
    grad_down = grads([r[4] for r in done], [r[1] for r in done])
    d_tokens = call(
        functools.partial(unpack_kernel, window), shape(count, width), select, *returned
    )
    return (d_tokens, grad_gate[None], grad_up[None], grad_down[None])


def solution(mesh):
    rows = P(("grp", "exp"), None)
    tiles = P("exp", None, None)
    grown = P(("grp", "exp"), None, None)
    return jax.shard_map(
        on_device,
        mesh=mesh,
        in_specs=(rows, rows, rows, rows, tiles, tiles, tiles),
        out_specs=(rows, grown, grown, grown),
        check_vma=False,
    )
```

time: 176 us -> 79.3 us (0.45)
  the two profiles are of different devices: /device:TPU:13 before, /device:TPU:0 now
where the time goes in v1:
time: 79.3 us; the launch traced here: 79 us
  waiting for transfers between devices  27.8 us (35%)
  starting transfers between devices  24.8 us (31%)
  Pallas kernels  21.7 us (27%)
  local copies, waits for them, and re-layouts  4.02 us (5%)
    ppermute x22, waiting for transfers between devices, swap(): return lax.ppermute(a, 'exp', [(i, i ^ bits) for i in range(devices)])  18.7 us
    ppermute x22, starting transfers between devices, swap(): return lax.ppermute(a, 'exp', [(i, i ^ bits) for i in range(devices)])  17.4 us
    pallas_call x8, Pallas kernels, call(): pl.pallas_call(kernel, out_shape=out_shape, in_specs=[SMEM] * smem + [VME...  13.3 us
    ppermute x2, waiting for transfers between devices, turn(): lax.ppermute(a, 'exp', [(i, (i + k * TILES) % devices) for i in range(dev...  9.04 us
    pallas_call x3, Pallas kernels, grads(): pl.pallas_call(functools.partial(grad_kernel, count), grid=(width // step...  8.39 us
    ppermute x2, starting transfers between devices, turn(): lax.ppermute(a, 'exp', [(i, (i + k * TILES) % devices) for i in range(dev...  7.46 us
    unnamed x6, local copies, waits for them, and re-layouts  4.02 us
  transfers between devices with their start and end apart: 24, of which 6 were waited for; matrix products, arithmetic and copies ran while one was open for 0% of the time, Pallas kernels for 25%

profile of v1, /device:TPU:0, one launch (start us, length us, event | category | flops | bytes accessed | tf_op | source)
XLA Modules:
  0.0 79.0 jit_solution(8383511741407537627)
XLA Ops:
  0.6 0.8 copy.11.ids_ref
  1.4 0.8 copy.12.gate_ref
  2.2 1.2 %copy-done = bf16[128,4096]{1,0:T(8,128)(2,1)S(1)} copy-done((bf16[128,4096]{1,0:T(8,128)(2,1)S(1)}, bf16[128,4096]{1,0:T(8,128)(2,1)}, u32[]{:S(2)}) %copy-start) | copy-done | bytes 1048600
  3.5 1.2 %copy-done.1 = bf16[128,4096]{1,0:T(8,128)(2,1)S(1)} copy-done((bf16[128,4096]{1,0:T(8,128)(2,1)S(1)}, bf16[128,4096]{1,0:T(8,128)(2,1)}, u32[]{:S(2)}) %copy-start.1) | copy-done | bytes 1048600
  4.7 0.7 shard_map.102
  5.4 4.1 %collective-permute-start.11 = (bf16[32,4096]{1,0:T(8,128)(2,1)S(1)}, bf16[32,4096]{1,0:T(8,128)(2,1)S(1)}, u32[]{:S(2)}, u32[]{:S(2)}) collective-permute-start(bf16[32,4096]{1,0:T(8,128)(2,1)S(1)} %get-tuple-element.37), channel_id=1, source_target_pairs={{0,8},{1,9},{2,10},{3,11},{4,12},{5,13},{6,14},{7,15},{8,0},{9,1},... | collective-permute-start | bytes 786440 | tf_op jit(solution)/shard_map/ppermute | solution.py:156
  9.5 2.5 %collective-permute-start.2 = (bf16[32,4096]{1,0:T(8,128)(2,1)S(1)}, bf16[32,4096]{1,0:T(8,128)(2,1)S(1)}, u32[]{:S(2)}, u32[]{:S(2)}) collective-permute-start(bf16[32,4096]{1,0:T(8,128)(2,1)S(1)} %get-tuple-element.30.refs_0_), channel_id=1, source_target_pairs={{0,6},{1,7},{2,4},{3,5},{4,2},{5,3},{6,0},{7,1},{8,14},{9,15},{10,... | collective-permute-start | bytes 786440 | tf_op jit(solution)/shard_map/ppermute | solution.py:153
  12.5 9.0 %collective-permute-done.11.refs_0_ = bf16[32,4096]{1,0:T(8,128)(2,1)S(1)} collective-permute-done((bf16[32,4096]{1,0:T(8,128)(2,1)S(1)}, bf16[32,4096]{1,0:T(8,128)(2,1)S(1)}, u32[]{:S(2)}, u32[]{:S(2)}) %collective-permute-start.11) | collective-permute-done | bytes 262176 | tf_op jit(solution)/shard_map/ppermute | solution.py:156
  21.5 1.6 %collective-permute-start.14 = (bf16[32,4096]{1,0:T(8,128)(2,1)S(1)}, bf16[32,4096]{1,0:T(8,128)(2,1)S(1)}, u32[]{:S(2)}, u32[]{:S(2)}) collective-permute-start(bf16[32,4096]{1,0:T(8,128)(2,1)S(1)} %collective-permute-done.11.refs_0_), channel_id=1, source_target_pairs={{0,6},{1,7},{2,4},{3,5},{4,2},{5,3},{6,0},{7,1},{8,14},{9,15},{10,... | collective-permute-start | bytes 786440 | tf_op jit(solution)/shard_map/ppermute | solution.py:153
  23.1 1.4 %collective-permute-start.13 = (bf16[32,4096]{1,0:T(8,128)(2,1)S(1)}, bf16[32,4096]{1,0:T(8,128)(2,1)S(1)}, u32[]{:S(2)}, u32[]{:S(2)}) collective-permute-start(bf16[32,4096]{1,0:T(8,128)(2,1)S(1)} %collective-permute-done.11.refs_0_), channel_id=1, source_target_pairs={{0,4},{1,5},{2,6},{3,7},{4,0},{5,1},{6,2},{7,3},{8,12},{9,13},{10,... | collective-permute-start | bytes 786440 | tf_op jit(solution)/shard_map/ppermute | solution.py:153
  24.5 0.5 collective-permute-start.12
  25.0 1.6 %collective-permute-start = (bf16[32,4096]{1,0:T(8,128)(2,1)S(1)}, bf16[32,4096]{1,0:T(8,128)(2,1)S(1)}, u32[]{:S(2)}, u32[]{:S(2)}) collective-permute-start(bf16[32,4096]{1,0:T(8,128)(2,1)S(1)} %get-tuple-element.30.refs_0_), channel_id=1, source_target_pairs={{0,2},{1,3},{2,0},{3,1},{4,6},{5,7},{6,4},{7,5},{8,10},{9,11},{10,... | collective-permute-start | bytes 786440 | tf_op jit(solution)/shard_map/ppermute | solution.py:153
  26.6 3.2 %collective-permute-done.1.refs_2_ = bf16[32,4096]{1,0:T(8,128)(2,1)S(1)} collective-permute-done((bf16[32,4096]{1,0:T(8,128)(2,1)S(1)}, bf16[32,4096]{1,0:T(8,128)(2,1)S(1)}, u32[]{:S(2)}, u32[]{:S(2)}) %collective-permute-start.1) | collective-permute-done | bytes 262176 | tf_op jit(solution)/shard_map/ppermute | solution.py:153
  29.7 5.6 %collective-permute-done.14.refs_3_ = bf16[32,4096]{1,0:T(8,128)(2,1)S(1)} collective-permute-done((bf16[32,4096]{1,0:T(8,128)(2,1)S(1)}, bf16[32,4096]{1,0:T(8,128)(2,1)S(1)}, u32[]{:S(2)}, u32[]{:S(2)}) %collective-permute-start.14) | collective-permute-done | bytes 262176 | tf_op jit(solution)/shard_map/ppermute | solution.py:153
  35.4 4.2 %collective-permute-done.13.refs_2_ = bf16[32,4096]{1,0:T(8,128)(2,1)S(1)} collective-permute-done((bf16[32,4096]{1,0:T(8,128)(2,1)S(1)}, bf16[32,4096]{1,0:T(8,128)(2,1)S(1)}, u32[]{:S(2)}, u32[]{:S(2)}) %collective-permute-start.13) | collective-permute-done | bytes 262176 | tf_op jit(solution)/shard_map/ppermute | solution.py:153
  39.5 0.5 collective-permute-start.16
  40.1 2.3 %collective-permute-done.refs_1_ = bf16[32,4096]{1,0:T(8,128)(2,1)S(1)} collective-permute-done((bf16[32,4096]{1,0:T(8,128)(2,1)S(1)}, bf16[32,4096]{1,0:T(8,128)(2,1)S(1)}, u32[]{:S(2)}, u32[]{:S(2)}) %collective-permute-start) | collective-permute-done | bytes 262176 | tf_op jit(solution)/shard_map/ppermute | solution.py:153
  42.4 0.5 collective-permute-start.6
  43.4 5.4 %shard_map.106 = (bf16[128,4096]{1,0:T(8,128)(2,1)S(1)}, bf16[128,4096]{1,0:T(8,128)(2,1)S(1)}, bf16[128,192]{1,0:T(8,128)(2,1)S(1)}, bf16[128,192]{1,0:T(8,128)...) custom-call(bf16[32,4096]{1,0:T(8,128)(2,1)S(1)} %collective-permute-done.11.ref, ...), custom_call_target="tpu_custom_call" | custom-call | tf_op jit(solution)/shard_map/pallas_call | solution.py:117
  49.1 5.4 %shard_map.103 = (bf16[128,4096]{1,0:T(8,128)(2,1)S(1)}, bf16[128,4096]{1,0:T(8,128)(2,1)S(1)}, bf16[128,192]{1,0:T(8,128)(2,1)S(1)}, bf16[128,192]{1,0:T(8,128)...) custom-call(bf16[32,4096]{1,0:T(8,128)(2,1)S(1)} %get-tuple-element.30.refs_0_, ...), custom_call_target="tpu_custom_call" | custom-call | tf_op jit(solution)/shard_map/pallas_call | solution.py:117
  55.0 0.9 %collective-permute-start.20 = (bf16[16,4096]{1,0:T(8,128)(2,1)S(1)}, bf16[16,4096]{1,0:T(8,128)(2,1)S(1)}, u32[]{:S(2)}, u32[]{:S(2)}) collective-permute-start(bf16[16,4096]{1,0:T(8,128)(2,1)S(1)} %get-tuple-element.41), channel_id=1, source_target_pairs={{0,2},{1,3},{2,0},{3,1},{4,6},{5,7},{6,4},{7,5},{8,10},{9,11},{10,... | collective-permute-start | bytes 393224 | tf_op jit(solution)/shard_map/ppermute | solution.py:153
  55.9 1.5 %collective-permute-start.21 = (bf16[16,4096]{1,0:T(8,128)(2,1)S(1)}, bf16[16,4096]{1,0:T(8,128)(2,1)S(1)}, u32[]{:S(2)}, u32[]{:S(2)}) collective-permute-start(bf16[16,4096]{1,0:T(8,128)(2,1)S(1)} %get-tuple-element.42), channel_id=1, source_target_pairs={{0,4},{1,5},{2,6},{3,7},{4,0},{5,1},{6,2},{7,3},{8,12},{9,13},{10,... | collective-permute-start | bytes 393224 | tf_op jit(solution)/shard_map/ppermute | solution.py:153
  57.4 1.2 %collective-permute-start.22 = (bf16[16,4096]{1,0:T(8,128)(2,1)S(1)}, bf16[16,4096]{1,0:T(8,128)(2,1)S(1)}, u32[]{:S(2)}, u32[]{:S(2)}) collective-permute-start(bf16[16,4096]{1,0:T(8,128)(2,1)S(1)} %get-tuple-element.43), channel_id=1, source_target_pairs={{0,6},{1,7},{2,4},{3,5},{4,2},{5,3},{6,0},{7,1},{8,14},{9,15},{10,... | collective-permute-start | bytes 393224 | tf_op jit(solution)/shard_map/ppermute | solution.py:153
  58.7 0.9 %collective-permute-start.8 = (bf16[16,4096]{1,0:T(8,128)(2,1)S(1)}, bf16[16,4096]{1,0:T(8,128)(2,1)S(1)}, u32[]{:S(2)}, u32[]{:S(2)}) collective-permute-start(bf16[16,4096]{1,0:T(8,128)(2,1)S(1)} %get-tuple-element.34), channel_id=1, source_target_pairs={{0,2},{1,3},{2,0},{3,1},{4,6},{5,7},{6,4},{7,5},{8,10},{9,11},{10,... | collective-permute-start | bytes 393224 | tf_op jit(solution)/shard_map/ppermute | solution.py:153
  59.6 1.5 %collective-permute-start.9 = (bf16[16,4096]{1,0:T(8,128)(2,1)S(1)}, bf16[16,4096]{1,0:T(8,128)(2,1)S(1)}, u32[]{:S(2)}, u32[]{:S(2)}) collective-permute-start(bf16[16,4096]{1,0:T(8,128)(2,1)S(1)} %get-tuple-element.35), channel_id=1, source_target_pairs={{0,4},{1,5},{2,6},{3,7},{4,0},{5,1},{6,2},{7,3},{8,12},{9,13},{10,... | collective-permute-start | bytes 393224 | tf_op jit(solution)/shard_map/ppermute | solution.py:153
  61.1 1.2 %collective-permute-start.10 = (bf16[16,4096]{1,0:T(8,128)(2,1)S(1)}, bf16[16,4096]{1,0:T(8,128)(2,1)S(1)}, u32[]{:S(2)}, u32[]{:S(2)}) collective-permute-start(bf16[16,4096]{1,0:T(8,128)(2,1)S(1)} %get-tuple-element.36), channel_id=1, source_target_pairs={{0,6},{1,7},{2,4},{3,5},{4,2},{5,3},{6,0},{7,1},{8,14},{9,15},{10,... | collective-permute-start | bytes 393224 | tf_op jit(solution)/shard_map/ppermute | solution.py:153
  62.3 3.4 %collective-permute-done.22.refs_3_ = bf16[16,4096]{1,0:T(8,128)(2,1)S(1)} collective-permute-done((bf16[16,4096]{1,0:T(8,128)(2,1)S(1)}, bf16[16,4096]{1,0:T(8,128)(2,1)S(1)}, u32[]{:S(2)}, u32[]{:S(2)}) %collective-permute-start.22) | collective-permute-done | bytes 131104 | tf_op jit(solution)/shard_map/ppermute | solution.py:153
  65.8 3.4 %collective-permute-start.23 = (bf16[16,4096]{1,0:T(8,128)(2,1)S(1)}, bf16[16,4096]{1,0:T(8,128)(2,1)S(1)}, u32[]{:S(2)}, u32[]{:S(2)}) collective-permute-start(bf16[16,4096]{1,0:T(8,128)(2,1)S(1)} %shard_map.108), channel_id=1, source_target_pairs={{0,8},{1,9},{2,10},{3,11},{4,12},{5,13},{6,14},{7,15},{8,0},{9,1},... | collective-permute-start | bytes 393224 | tf_op jit(solution)/shard_map/ppermute | solution.py:156
  69.2 2.8 %shard_map.110 = bf16[192,4096]{1,0:T(8,128)(2,1)} custom-call(bf16[128,192]{1,0:T(8,128)(2,1)S(1)} %get-tuple-element.44.refs_0_, bf16[128,192]{1,0:T(8,128)(2,1)S(1)} %get-tuple-element.45.refs_1_, bf16[128,4096]{1,0:T(8,128)(2,1)S(1)} %get-tuple-element.46.refs_2_, bf16[128,4096]{1,0:T(8,128)(2,1)S(1)} %get-tuple-element.47.refs_3_), custom_call_target="tpu_custom_call" | custom-call | tf_op jit(solution)/shard_map/pallas_call | solution.py:134
  72.0 2.8 %shard_map.111 = bf16[192,4096]{1,0:T(8,128)(2,1)} custom-call(bf16[128,192]{1,0:T(8,128)(2,1)S(1)} %get-tuple-element.48.refs_0_, bf16[128,192]{1,0:T(8,128)(2,1)S(1)} %get-tuple-element.49.refs_1_, bf16[128,4096]{1,0:T(8,128)(2,1)S(1)} %get-tuple-element.46.refs_2_, bf16[128,4096]{1,0:T(8,128)(2,1)S(1)} %get-tuple-element.47.refs_3_), custom_call_target="tpu_custom_call" | custom-call | tf_op jit(solution)/shard_map/pallas_call | solution.py:134
  74.8 2.8 %shard_map.112 = bf16[192,4096]{1,0:T(8,128)(2,1)} custom-call(bf16[128,192]{1,0:T(8,128)(2,1)S(1)} %get-tuple-element.50.refs_0_, bf16[128,192]{1,0:T(8,128)(2,1)S(1)} %get-tuple-element.51.refs_1_, bf16[128,4096]{1,0:T(8,128)(2,1)S(1)} %get-tuple-element.52.refs_2_, bf16[128,4096]{1,0:T(8,128)(2,1)S(1)} %get-tuple-element.53.refs_3_), custom_call_target="tpu_custom_call" | custom-call | tf_op jit(solution)/shard_map/pallas_call | solution.py:134
  77.7 1.4 %shard_map.109 = bf16[128,4096]{1,0:T(8,128)(2,1)} custom-call(bf16[128,32]{1,0:T(8,128)(2,1)S(1)} %get-tuple-element.29.select_ref, bf16[16,4096]{1,0:T(8,128)(2,1)S(1)} %shard_map.105.refs_0_, bf16[16,4096]{1,0:T(8,128)(2,1)S(1)} %collective-permute-done.23.refs_1_), custom_call_target="tpu_custom_call" | custom-call | tf_op jit(solution)/shard_map/pallas_call | solution.py:117
  (33 shorter events, 2.0 us)
Async XLA Ops:
  2.2 1.2 %copy-start = (bf16[128,4096]{1,0:T(8,128)(2,1)S(1)}, bf16[128,4096]{1,0:T(8,128)(2,1)}, u32[]{:S(2)}) copy-start(bf16[128,4096]{1,0:T(8,128)(2,1)} %tokens_ref.1) | copy-start | bytes 3145732
  3.5 1.2 %copy-start.1 = (bf16[128,4096]{1,0:T(8,128)(2,1)S(1)}, bf16[128,4096]{1,0:T(8,128)(2,1)}, u32[]{:S(2)}) copy-start(bf16[128,4096]{1,0:T(8,128)(2,1)} %upstream_ref.1) | copy-start | bytes 3145732
  5.4 16.1 %collective-permute-start.11 = (bf16[32,4096]{1,0:T(8,128)(2,1)S(1)}, bf16[32,4096]{1,0:T(8,128)(2,1)S(1)}, u32[]{:S(2)}, u32[]{:S(2)}) collective-permute-start(bf16[32,4096]{1,0:T(8,128)(2,1)S(1)} %get-tuple-element.37), channel_id=1, source_target_pairs={{0,8},{1,9},{2,10},{3,11},{4,12},{5,13},{6,14},{7,15},{8,0},{9,1},... | collective-permute-start | bytes 786440 | tf_op jit(solution)/shard_map/ppermute | solution.py:156
  9.5 15.5 %collective-permute-start.2 = (bf16[32,4096]{1,0:T(8,128)(2,1)S(1)}, bf16[32,4096]{1,0:T(8,128)(2,1)S(1)}, u32[]{:S(2)}, u32[]{:S(2)}) collective-permute-start(bf16[32,4096]{1,0:T(8,128)(2,1)S(1)} %get-tuple-element.30.refs_0_), channel_id=1, source_target_pairs={{0,6},{1,7},{2,4},{3,5},{4,2},{5,3},{6,0},{7,1},{8,14},{9,15},{10,... | collective-permute-start | bytes 786440 | tf_op jit(solution)/shard_map/ppermute | solution.py:153
  12.0 17.7 %collective-permute-start.1 = (bf16[32,4096]{1,0:T(8,128)(2,1)S(1)}, bf16[32,4096]{1,0:T(8,128)(2,1)S(1)}, u32[]{:S(2)}, u32[]{:S(2)}) collective-permute-start(bf16[32,4096]{1,0:T(8,128)(2,1)S(1)} %get-tuple-element.30.refs_0_), channel_id=1, source_target_pairs={{0,4},{1,5},{2,6},{3,7},{4,0},{5,1},{6,2},{7,3},{8,12},{9,13},{10,... | collective-permute-start | bytes 786440 | tf_op jit(solution)/shard_map/ppermute | solution.py:153
  21.5 13.9 %collective-permute-start.14 = (bf16[32,4096]{1,0:T(8,128)(2,1)S(1)}, bf16[32,4096]{1,0:T(8,128)(2,1)S(1)}, u32[]{:S(2)}, u32[]{:S(2)}) collective-permute-start(bf16[32,4096]{1,0:T(8,128)(2,1)S(1)} %collective-permute-done.11.refs_0_), channel_id=1, source_target_pairs={{0,6},{1,7},{2,4},{3,5},{4,2},{5,3},{6,0},{7,1},{8,14},{9,15},{10,... | collective-permute-start | bytes 786440 | tf_op jit(solution)/shard_map/ppermute | solution.py:153
  23.1 16.4 %collective-permute-start.13 = (bf16[32,4096]{1,0:T(8,128)(2,1)S(1)}, bf16[32,4096]{1,0:T(8,128)(2,1)S(1)}, u32[]{:S(2)}, u32[]{:S(2)}) collective-permute-start(bf16[32,4096]{1,0:T(8,128)(2,1)S(1)} %collective-permute-done.11.refs_0_), channel_id=1, source_target_pairs={{0,4},{1,5},{2,6},{3,7},{4,0},{5,1},{6,2},{7,3},{8,12},{9,13},{10,... | collective-permute-start | bytes 786440 | tf_op jit(solution)/shard_map/ppermute | solution.py:153
  24.5 15.0 %collective-permute-start.12 = (bf16[32,4096]{1,0:T(8,128)(2,1)S(1)}, bf16[32,4096]{1,0:T(8,128)(2,1)S(1)}, u32[]{:S(2)}, u32[]{:S(2)}) collective-permute-start(bf16[32,4096]{1,0:T(8,128)(2,1)S(1)} %collective-permute-done.11.refs_0_), channel_id=1, source_target_pairs={{0,2},{1,3},{2,0},{3,1},{4,6},{5,7},{6,4},{7,5},{8,10},{9,11},{10,... | collective-permute-start | bytes 786440 | tf_op jit(solution)/shard_map/ppermute | solution.py:153
  25.0 17.4 %collective-permute-start = (bf16[32,4096]{1,0:T(8,128)(2,1)S(1)}, bf16[32,4096]{1,0:T(8,128)(2,1)S(1)}, u32[]{:S(2)}, u32[]{:S(2)}) collective-permute-start(bf16[32,4096]{1,0:T(8,128)(2,1)S(1)} %get-tuple-element.30.refs_0_), channel_id=1, source_target_pairs={{0,2},{1,3},{2,0},{3,1},{4,6},{5,7},{6,4},{7,5},{8,10},{9,11},{10,... | collective-permute-start | bytes 786440 | tf_op jit(solution)/shard_map/ppermute | solution.py:153
  29.7 12.6 %collective-permute-start.15 = (bf16[32,4096]{1,0:T(8,128)(2,1)S(1)}, bf16[32,4096]{1,0:T(8,128)(2,1)S(1)}, u32[]{:S(2)}, u32[]{:S(2)}) collective-permute-start(bf16[32,4096]{1,0:T(8,128)(2,1)S(1)} %collective-permute-done.11.refs_0_), channel_id=1, source_target_pairs={{0,1},{1,0},{2,3},{3,2},{4,5},{5,4},{6,7},{7,6},{8,9},{9,8},{10,11... | collective-permute-start | bytes 786440 | tf_op jit(solution)/shard_map/ppermute | solution.py:153
  35.4 7.5 %collective-permute-start.18 = (bf16[32,4096]{1,0:T(8,128)(2,1)S(1)}, bf16[32,4096]{1,0:T(8,128)(2,1)S(1)}, u32[]{:S(2)}, u32[]{:S(2)}) collective-permute-start(bf16[32,4096]{1,0:T(8,128)(2,1)S(1)} %collective-permute-done.14.refs_3_), channel_id=1, source_target_pairs={{0,1},{1,0},{2,3},{3,2},{4,5},{5,4},{6,7},{7,6},{8,9},{9,8},{10,11... | collective-permute-start | bytes 786440 | tf_op jit(solution)/shard_map/ppermute | solution.py:153
  39.5 3.4 %collective-permute-start.17 = (bf16[32,4096]{1,0:T(8,128)(2,1)S(1)}, bf16[32,4096]{1,0:T(8,128)(2,1)S(1)}, u32[]{:S(2)}, u32[]{:S(2)}) collective-permute-start(bf16[32,4096]{1,0:T(8,128)(2,1)S(1)} %collective-permute-done.13.refs_2_), channel_id=1, source_target_pairs={{0,1},{1,0},{2,3},{3,2},{4,5},{5,4},{6,7},{7,6},{8,9},{9,8},{10,11... | collective-permute-start | bytes 786440 | tf_op jit(solution)/shard_map/ppermute | solution.py:153
  39.5 3.8 %collective-permute-start.16 = (bf16[32,4096]{1,0:T(8,128)(2,1)S(1)}, bf16[32,4096]{1,0:T(8,128)(2,1)S(1)}, u32[]{:S(2)}, u32[]{:S(2)}) collective-permute-start(bf16[32,4096]{1,0:T(8,128)(2,1)S(1)} %collective-permute-done.12.refs_1_), channel_id=1, source_target_pairs={{0,1},{1,0},{2,3},{3,2},{4,5},{5,4},{6,7},{7,6},{8,9},{9,8},{10,11... | collective-permute-start | bytes 786440 | tf_op jit(solution)/shard_map/ppermute | solution.py:153
  42.3 6.7 %collective-permute-start.3 = (bf16[32,4096]{1,0:T(8,128)(2,1)S(1)}, bf16[32,4096]{1,0:T(8,128)(2,1)S(1)}, u32[]{:S(2)}, u32[]{:S(2)}) collective-permute-start(bf16[32,4096]{1,0:T(8,128)(2,1)S(1)} %get-tuple-element.30.refs_0_), channel_id=1, source_target_pairs={{0,1},{1,0},{2,3},{3,2},{4,5},{5,4},{6,7},{7,6},{8,9},{9,8},{10,11... | collective-permute-start | bytes 786440 | tf_op jit(solution)/shard_map/ppermute | solution.py:153
  42.4 6.7 %collective-permute-start.6 = (bf16[32,4096]{1,0:T(8,128)(2,1)S(1)}, bf16[32,4096]{1,0:T(8,128)(2,1)S(1)}, u32[]{:S(2)}, u32[]{:S(2)}) collective-permute-start(bf16[32,4096]{1,0:T(8,128)(2,1)S(1)} %collective-permute-done.2.refs_3_), channel_id=1, source_target_pairs={{0,1},{1,0},{2,3},{3,2},{4,5},{5,4},{6,7},{7,6},{8,9},{9,8},{10,11... | collective-permute-start | bytes 786440 | tf_op jit(solution)/shard_map/ppermute | solution.py:153
  42.9 6.2 %collective-permute-start.5 = (bf16[32,4096]{1,0:T(8,128)(2,1)S(1)}, bf16[32,4096]{1,0:T(8,128)(2,1)S(1)}, u32[]{:S(2)}, u32[]{:S(2)}) collective-permute-start(bf16[32,4096]{1,0:T(8,128)(2,1)S(1)} %collective-permute-done.1.refs_2_), channel_id=1, source_target_pairs={{0,1},{1,0},{2,3},{3,2},{4,5},{5,4},{6,7},{7,6},{8,9},{9,8},{10,11... | collective-permute-start | bytes 786440 | tf_op jit(solution)/shard_map/ppermute | solution.py:153
  42.9 6.1 %collective-permute-start.4 = (bf16[32,4096]{1,0:T(8,128)(2,1)S(1)}, bf16[32,4096]{1,0:T(8,128)(2,1)S(1)}, u32[]{:S(2)}, u32[]{:S(2)}) collective-permute-start(bf16[32,4096]{1,0:T(8,128)(2,1)S(1)} %collective-permute-done.refs_1_), channel_id=1, source_target_pairs={{0,1},{1,0},{2,3},{3,2},{4,5},{5,4},{6,7},{7,6},{8,9},{9,8},{10,11... | collective-permute-start | bytes 786440 | tf_op jit(solution)/shard_map/ppermute | solution.py:153
  48.8 6.1 %collective-permute-start.19 = (bf16[64,4096]{1,0:T(8,128)(2,1)S(1)}, bf16[64,4096]{1,0:T(8,128)(2,1)S(1)}, u32[]{:S(2)}, u32[]{:S(2)}) collective-permute-start(bf16[64,4096]{1,0:T(8,128)(2,1)S(1)} %get-tuple-element.39), channel_id=1, source_target_pairs={{0,1},{1,0},{2,3},{3,2},{4,5},{5,4},{6,7},{7,6},{8,9},{9,8},{10,11... | collective-permute-start | bytes 1572872 | tf_op jit(solution)/shard_map/ppermute | solution.py:153
  54.5 4.1 %collective-permute-start.7 = (bf16[64,4096]{1,0:T(8,128)(2,1)S(1)}, bf16[64,4096]{1,0:T(8,128)(2,1)S(1)}, u32[]{:S(2)}, u32[]{:S(2)}) collective-permute-start(bf16[64,4096]{1,0:T(8,128)(2,1)S(1)} %get-tuple-element.32), channel_id=1, source_target_pairs={{0,1},{1,0},{2,3},{3,2},{4,5},{5,4},{6,7},{7,6},{8,9},{9,8},{10,11... | collective-permute-start | bytes 1572872 | tf_op jit(solution)/shard_map/ppermute | solution.py:153
  55.0 6.1 %collective-permute-start.20 = (bf16[16,4096]{1,0:T(8,128)(2,1)S(1)}, bf16[16,4096]{1,0:T(8,128)(2,1)S(1)}, u32[]{:S(2)}, u32[]{:S(2)}) collective-permute-start(bf16[16,4096]{1,0:T(8,128)(2,1)S(1)} %get-tuple-element.41), channel_id=1, source_target_pairs={{0,2},{1,3},{2,0},{3,1},{4,6},{5,7},{6,4},{7,5},{8,10},{9,11},{10,... | collective-permute-start | bytes 393224 | tf_op jit(solution)/shard_map/ppermute | solution.py:153
  55.9 6.4 %collective-permute-start.21 = (bf16[16,4096]{1,0:T(8,128)(2,1)S(1)}, bf16[16,4096]{1,0:T(8,128)(2,1)S(1)}, u32[]{:S(2)}, u32[]{:S(2)}) collective-permute-start(bf16[16,4096]{1,0:T(8,128)(2,1)S(1)} %get-tuple-element.42), channel_id=1, source_target_pairs={{0,4},{1,5},{2,6},{3,7},{4,0},{5,1},{6,2},{7,3},{8,12},{9,13},{10,... | collective-permute-start | bytes 393224 | tf_op jit(solution)/shard_map/ppermute | solution.py:153
  57.4 8.4 %collective-permute-start.22 = (bf16[16,4096]{1,0:T(8,128)(2,1)S(1)}, bf16[16,4096]{1,0:T(8,128)(2,1)S(1)}, u32[]{:S(2)}, u32[]{:S(2)}) collective-permute-start(bf16[16,4096]{1,0:T(8,128)(2,1)S(1)} %get-tuple-element.43), channel_id=1, source_target_pairs={{0,6},{1,7},{2,4},{3,5},{4,2},{5,3},{6,0},{7,1},{8,14},{9,15},{10,... | collective-permute-start | bytes 393224 | tf_op jit(solution)/shard_map/ppermute | solution.py:153
  58.7 18.9 %collective-permute-start.8 = (bf16[16,4096]{1,0:T(8,128)(2,1)S(1)}, bf16[16,4096]{1,0:T(8,128)(2,1)S(1)}, u32[]{:S(2)}, u32[]{:S(2)}) collective-permute-start(bf16[16,4096]{1,0:T(8,128)(2,1)S(1)} %get-tuple-element.34), channel_id=1, source_target_pairs={{0,2},{1,3},{2,0},{3,1},{4,6},{5,7},{6,4},{7,5},{8,10},{9,11},{10,... | collective-permute-start | bytes 393224 | tf_op jit(solution)/shard_map/ppermute | solution.py:153
  59.6 18.0 %collective-permute-start.9 = (bf16[16,4096]{1,0:T(8,128)(2,1)S(1)}, bf16[16,4096]{1,0:T(8,128)(2,1)S(1)}, u32[]{:S(2)}, u32[]{:S(2)}) collective-permute-start(bf16[16,4096]{1,0:T(8,128)(2,1)S(1)} %get-tuple-element.35), channel_id=1, source_target_pairs={{0,4},{1,5},{2,6},{3,7},{4,0},{5,1},{6,2},{7,3},{8,12},{9,13},{10,... | collective-permute-start | bytes 393224 | tf_op jit(solution)/shard_map/ppermute | solution.py:153
  61.1 16.5 %collective-permute-start.10 = (bf16[16,4096]{1,0:T(8,128)(2,1)S(1)}, bf16[16,4096]{1,0:T(8,128)(2,1)S(1)}, u32[]{:S(2)}, u32[]{:S(2)}) collective-permute-start(bf16[16,4096]{1,0:T(8,128)(2,1)S(1)} %get-tuple-element.36), channel_id=1, source_target_pairs={{0,6},{1,7},{2,4},{3,5},{4,2},{5,3},{6,0},{7,1},{8,14},{9,15},{10,... | collective-permute-start | bytes 393224 | tf_op jit(solution)/shard_map/ppermute | solution.py:153
  65.8 11.8 %collective-permute-start.23 = (bf16[16,4096]{1,0:T(8,128)(2,1)S(1)}, bf16[16,4096]{1,0:T(8,128)(2,1)S(1)}, u32[]{:S(2)}, u32[]{:S(2)}) collective-permute-start(bf16[16,4096]{1,0:T(8,128)(2,1)S(1)} %shard_map.108), channel_id=1, source_target_pairs={{0,8},{1,9},{2,10},{3,11},{4,12},{5,13},{6,14},{7,15},{8,0},{9,1},... | collective-permute-start | bytes 393224 | tf_op jit(solution)/shard_map/ppermute | solution.py:156

commit v2 on v1

v2 whole, which is shorter than its diff:
```python
import functools

import jax
import jax.numpy as jnp
from jax import lax
from jax.experimental import pallas as pl
from jax.experimental.pallas import tpu as pltpu
from jax.sharding import PartitionSpec as P

TILES = 8
CAP = 16
BF = jnp.bfloat16
F32 = jnp.float32
VMEM = pl.BlockSpec(memory_space=pltpu.VMEM)
SMEM = pl.BlockSpec(memory_space=pltpu.SMEM)
HBM = pl.BlockSpec(memory_space=pltpu.HBM)
STEP = 1024


def params(mib):
    return pltpu.CompilerParams(vmem_limit_bytes=mib * 1024 * 1024)


def dot(left, right, left_dim, right_dim):
    return lax.dot_general(
        left, right, (((left_dim,), (right_dim,)), ((), ())), preferred_element_type=F32
    )


def pack_kernel(window, own_ref, ids_hbm, gate_hbm, tokens_hbm, upstream_hbm, *refs):
    select_ref, blocks = refs[0], refs[1 : window + 1]
    ids_ref, gate_ref, tokens_ref, upstream_ref, small, large = refs[window + 1 :]
    count, width = tokens_ref.shape
    first_copies = [
        pltpu.make_async_copy(ids_hbm, ids_ref, small.at[0]),
        pltpu.make_async_copy(gate_hbm, gate_ref, small.at[1]),
    ]
    step = min(STEP, width)
    copies = []
    for j, at in enumerate(range(0, width, step)):
        cols = pl.ds(at, step)
        copies.append(
            (
                pltpu.make_async_copy(tokens_hbm.at[:, cols], tokens_ref.at[:, cols], large.at[2 * j]),
                pltpu.make_async_copy(
                    upstream_hbm.at[:, cols], upstream_ref.at[:, cols], large.at[2 * j + 1]
                ),
            )
        )
    for copy in first_copies:
        copy.start()
    for pair in copies:
        for copy in pair:
            copy.start()
    for copy in first_copies:
        copy.wait()
    ids = ids_ref[...]
    inside = ids < window
    chosen = jnp.sum(jnp.where(inside, ids, 0).astype(F32), axis=0, keepdims=True).astype(jnp.int32)
    has_slot = jnp.sum(inside.astype(F32), axis=0, keepdims=True) > 0.0
    weight = jnp.sum(jnp.where(inside, gate_ref[...], 0.0), axis=0, keepdims=True)
    shift = chosen - own_ref[0]
    shift = jnp.where(shift < 0, shift + window, shift)
    slots = window * CAP
    slot = lax.broadcasted_iota(jnp.int32, (slots, count), 0)
    first = shift * CAP
    member = ((slot >= first) & (slot < first + CAP) & has_slot).astype(F32)
    row = lax.broadcasted_iota(jnp.int32, (count, count), 0)
    col = lax.broadcasted_iota(jnp.int32, (count, count), 1)
    before = (row < col).astype(BF)
    earlier = dot(member.astype(BF), before, 1, 0)
    select = ((member > 0.0) & ((slot - first).astype(F32) == earlier)).astype(F32)
    scale = jnp.sum(select * weight, axis=1, keepdims=True)
    select = select.astype(BF)
    select_ref[...] = select
    for j, at in enumerate(range(0, width, step)):
        cols = pl.ds(at, step)
        for copy in copies[j]:
            copy.wait()
        x = dot(select, tokens_ref[:, cols], 1, 0).astype(BF)
        z = (dot(select, upstream_ref[:, cols], 1, 0) * scale).astype(BF)
        for k in range(window):
            part = slice(k * CAP, (k + 1) * CAP)
            blocks[k][:CAP, cols] = x[part]
            blocks[k][CAP:, cols] = z[part]


def expert_kernel(count, *refs):
    blocks, refs = refs[:count], refs[count:]
    gate_ref, up_ref, down_ref, x_ref, z_ref, dg_ref, du_ref, hidden_ref = refs[:8]
    parts = refs[8:]
    for j, block in enumerate(blocks):
        x_ref[j * CAP : (j + 1) * CAP, :] = block[:CAP, :]
        z_ref[j * CAP : (j + 1) * CAP, :] = block[CAP:, :]
    x = x_ref[...]
    pre_gate = dot(x, gate_ref[...], 1, 1)
    pre_up = dot(x, up_ref[...], 1, 1)
    d_hidden = dot(z_ref[...], down_ref[...], 1, 1)
    sigma = 1.0 / (1.0 + jnp.exp(-pre_gate))
    active = pre_gate * sigma
    hidden_ref[...] = (active * pre_up).astype(BF)
    d_gate = (d_hidden * pre_up * sigma * (1.0 + pre_gate * (1.0 - sigma))).astype(BF)
    d_up = (d_hidden * active).astype(BF)
    dg_ref[...] = d_gate
    du_ref[...] = d_up
    half = count * CAP // 2
    width = gate_ref.shape[1]
    step = min(STEP, width)
    for at in range(0, width, step):
        cols = pl.ds(at, step)
        value = dot(d_gate, gate_ref[:, cols], 1, 0) + dot(d_up, up_ref[:, cols], 1, 0)
        value = value.astype(BF)
        parts[0][:, cols] = value[:half]
        parts[1][:, cols] = value[half:]


def grad_kernel(count, *refs):
    lefts, rights, outs = refs[: 3 * count], refs[3 * count : 5 * count], refs[5 * count :]
    for m, out in enumerate(outs):
        total = None
        for j in range(count):
            right = rights[j + (count if m == 2 else 0)]
            term = dot(lefts[m * count + j][...], right[...], 0, 0)
            total = term if total is None else total + term
        out[...] = total.astype(BF)


def sum_kernel(terms, *refs):
    outs = refs[terms:]
    rows = outs[0].shape[0]
    for j, out in enumerate(outs):
        total = refs[0][j * rows : (j + 1) * rows, :].astype(F32)
        for ref in refs[1:terms]:
            total = total + ref[j * rows : (j + 1) * rows, :].astype(F32)
        out[...] = total.astype(BF)


def unpack_kernel(count, select_ref, *refs):
    out = refs[-1]
    width = out.shape[1]
    step = min(STEP, width)
    for at in range(0, width, step):
        cols = pl.ds(at, step)
        rows = jnp.concatenate([refs[k][:, cols] for k in range(count)], axis=0)
        out[:, cols] = dot(select_ref[...], rows, 0, 0).astype(BF)


def call(kernel, out_shape, *args, mib=24):
    return pl.pallas_call(
        kernel,
        out_shape=out_shape,
        in_specs=[VMEM] * len(args),
        out_specs=jax.tree.map(lambda _: VMEM, out_shape),
        compiler_params=params(mib),
    )(*args)


def shape(*dims):
    return jax.ShapeDtypeStruct(dims, BF)


def whole(a):
    return pl.BlockSpec(a.shape, lambda i: (0, 0))


def columns(rows, step):
    return pl.BlockSpec((rows, step), lambda i: (0, i))


def pack(window, own, expert_ids, gate_values, tokens, upstream):
    count, width = tokens.shape
    outs = [shape(window * CAP, count), *[shape(2 * CAP, width)] * window]
    return pl.pallas_call(
        functools.partial(pack_kernel, window),
        out_shape=outs,
        in_specs=[SMEM] + [HBM] * 4,
        out_specs=[VMEM] * len(outs),
        scratch_shapes=[
            pltpu.VMEM(expert_ids.shape, jnp.int32),
            pltpu.VMEM(gate_values.shape, F32),
            pltpu.VMEM(tokens.shape, BF),
            pltpu.VMEM(upstream.shape, BF),
            pltpu.SemaphoreType.DMA((2,)),
            pltpu.SemaphoreType.DMA((2 * (width // min(STEP, width)),)),
        ],
        compiler_params=params(56),
    )(own, expert_ids, gate_values, tokens, upstream)


def fetch_kernel(*refs):
    count = len(refs) // 2
    for source, out in zip(refs[:count], refs[count:]):
        out[...] = source[...]


def grads(lefts, rights):
    count = len(rights) // 2
    hidden, width = lefts[0].shape[1], rights[0].shape[1]
    step = min(STEP, width)
    return pl.pallas_call(
        functools.partial(grad_kernel, count),
        grid=(width // step,),
        out_shape=[shape(hidden, width)] * 3,
        in_specs=[whole(a) for a in lefts] + [columns(a.shape[0], step) for a in rights],
        out_specs=[columns(hidden, step)] * 3,
        compiler_params=params(24),
    )(*lefts, *rights)


def on_device(tokens, upstream, expert_ids, gate_values, w_gate, w_up, w_down):
    devices = lax.axis_size("exp")
    window = devices // TILES
    width = tokens.shape[1]
    hidden = w_gate.shape[1]
    gate, up, down = [
        call(fetch_kernel, shape(*w.shape[1:]), w[0], mib=8) for w in (w_gate, w_up, w_down)
    ]
    own = (lax.axis_index("exp") // TILES).astype(jnp.int32)[None]

    def swap(a, bits):
        return lax.ppermute(a, "exp", [(i, i ^ bits) for i in range(devices)])

    def turn(a, k):
        return lax.ppermute(a, "exp", [(i, (i + k * TILES) % devices) for i in range(devices)])

    def near(block):
        return [block] + [swap(block, bits) for bits in (2, 4, 6)]

    def both(blocks):
        return blocks + [swap(b, 1) for b in blocks]

    def later(values, *first):
        count = len(values)
        return lax.optimization_barrier((*values, *first))[:count]

    def expert(blocks):
        rows = len(blocks) * CAP
        return call(
            functools.partial(expert_kernel, len(blocks)),
            [shape(rows, width)] * 2 + [shape(rows, hidden)] * 3 + [shape(rows // 2, width)] * 2,
            *blocks, gate, up, down,
        )

    select, *packed = pack(window, own, expert_ids.T, gate_values.T, tokens, upstream)
    crossed = [turn(packed[k], k) for k in range(1, window)]
    mine = packed[0]
    across, along = swap(mine, 2), swap(mine, 4)
    *crossed, across, along, gate, up, down = later([*crossed, across, along, gate, up, down])

    def halve(result):
        kept, other = result[5:]
        return call(functools.partial(sum_kernel, 2), [shape(CAP, width)] * 4, kept, swap(other, 1))

    def gather(pieces):
        pieces = [pieces[0]] + [swap(pieces[j], 2 * j) for j in (1, 2, 3)]
        return call(functools.partial(sum_kernel, 4), [shape(CAP, width)], *pieces)[0]

    results, returned = [], []
    for k in range(1, window):
        blocks = near(crossed[k - 1])
        if k == window - 1:
            (along,) = later([along], *blocks)
        results.append(expert(both(blocks)))
        pieces = halve(results[-1])
        returned.append(turn(gather(pieces), window - k))
    (corner,) = later([swap(along, 2)], results[-1][5])
    own_blocks = later(both([mine, across, along, corner]), *pieces)
    results.append(expert(own_blocks))
    returned.append(gather(halve(results[-1])))
    results = results[-1:] + results[:-1]
    returned = returned[-1:] + returned[:-1]
    grad_gate, grad_up, grad_down = grads(
        [r[m] for m in (2, 3, 4) for r in results], [r[m] for m in (0, 1) for r in results]
    )
    d_tokens = call(
        functools.partial(unpack_kernel, window), shape(*tokens.shape), select, *returned
    )
    return (d_tokens, grad_gate[None], grad_up[None], grad_down[None])


def solution(mesh):
    rows = P(("grp", "exp"), None)
    tiles = P("exp", None, None)
    grown = P(("grp", "exp"), None, None)
    return jax.shard_map(
        on_device,
        mesh=mesh,
        in_specs=(rows, rows, rows, rows, tiles, tiles, tiles),
        out_specs=(rows, grown, grown, grown),
        check_vma=False,
    )
```

time: 79.3 us -> 67.8 us (0.85)
  Pallas kernels: 21.7 us -> 15.9 us
  waiting for transfers between devices: 27.8 us -> 23.5 us
  local copies, waits for them, and re-layouts: 4.02 us -> 2.62 us
    pallas_call x3 -> x1, Pallas kernels: 8.39 us -> 4.38 us  [grads(): pl.pallas_call(functools.partial(grad_kernel, count), grid=(width // step...]
    ppermute x2, waiting for transfers between devices: 9.04 us -> 6.21 us  [turn(): lax.ppermute(a, 'exp', [(i, (i + k * TILES) % devices) for i in range(dev...]
    pallas_call x8 -> x11, Pallas kernels: 13.3 us -> 11.5 us  [the longest x10 8.2 us: call(): pl.pallas_call(kernel, out_shape=out_shape, in_specs=[VMEM] * len(args),...]
    ppermute x22, waiting for transfers between devices: 18.7 us -> 17.3 us  [swap(): return lax.ppermute(a, 'exp', [(i, i ^ bits) for i in range(devices)])]
    unnamed x6 -> x10, local copies, waits for them, and re-layouts: 4.02 us -> 2.62 us
  transfers between devices with their start and end apart: 24 -> 24, of which waited for: 6 -> 10; matrix products, arithmetic and copies ran while one was open for 0% -> 0% of each run, Pallas kernels for 25% -> 12%
where the time goes in v2:
time: 67.8 us; the launch traced here: 67.6 us
  starting transfers between devices  24.8 us (37%)
  waiting for transfers between devices  23.5 us (35%)
  Pallas kernels  15.9 us (23%)
  local copies, waits for them, and re-layouts  2.62 us (4%)
  between operations  0.78 us (1%)
    ppermute x22, starting transfers between devices, swap(): return lax.ppermute(a, 'exp', [(i, i ^ bits) for i in range(devices)])  17.3 us
    ppermute x22, waiting for transfers between devices, swap(): return lax.ppermute(a, 'exp', [(i, i ^ bits) for i in range(devices)])  17.3 us
    pallas_call x10, Pallas kernels, call(): pl.pallas_call(kernel, out_shape=out_shape, in_specs=[VMEM] * len(args),...  8.2 us
    ppermute x2, starting transfers between devices, turn(): lax.ppermute(a, 'exp', [(i, (i + k * TILES) % devices) for i in range(dev...  7.53 us
    ppermute x2, waiting for transfers between devices, turn(): lax.ppermute(a, 'exp', [(i, (i + k * TILES) % devices) for i in range(dev...  6.21 us
    pallas_call x1, Pallas kernels, grads(): pl.pallas_call(functools.partial(grad_kernel, count), grid=(width // step...  4.38 us
    pallas_call x1, Pallas kernels, pack(): pl.pallas_call(functools.partial(pack_kernel, window), out_shape=outs, in...  3.31 us
    unnamed x10, local copies, waits for them, and re-layouts  2.62 us
  transfers between devices with their start and end apart: 24, of which 10 were waited for; matrix products, arithmetic and copies ran while one was open for 0% of the time, Pallas kernels for 12%

profile of v2, /device:TPU:0, one launch (start us, length us, event | category | flops | bytes accessed | tf_op | source)
XLA Modules:
  0.0 67.6 jit_solution(12924161941777211495)
XLA Ops:
  0.7 3.3 %shard_map.102 = (bf16[32,128]{1,0:T(8,128)(2,1)}, bf16[32,4096]{1,0:T(8,128)(2,1)}, bf16[32,4096]{1,0:T(8,128)(2,1)}) custom-call(s32[1]{0:T(128)} %bitcast.own_ref, s32[8,128]{1,0:T(8,128)} %bitcast.12, f32[8,128]{1,0:T(8,128)} %bitcast.13, bf16[128,4096]{1,0:T(8,128)(2,1)} %tokens_hbm.1, bf16[128,4096]{1,0:T(8,128)(2,1)} %upstream_hbm.1), custom_call_target="tpu_custom_call" | custom-call | tf_op jit(solution)/shard_map/pallas_call | solution.py:173
  4.0 4.1 %collective-permute-start = (bf16[32,4096]{1,0:T(8,128)(2,1)}, bf16[32,4096]{1,0:T(8,128)(2,1)S(1)}, u32[]{:S(2)}, u32[]{:S(2)}) collective-permute-start(bf16[32,4096]{1,0:T(8,128)(2,1)} %get-tuple-element.50), channel_id=1, source_target_pairs={{0,8},{1,9},{2,10},{3,11},{4,12},{5,13},{6,14},{7,15},{8,0},{9,1},... | collective-permute-start | bytes 786440 | tf_op jit(solution)/shard_map/ppermute | solution.py:224
  8.1 1.6 %collective-permute-start.2 = (bf16[32,4096]{1,0:T(8,128)(2,1)}, bf16[32,4096]{1,0:T(8,128)(2,1)S(1)}, u32[]{:S(2)}, u32[]{:S(2)}) collective-permute-start(bf16[32,4096]{1,0:T(8,128)(2,1)} %get-tuple-element.65.refs_0_), channel_id=1, source_target_pairs={{0,4},{1,5},{2,6},{3,7},{4,0},{5,1},{6,2},{7,3},{8,12},{9,13},{10,... | collective-permute-start | bytes 786440 | tf_op jit(solution)/shard_map/ppermute | solution.py:221
  9.6 1.5 %collective-permute-start.1 = (bf16[32,4096]{1,0:T(8,128)(2,1)}, bf16[32,4096]{1,0:T(8,128)(2,1)S(1)}, u32[]{:S(2)}, u32[]{:S(2)}) collective-permute-start(bf16[32,4096]{1,0:T(8,128)(2,1)} %get-tuple-element.65.refs_0_), channel_id=1, source_target_pairs={{0,2},{1,3},{2,0},{3,1},{4,6},{5,7},{6,4},{7,5},{8,10},{9,11},{10,... | collective-permute-start | bytes 786440 | tf_op jit(solution)/shard_map/ppermute | solution.py:221
  11.3 1.3 %copy-done.1 = bf16[1,192,4096]{2,1,0:T(8,128)(2,1)S(1)} copy-done((bf16[1,192,4096]{2,1,0:T(8,128)(2,1)S(1)}, bf16[1,192,4096]{2,1,0:T(8,128)(2,1)}, u32[]{:S(2)}) %copy-start.1) | copy-done | bytes 1572888
  12.7 1.3 %copy-done.2 = bf16[1,192,4096]{2,1,0:T(8,128)(2,1)S(1)} copy-done((bf16[1,192,4096]{2,1,0:T(8,128)(2,1)S(1)}, bf16[1,192,4096]{2,1,0:T(8,128)(2,1)}, u32[]{:S(2)}) %copy-start.2) | copy-done | bytes 1572888
  14.1 6.2 %collective-permute-done.refs_0_ = bf16[32,4096]{1,0:T(8,128)(2,1)S(1)} collective-permute-done((bf16[32,4096]{1,0:T(8,128)(2,1)}, bf16[32,4096]{1,0:T(8,128)(2,1)S(1)}, u32[]{:S(2)}, u32[]{:S(2)}) %collective-permute-start) | collective-permute-done | bytes 262176 | tf_op jit(solution)/shard_map/ppermute | solution.py:224
  20.5 2.4 %collective-permute-start.5 = (bf16[32,4096]{1,0:T(8,128)(2,1)S(1)}, bf16[32,4096]{1,0:T(8,128)(2,1)S(1)}, u32[]{:S(2)}, u32[]{:S(2)}) collective-permute-start(bf16[32,4096]{1,0:T(8,128)(2,1)S(1)} %collective-permute-done.refs_0_), channel_id=1, source_target_pairs={{0,6},{1,7},{2,4},{3,5},{4,2},{5,3},{6,0},{7,1},{8,14},{9,15},{10,... | collective-permute-start | bytes 786440 | tf_op jit(solution)/shard_map/ppermute | solution.py:221
  22.9 0.6 collective-permute-start.4
  23.5 0.5 collective-permute-start.3
  24.0 6.7 %collective-permute-done.5.refs_3_ = bf16[32,4096]{1,0:T(8,128)(2,1)S(1)} collective-permute-done((bf16[32,4096]{1,0:T(8,128)(2,1)S(1)}, bf16[32,4096]{1,0:T(8,128)(2,1)S(1)}, u32[]{:S(2)}, u32[]{:S(2)}) %collective-permute-start.5) | collective-permute-done | bytes 262176 | tf_op jit(solution)/shard_map/ppermute | solution.py:221
  30.7 3.4 %collective-permute-done.4.refs_2_ = bf16[32,4096]{1,0:T(8,128)(2,1)S(1)} collective-permute-done((bf16[32,4096]{1,0:T(8,128)(2,1)S(1)}, bf16[32,4096]{1,0:T(8,128)(2,1)S(1)}, u32[]{:S(2)}, u32[]{:S(2)}) %collective-permute-start.4) | collective-permute-done | bytes 262176 | tf_op jit(solution)/shard_map/ppermute | solution.py:221
  34.3 0.4 collective-permute-start.8
  34.6 0.9 %collective-permute-start.6 = (bf16[32,4096]{1,0:T(8,128)(2,1)S(1)}, bf16[32,4096]{1,0:T(8,128)(2,1)S(1)}, u32[]{:S(2)}, u32[]{:S(2)}) collective-permute-start(bf16[32,4096]{1,0:T(8,128)(2,1)S(1)} %collective-permute-done.2.refs_2_), channel_id=1, source_target_pairs={{0,2},{1,3},{2,0},{3,1},{4,6},{5,7},{6,4},{7,5},{8,10},{9,11},{10,... | collective-permute-start | bytes 786440 | tf_op jit(solution)/shard_map/ppermute | solution.py:221
  35.7 0.4 collective-permute-done.8.refs_5_
  36.0 3.0 %shard_map.106 = (bf16[128,4096]{1,0:T(8,128)(2,1)S(1)}, bf16[128,4096]{1,0:T(8,128)(2,1)S(1)}, bf16[128,192]{1,0:T(8,128)(2,1)S(1)}, bf16[128,192]{1,0:T(8,128)...) custom-call(bf16[32,4096]{1,0:T(8,128)(2,1)S(1)} %collective-permute-done.refs_0, ...), custom_call_target="tpu_custom_call" | custom-call | tf_op jit(solution)/shard_map/pallas_call | solution.py:149
  39.3 0.4 collective-permute-start.11
  39.8 0.4 collective-permute-start.13
  40.2 2.8 %collective-permute-done.6.refs_3_ = bf16[32,4096]{1,0:T(8,128)(2,1)S(1)} collective-permute-done((bf16[32,4096]{1,0:T(8,128)(2,1)S(1)}, bf16[32,4096]{1,0:T(8,128)(2,1)S(1)}, u32[]{:S(2)}, u32[]{:S(2)}) %collective-permute-start.6) | collective-permute-done | bytes 262176 | tf_op jit(solution)/shard_map/ppermute | solution.py:221
  43.2 1.4 %collective-permute-done.14.refs_7_ = bf16[32,4096]{1,0:T(8,128)(2,1)S(1)} collective-permute-done((bf16[32,4096]{1,0:T(8,128)(2,1)S(1)}, bf16[32,4096]{1,0:T(8,128)(2,1)S(1)}, u32[]{:S(2)}, u32[]{:S(2)}) %collective-permute-start.14) | collective-permute-done | bytes 262176 | tf_op jit(solution)/shard_map/ppermute | solution.py:221
  44.5 3.0 %shard_map.108 = (bf16[128,4096]{1,0:T(8,128)(2,1)S(1)}, bf16[128,4096]{1,0:T(8,128)(2,1)S(1)}, bf16[128,192]{1,0:T(8,128)(2,1)S(1)}, bf16[128,192]{1,0:T(8,128)...) custom-call(bf16[32,4096]{1,0:T(8,128)(2,1)S(1)} %copy-done.3, ...), custom_call_target="tpu_custom_call" | custom-call | tf_op jit(solution)/shard_map/pallas_call | solution.py:149
  47.6 0.3 collective-permute-start.16
  47.9 1.2 %collective-permute-start.20 = (bf16[16,4096]{1,0:T(8,128)(2,1)S(1)}, bf16[16,4096]{1,0:T(8,128)(2,1)S(1)}, u32[]{:S(2)}, u32[]{:S(2)}) collective-permute-start(bf16[16,4096]{1,0:T(8,128)(2,1)S(1)} %get-tuple-element.62), channel_id=1, source_target_pairs={{0,2},{1,3},{2,0},{3,1},{4,6},{5,7},{6,4},{7,5},{8,10},{9,11},{10,... | collective-permute-start | bytes 393224 | tf_op jit(solution)/shard_map/ppermute | solution.py:221
  49.1 1.7 %collective-permute-start.21 = (bf16[16,4096]{1,0:T(8,128)(2,1)S(1)}, bf16[16,4096]{1,0:T(8,128)(2,1)S(1)}, u32[]{:S(2)}, u32[]{:S(2)}) collective-permute-start(bf16[16,4096]{1,0:T(8,128)(2,1)S(1)} %get-tuple-element.63), channel_id=1, source_target_pairs={{0,4},{1,5},{2,6},{3,7},{4,0},{5,1},{6,2},{7,3},{8,12},{9,13},{10,... | collective-permute-start | bytes 393224 | tf_op jit(solution)/shard_map/ppermute | solution.py:221
  50.8 0.5 collective-permute-start.22
  51.5 1.3 %collective-permute-start.17 = (bf16[16,4096]{1,0:T(8,128)(2,1)S(1)}, bf16[16,4096]{1,0:T(8,128)(2,1)S(1)}, u32[]{:S(2)}, u32[]{:S(2)}) collective-permute-start(bf16[16,4096]{1,0:T(8,128)(2,1)S(1)} %get-tuple-element.76), channel_id=1, source_target_pairs={{0,2},{1,3},{2,0},{3,1},{4,6},{5,7},{6,4},{7,5},{8,10},{9,11},{10,... | collective-permute-start | bytes 393224 | tf_op jit(solution)/shard_map/ppermute | solution.py:221
  52.8 1.7 %collective-permute-start.18 = (bf16[16,4096]{1,0:T(8,128)(2,1)S(1)}, bf16[16,4096]{1,0:T(8,128)(2,1)S(1)}, u32[]{:S(2)}, u32[]{:S(2)}) collective-permute-start(bf16[16,4096]{1,0:T(8,128)(2,1)S(1)} %get-tuple-element.77), channel_id=1, source_target_pairs={{0,4},{1,5},{2,6},{3,7},{4,0},{5,1},{6,2},{7,3},{8,12},{9,13},{10,... | collective-permute-start | bytes 393224 | tf_op jit(solution)/shard_map/ppermute | solution.py:221
  54.5 1.5 %collective-permute-start.19 = (bf16[16,4096]{1,0:T(8,128)(2,1)S(1)}, bf16[16,4096]{1,0:T(8,128)(2,1)S(1)}, u32[]{:S(2)}, u32[]{:S(2)}) collective-permute-start(bf16[16,4096]{1,0:T(8,128)(2,1)S(1)} %get-tuple-element.78), channel_id=1, source_target_pairs={{0,6},{1,7},{2,4},{3,5},{4,2},{5,3},{6,0},{7,1},{8,14},{9,15},{10,... | collective-permute-start | bytes 393224 | tf_op jit(solution)/shard_map/ppermute | solution.py:221
  56.0 2.1 %collective-permute-done.22.refs_3_ = bf16[16,4096]{1,0:T(8,128)(2,1)S(1)} collective-permute-done((bf16[16,4096]{1,0:T(8,128)(2,1)S(1)}, bf16[16,4096]{1,0:T(8,128)(2,1)S(1)}, u32[]{:S(2)}, u32[]{:S(2)}) %collective-permute-start.22) | collective-permute-done | bytes 131104 | tf_op jit(solution)/shard_map/ppermute | solution.py:221
  58.2 3.4 %collective-permute-start.23 = (bf16[16,4096]{1,0:T(8,128)(2,1)S(1)}, bf16[16,4096]{1,0:T(8,128)(2,1)S(1)}, u32[]{:S(2)}, u32[]{:S(2)}) collective-permute-start(bf16[16,4096]{1,0:T(8,128)(2,1)S(1)} %shard_map.111), channel_id=1, source_target_pairs={{0,8},{1,9},{2,10},{3,11},{4,12},{5,13},{6,14},{7,15},{8,0},{9,1},... | collective-permute-start | bytes 393224 | tf_op jit(solution)/shard_map/ppermute | solution.py:224
  61.7 4.4 %shard_map.113 = (bf16[192,4096]{1,0:T(8,128)(2,1)}, bf16[192,4096]{1,0:T(8,128)(2,1)}, bf16[192,4096]{1,0:T(8,128)(2,1)}) custom-call(bf16[128,192]{1,0:T(8,128)(2,1)S(1)} %get-tuple-element.79.refs_0_, bf16[128,192]{1,0:T(8,128)(2,1)S(1)} %get-tuple-element.80.refs_1_, bf16[128,192]{1,0:T(8,128)(2,1)S(1)} %get-tuple-element.81.refs_2_, ...), custom_call_target="tpu_custom_call" | custom-call | tf_op jit(solution)/shard_map/pallas_call | solution.py:200
  66.2 1.4 %shard_map.112 = bf16[128,4096]{1,0:T(8,128)(2,1)} custom-call(bf16[32,128]{1,0:T(8,128)(2,1)S(1)} %copy-done.4, bf16[16,4096]{1,0:T(8,128)(2,1)S(1)} %shard_map.110.refs_0_, bf16[16,4096]{1,0:T(8,128)(2,1)S(1)} %collective-permute-done.23.refs_1_), custom_call_target="tpu_custom_call" | custom-call | tf_op jit(solution)/shard_map/pallas_call | solution.py:149
  (38 shorter events, 1.5 us)
Async XLA Ops:
  0.6 10.5 %copy-start = (bf16[1,192,4096]{2,1,0:T(8,128)(2,1)S(1)}, bf16[1,192,4096]{2,1,0:T(8,128)(2,1)}, u32[]{:S(2)}) copy-start(bf16[1,192,4096]{2,1,0:T(8,128)(2,1)} %param.11) | copy-start | bytes 4718596
  4.0 16.3 %collective-permute-start = (bf16[32,4096]{1,0:T(8,128)(2,1)}, bf16[32,4096]{1,0:T(8,128)(2,1)S(1)}, u32[]{:S(2)}, u32[]{:S(2)}) collective-permute-start(bf16[32,4096]{1,0:T(8,128)(2,1)} %get-tuple-element.50), channel_id=1, source_target_pairs={{0,8},{1,9},{2,10},{3,11},{4,12},{5,13},{6,14},{7,15},{8,0},{9,1},... | collective-permute-start | bytes 786440 | tf_op jit(solution)/shard_map/ppermute | solution.py:224
  8.1 12.4 %collective-permute-start.2 = (bf16[32,4096]{1,0:T(8,128)(2,1)}, bf16[32,4096]{1,0:T(8,128)(2,1)S(1)}, u32[]{:S(2)}, u32[]{:S(2)}) collective-permute-start(bf16[32,4096]{1,0:T(8,128)(2,1)} %get-tuple-element.65.refs_0_), channel_id=1, source_target_pairs={{0,4},{1,5},{2,6},{3,7},{4,0},{5,1},{6,2},{7,3},{8,12},{9,13},{10,... | collective-permute-start | bytes 786440 | tf_op jit(solution)/shard_map/ppermute | solution.py:221
  9.6 10.9 %collective-permute-start.1 = (bf16[32,4096]{1,0:T(8,128)(2,1)}, bf16[32,4096]{1,0:T(8,128)(2,1)S(1)}, u32[]{:S(2)}, u32[]{:S(2)}) collective-permute-start(bf16[32,4096]{1,0:T(8,128)(2,1)} %get-tuple-element.65.refs_0_), channel_id=1, source_target_pairs={{0,2},{1,3},{2,0},{3,1},{4,6},{5,7},{6,4},{7,5},{8,10},{9,11},{10,... | collective-permute-start | bytes 786440 | tf_op jit(solution)/shard_map/ppermute | solution.py:221
  11.2 1.4 %copy-start.1 = (bf16[1,192,4096]{2,1,0:T(8,128)(2,1)S(1)}, bf16[1,192,4096]{2,1,0:T(8,128)(2,1)}, u32[]{:S(2)}) copy-start(bf16[1,192,4096]{2,1,0:T(8,128)(2,1)} %param.12) | copy-start | bytes 4718596
  12.6 1.4 %copy-start.2 = (bf16[1,192,4096]{2,1,0:T(8,128)(2,1)S(1)}, bf16[1,192,4096]{2,1,0:T(8,128)(2,1)}, u32[]{:S(2)}) copy-start(bf16[1,192,4096]{2,1,0:T(8,128)(2,1)} %param.13) | copy-start | bytes 4718596
  14.1 25.2 %copy-start.3 = (bf16[32,4096]{1,0:T(8,128)(2,1)S(1)}, bf16[32,4096]{1,0:T(8,128)(2,1)}, u32[]{:S(2)}) copy-start(bf16[32,4096]{1,0:T(8,128)(2,1)} %get-tuple-element.65.refs_0_) | copy-start | bytes 786436
  20.5 10.2 %collective-permute-start.5 = (bf16[32,4096]{1,0:T(8,128)(2,1)S(1)}, bf16[32,4096]{1,0:T(8,128)(2,1)S(1)}, u32[]{:S(2)}, u32[]{:S(2)}) collective-permute-start(bf16[32,4096]{1,0:T(8,128)(2,1)S(1)} %collective-permute-done.refs_0_), channel_id=1, source_target_pairs={{0,6},{1,7},{2,4},{3,5},{4,2},{5,3},{6,0},{7,1},{8,14},{9,15},{10,... | collective-permute-start | bytes 786440 | tf_op jit(solution)/shard_map/ppermute | solution.py:221
  22.9 11.2 %collective-permute-start.4 = (bf16[32,4096]{1,0:T(8,128)(2,1)S(1)}, bf16[32,4096]{1,0:T(8,128)(2,1)S(1)}, u32[]{:S(2)}, u32[]{:S(2)}) collective-permute-start(bf16[32,4096]{1,0:T(8,128)(2,1)S(1)} %collective-permute-done.refs_0_), channel_id=1, source_target_pairs={{0,4},{1,5},{2,6},{3,7},{4,0},{5,1},{6,2},{7,3},{8,12},{9,13},{10,... | collective-permute-start | bytes 786440 | tf_op jit(solution)/shard_map/ppermute | solution.py:221
  23.5 10.7 %collective-permute-start.3 = (bf16[32,4096]{1,0:T(8,128)(2,1)S(1)}, bf16[32,4096]{1,0:T(8,128)(2,1)S(1)}, u32[]{:S(2)}, u32[]{:S(2)}) collective-permute-start(bf16[32,4096]{1,0:T(8,128)(2,1)S(1)} %collective-permute-done.refs_0_), channel_id=1, source_target_pairs={{0,2},{1,3},{2,0},{3,1},{4,6},{5,7},{6,4},{7,5},{8,10},{9,11},{10,... | collective-permute-start | bytes 786440 | tf_op jit(solution)/shard_map/ppermute | solution.py:221
  24.0 11.6 %collective-permute-start.7 = (bf16[32,4096]{1,0:T(8,128)(2,1)S(1)}, bf16[32,4096]{1,0:T(8,128)(2,1)S(1)}, u32[]{:S(2)}, u32[]{:S(2)}) collective-permute-start(bf16[32,4096]{1,0:T(8,128)(2,1)S(1)} %collective-permute-done.refs_0_), channel_id=1, source_target_pairs={{0,1},{1,0},{2,3},{3,2},{4,5},{5,4},{6,7},{7,6},{8,9},{9,8},{10,11... | collective-permute-start | bytes 786440 | tf_op jit(solution)/shard_map/ppermute | solution.py:221
  30.7 4.9 %collective-permute-start.10 = (bf16[32,4096]{1,0:T(8,128)(2,1)S(1)}, bf16[32,4096]{1,0:T(8,128)(2,1)S(1)}, u32[]{:S(2)}, u32[]{:S(2)}) collective-permute-start(bf16[32,4096]{1,0:T(8,128)(2,1)S(1)} %collective-permute-done.5.refs_3_), channel_id=1, source_target_pairs={{0,1},{1,0},{2,3},{3,2},{4,5},{5,4},{6,7},{7,6},{8,9},{9,8},{10,11... | collective-permute-start | bytes 786440 | tf_op jit(solution)/shard_map/ppermute | solution.py:221
  34.1 1.5 %collective-permute-start.9 = (bf16[32,4096]{1,0:T(8,128)(2,1)S(1)}, bf16[32,4096]{1,0:T(8,128)(2,1)S(1)}, u32[]{:S(2)}, u32[]{:S(2)}) collective-permute-start(bf16[32,4096]{1,0:T(8,128)(2,1)S(1)} %collective-permute-done.4.refs_2_), channel_id=1, source_target_pairs={{0,1},{1,0},{2,3},{3,2},{4,5},{5,4},{6,7},{7,6},{8,9},{9,8},{10,11... | collective-permute-start | bytes 786440 | tf_op jit(solution)/shard_map/ppermute | solution.py:221
  34.3 1.8 %collective-permute-start.8 = (bf16[32,4096]{1,0:T(8,128)(2,1)S(1)}, bf16[32,4096]{1,0:T(8,128)(2,1)S(1)}, u32[]{:S(2)}, u32[]{:S(2)}) collective-permute-start(bf16[32,4096]{1,0:T(8,128)(2,1)S(1)} %collective-permute-done.3.refs_1_), channel_id=1, source_target_pairs={{0,1},{1,0},{2,3},{3,2},{4,5},{5,4},{6,7},{7,6},{8,9},{9,8},{10,11... | collective-permute-start | bytes 786440 | tf_op jit(solution)/shard_map/ppermute | solution.py:221
  34.6 8.4 %collective-permute-start.6 = (bf16[32,4096]{1,0:T(8,128)(2,1)S(1)}, bf16[32,4096]{1,0:T(8,128)(2,1)S(1)}, u32[]{:S(2)}, u32[]{:S(2)}) collective-permute-start(bf16[32,4096]{1,0:T(8,128)(2,1)S(1)} %collective-permute-done.2.refs_2_), channel_id=1, source_target_pairs={{0,2},{1,3},{2,0},{3,1},{4,6},{5,7},{6,4},{7,5},{8,10},{9,11},{10,... | collective-permute-start | bytes 786440 | tf_op jit(solution)/shard_map/ppermute | solution.py:221
  39.1 3.9 %collective-permute-start.15 = (bf16[64,4096]{1,0:T(8,128)(2,1)S(1)}, bf16[64,4096]{1,0:T(8,128)(2,1)S(1)}, u32[]{:S(2)}, u32[]{:S(2)}) collective-permute-start(bf16[64,4096]{1,0:T(8,128)(2,1)S(1)} %get-tuple-element.60), channel_id=1, source_target_pairs={{0,1},{1,0},{2,3},{3,2},{4,5},{5,4},{6,7},{7,6},{8,9},{9,8},{10,11... | collective-permute-start | bytes 1572872 | tf_op jit(solution)/shard_map/ppermute | solution.py:221
  39.3 3.8 %collective-permute-start.11 = (bf16[32,4096]{1,0:T(8,128)(2,1)S(1)}, bf16[32,4096]{1,0:T(8,128)(2,1)S(1)}, u32[]{:S(2)}, u32[]{:S(2)}) collective-permute-start(bf16[32,4096]{1,0:T(8,128)(2,1)S(1)} %copy-done.3), channel_id=1, source_target_pairs={{0,1},{1,0},{2,3},{3,2},{4,5},{5,4},{6,7},{7,6},{8,9},{9,8},{10,11... | collective-permute-start | bytes 786440 | tf_op jit(solution)/shard_map/ppermute | solution.py:221
  39.7 3.5 %collective-permute-start.12 = (bf16[32,4096]{1,0:T(8,128)(2,1)S(1)}, bf16[32,4096]{1,0:T(8,128)(2,1)S(1)}, u32[]{:S(2)}, u32[]{:S(2)}) collective-permute-start(bf16[32,4096]{1,0:T(8,128)(2,1)S(1)} %collective-permute-done.1.refs_1_), channel_id=1, source_target_pairs={{0,1},{1,0},{2,3},{3,2},{4,5},{5,4},{6,7},{7,6},{8,9},{9,8},{10,11... | collective-permute-start | bytes 786440 | tf_op jit(solution)/shard_map/ppermute | solution.py:221
  39.8 3.3 %collective-permute-start.13 = (bf16[32,4096]{1,0:T(8,128)(2,1)S(1)}, bf16[32,4096]{1,0:T(8,128)(2,1)S(1)}, u32[]{:S(2)}, u32[]{:S(2)}) collective-permute-start(bf16[32,4096]{1,0:T(8,128)(2,1)S(1)} %collective-permute-done.2.refs_2_), channel_id=1, source_target_pairs={{0,1},{1,0},{2,3},{3,2},{4,5},{5,4},{6,7},{7,6},{8,9},{9,8},{10,11... | collective-permute-start | bytes 786440 | tf_op jit(solution)/shard_map/ppermute | solution.py:221
  43.0 1.5 %collective-permute-start.14 = (bf16[32,4096]{1,0:T(8,128)(2,1)S(1)}, bf16[32,4096]{1,0:T(8,128)(2,1)S(1)}, u32[]{:S(2)}, u32[]{:S(2)}) collective-permute-start(bf16[32,4096]{1,0:T(8,128)(2,1)S(1)} %collective-permute-done.6.refs_3_), channel_id=1, source_target_pairs={{0,1},{1,0},{2,3},{3,2},{4,5},{5,4},{6,7},{7,6},{8,9},{9,8},{10,11... | collective-permute-start | bytes 786440 | tf_op jit(solution)/shard_map/ppermute | solution.py:221
  47.6 3.8 %collective-permute-start.16 = (bf16[64,4096]{1,0:T(8,128)(2,1)S(1)}, bf16[64,4096]{1,0:T(8,128)(2,1)S(1)}, u32[]{:S(2)}, u32[]{:S(2)}) collective-permute-start(bf16[64,4096]{1,0:T(8,128)(2,1)S(1)} %get-tuple-element.74), channel_id=1, source_target_pairs={{0,1},{1,0},{2,3},{3,2},{4,5},{5,4},{6,7},{7,6},{8,9},{9,8},{10,11... | collective-permute-start | bytes 1572872 | tf_op jit(solution)/shard_map/ppermute | solution.py:221
  47.9 6.6 %collective-permute-start.20 = (bf16[16,4096]{1,0:T(8,128)(2,1)S(1)}, bf16[16,4096]{1,0:T(8,128)(2,1)S(1)}, u32[]{:S(2)}, u32[]{:S(2)}) collective-permute-start(bf16[16,4096]{1,0:T(8,128)(2,1)S(1)} %get-tuple-element.62), channel_id=1, source_target_pairs={{0,2},{1,3},{2,0},{3,1},{4,6},{5,7},{6,4},{7,5},{8,10},{9,11},{10,... | collective-permute-start | bytes 393224 | tf_op jit(solution)/shard_map/ppermute | solution.py:221
  49.1 7.0 %collective-permute-start.21 = (bf16[16,4096]{1,0:T(8,128)(2,1)S(1)}, bf16[16,4096]{1,0:T(8,128)(2,1)S(1)}, u32[]{:S(2)}, u32[]{:S(2)}) collective-permute-start(bf16[16,4096]{1,0:T(8,128)(2,1)S(1)} %get-tuple-element.63), channel_id=1, source_target_pairs={{0,4},{1,5},{2,6},{3,7},{4,0},{5,1},{6,2},{7,3},{8,12},{9,13},{10,... | collective-permute-start | bytes 393224 | tf_op jit(solution)/shard_map/ppermute | solution.py:221
  50.8 7.3 %collective-permute-start.22 = (bf16[16,4096]{1,0:T(8,128)(2,1)S(1)}, bf16[16,4096]{1,0:T(8,128)(2,1)S(1)}, u32[]{:S(2)}, u32[]{:S(2)}) collective-permute-start(bf16[16,4096]{1,0:T(8,128)(2,1)S(1)} %get-tuple-element.64), channel_id=1, source_target_pairs={{0,6},{1,7},{2,4},{3,5},{4,2},{5,3},{6,0},{7,1},{8,14},{9,15},{10,... | collective-permute-start | bytes 393224 | tf_op jit(solution)/shard_map/ppermute | solution.py:221
  51.5 14.6 %collective-permute-start.17 = (bf16[16,4096]{1,0:T(8,128)(2,1)S(1)}, bf16[16,4096]{1,0:T(8,128)(2,1)S(1)}, u32[]{:S(2)}, u32[]{:S(2)}) collective-permute-start(bf16[16,4096]{1,0:T(8,128)(2,1)S(1)} %get-tuple-element.76), channel_id=1, source_target_pairs={{0,2},{1,3},{2,0},{3,1},{4,6},{5,7},{6,4},{7,5},{8,10},{9,11},{10,... | collective-permute-start | bytes 393224 | tf_op jit(solution)/shard_map/ppermute | solution.py:221
  52.8 13.3 %collective-permute-start.18 = (bf16[16,4096]{1,0:T(8,128)(2,1)S(1)}, bf16[16,4096]{1,0:T(8,128)(2,1)S(1)}, u32[]{:S(2)}, u32[]{:S(2)}) collective-permute-start(bf16[16,4096]{1,0:T(8,128)(2,1)S(1)} %get-tuple-element.77), channel_id=1, source_target_pairs={{0,4},{1,5},{2,6},{3,7},{4,0},{5,1},{6,2},{7,3},{8,12},{9,13},{10,... | collective-permute-start | bytes 393224 | tf_op jit(solution)/shard_map/ppermute | solution.py:221
  54.5 11.5 %collective-permute-start.19 = (bf16[16,4096]{1,0:T(8,128)(2,1)S(1)}, bf16[16,4096]{1,0:T(8,128)(2,1)S(1)}, u32[]{:S(2)}, u32[]{:S(2)}) collective-permute-start(bf16[16,4096]{1,0:T(8,128)(2,1)S(1)} %get-tuple-element.78), channel_id=1, source_target_pairs={{0,6},{1,7},{2,4},{3,5},{4,2},{5,3},{6,0},{7,1},{8,14},{9,15},{10,... | collective-permute-start | bytes 393224 | tf_op jit(solution)/shard_map/ppermute | solution.py:221
  58.2 7.9 %collective-permute-start.23 = (bf16[16,4096]{1,0:T(8,128)(2,1)S(1)}, bf16[16,4096]{1,0:T(8,128)(2,1)S(1)}, u32[]{:S(2)}, u32[]{:S(2)}) collective-permute-start(bf16[16,4096]{1,0:T(8,128)(2,1)S(1)} %shard_map.111), channel_id=1, source_target_pairs={{0,8},{1,9},{2,10},{3,11},{4,12},{5,13},{6,14},{7,15},{8,0},{9,1},... | collective-permute-start | bytes 393224 | tf_op jit(solution)/shard_map/ppermute | solution.py:224
  61.7 4.5 %copy-start.4 = (bf16[32,128]{1,0:T(8,128)(2,1)S(1)}, bf16[32,128]{1,0:T(8,128)(2,1)}, u32[]{:S(2)}) copy-start(bf16[32,128]{1,0:T(8,128)(2,1)} %get-tuple-element.48.select_ref) | copy-start | bytes 24580

commit v3 on v2

--- a/solution.py
+++ b/solution.py
@@ -15,6 +15,10 @@
 SMEM = pl.BlockSpec(memory_space=pltpu.SMEM)
 HBM = pl.BlockSpec(memory_space=pltpu.HBM)
 STEP = 1024
+
+
+def padded(columns):
+    return -(-columns // 128) * 128
 
 
 def params(mib):
@@ -85,44 +89,46 @@
             blocks[k][CAP:, cols] = z[part]
 
 
-def expert_kernel(count, *refs):
-    blocks, refs = refs[:count], refs[count:]
-    gate_ref, up_ref, down_ref, x_ref, z_ref, dg_ref, du_ref, hidden_ref = refs[:8]
-    parts = refs[8:]
+def expert_kernel(count, hidden, *refs):
+    blocks, weights = refs[:count], refs[count : count + 2]
+    shared_ref, unit_ref, *parts = refs[count + 2 :]
+    rows = count * CAP
     for j, block in enumerate(blocks):
-        x_ref[j * CAP : (j + 1) * CAP, :] = block[:CAP, :]
-        z_ref[j * CAP : (j + 1) * CAP, :] = block[CAP:, :]
-    x = x_ref[...]
-    pre_gate = dot(x, gate_ref[...], 1, 1)
-    pre_up = dot(x, up_ref[...], 1, 1)
-    d_hidden = dot(z_ref[...], down_ref[...], 1, 1)
-    sigma = 1.0 / (1.0 + jnp.exp(-pre_gate))
-    active = pre_gate * sigma
-    hidden_ref[...] = (active * pre_up).astype(BF)
-    d_gate = (d_hidden * pre_up * sigma * (1.0 + pre_gate * (1.0 - sigma))).astype(BF)
-    d_up = (d_hidden * active).astype(BF)
-    dg_ref[...] = d_gate
-    du_ref[...] = d_up
-    half = count * CAP // 2
-    width = gate_ref.shape[1]
+        shared_ref[j * CAP : (j + 1) * CAP, :] = block[:CAP, :]
+        shared_ref[rows + j * CAP : rows + (j + 1) * CAP, :] = block[CAP:, :]
+    x, z = shared_ref[:rows, :], shared_ref[rows : 2 * rows, :]
+    terms = []
+    for ref, unit_rows, out in ((weights[0], 0, unit_ref), (weights[1], 2 * rows, shared_ref)):
+        pre_gate = dot(x, ref[:hidden, :], 1, 1)
+        pre_up = dot(x, ref[hidden : 2 * hidden, :], 1, 1)
+        d_hidden = dot(z, ref[2 * hidden :, :], 1, 1)
+        sigma = 1.0 / (1.0 + jnp.exp(-pre_gate))
+        active = pre_gate * sigma
+        d_gate = (d_hidden * pre_up * sigma * (1.0 + pre_gate * (1.0 - sigma))).astype(BF)
+        d_up = (d_hidden * active).astype(BF)
+        for m, unit in enumerate((d_gate, d_up, (active * pre_up).astype(BF))):
+            at = m * padded(hidden)
+            out[unit_rows : unit_rows + rows, at : at + hidden] = unit
+        terms += [(d_gate, ref, 0), (d_up, ref, hidden)]
+    width = x.shape[1]
     step = min(STEP, width)
     for at in range(0, width, step):
         cols = pl.ds(at, step)
-        value = dot(d_gate, gate_ref[:, cols], 1, 0) + dot(d_up, up_ref[:, cols], 1, 0)
+        value = sum(dot(left, ref[row : row + hidden, cols], 1, 0) for left, ref, row in terms)
         value = value.astype(BF)
-        parts[0][:, cols] = value[:half]
-        parts[1][:, cols] = value[half:]
+        for j, part in enumerate(parts):
+            part[:, cols] = value[j * CAP : (j + 1) * CAP]
 
 
 def grad_kernel(count, *refs):
-    lefts, rights, outs = refs[: 3 * count], refs[3 * count : 5 * count], refs[5 * count :]
-    for m, out in enumerate(outs):
-        total = None
-        for j in range(count):
-            right = rights[j + (count if m == 2 else 0)]
-            term = dot(lefts[m * count + j][...], right[...], 0, 0)
-            total = term if total is None else total + term
-        out[...] = total.astype(BF)
+    units, rows, outs = refs[:count], refs[count : 2 * count], refs[2 * count :]
+    hidden, size = outs[0].shape[0], rows[0].shape[0] // 2
+    x = jnp.concatenate([r[:size, :] for r in rows], axis=0)
+    z = jnp.concatenate([r[size:, :] for r in rows], axis=0)
+    for m, (out, right) in enumerate(zip(outs, (x, x, z))):
+        at = m * padded(hidden)
+        left = jnp.concatenate([u[:, at : at + hidden] for u in units], axis=0)
+        out[...] = dot(left, right, 0, 0).astype(BF)
 
 
 def sum_kernel(terms, *refs):
@@ -187,24 +193,33 @@
     )(own, expert_ids, gate_values, tokens, upstream)
 
 
-def fetch_kernel(*refs):
-    count = len(refs) // 2
-    for source, out in zip(refs[:count], refs[count:]):
-        out[...] = source[...]
-
-
-def grads(lefts, rights):
-    count = len(rights) // 2
-    hidden, width = lefts[0].shape[1], rights[0].shape[1]
+def copy_kernel(source, out):
+    out[...] = source[...]
+
+
+def fetch_kernel(gate_ref, up_ref, down_ref, out_ref):
+    rows = gate_ref.shape[0]
+    for m, ref in enumerate((gate_ref, up_ref, down_ref)):
+        out_ref[m * rows : (m + 1) * rows, :] = ref[...]
+
+
+def grads(hidden, results):
+    count, width = 2 * len(results), results[0][0].shape[1]
     step = min(STEP, width)
+    size = results[0][1].shape[0]
+    units, unit_specs, rows = [], [], []
+    for mine, unit, other in results:
+        units += [unit, other]
+        unit_specs += [whole(unit), pl.BlockSpec((size, 3 * padded(hidden)), lambda i: (2, 0))]
+        rows += [mine, other]
     return pl.pallas_call(
         functools.partial(grad_kernel, count),
         grid=(width // step,),
         out_shape=[shape(hidden, width)] * 3,
-        in_specs=[whole(a) for a in lefts] + [columns(a.shape[0], step) for a in rights],
+        in_specs=unit_specs + [columns(2 * size, step)] * count,
         out_specs=[columns(hidden, step)] * 3,
         compiler_params=params(24),
-    )(*lefts, *rights)
+    )(*units, *rows)
 
 
 def on_device(tokens, upstream, expert_ids, gate_values, w_gate, w_up, w_down):
@@ -212,9 +227,6 @@
     window = devices // TILES
     width = tokens.shape[1]
     hidden = w_gate.shape[1]
-    gate, up, down = [
-        call(fetch_kernel, shape(*w.shape[1:]), w[0], mib=8) for w in (w_gate, w_up, w_down)
-    ]
     own = (lax.axis_index("exp") // TILES).astype(jnp.int32)[None]
 
     def swap(a, bits):
@@ -224,10 +236,7 @@
         return lax.ppermute(a, "exp", [(i, (i + k * TILES) % devices) for i in range(devices)])
 
     def near(block):
-        return [block] + [swap(block, bits) for bits in (2, 4, 6)]
-
-    def both(blocks):
-        return blocks + [swap(b, 1) for b in blocks]
+        return [block] + [swap(block, bits) for bits in (6, 4, 2)]
 
     def later(values, *first):
         count = len(values)
@@ -236,23 +245,26 @@
     def expert(blocks):
         rows = len(blocks) * CAP
         return call(
-            functools.partial(expert_kernel, len(blocks)),
-            [shape(rows, width)] * 2 + [shape(rows, hidden)] * 3 + [shape(rows // 2, width)] * 2,
-            *blocks, gate, up, down,
+            functools.partial(expert_kernel, len(blocks), hidden),
+            [shape(3 * rows, width), shape(rows, 3 * padded(hidden))] + [shape(CAP, width)] * len(blocks),
+            *blocks, weights, sibling,
         )
 
     select, *packed = pack(window, own, expert_ids.T, gate_values.T, tokens, upstream)
     crossed = [turn(packed[k], k) for k in range(1, window)]
     mine = packed[0]
-    across, along = swap(mine, 2), swap(mine, 4)
-    *crossed, across, along, gate, up, down = later([*crossed, across, along, gate, up, down])
-
-    def halve(result):
-        kept, other = result[5:]
-        return call(functools.partial(sum_kernel, 2), [shape(CAP, width)] * 4, kept, swap(other, 1))
-
-    def gather(pieces):
-        pieces = [pieces[0]] + [swap(pieces[j], 2 * j) for j in (1, 2, 3)]
+    along, across = swap(mine, 4), swap(mine, 2)
+    weights = call(
+        fetch_kernel, shape(3 * hidden, width), *later([w_gate[0], w_up[0], w_down[0]], select)
+    )
+    crossed = [call(copy_kernel, shape(*c.shape), c, mib=4) for c in crossed]
+    *crossed, along, across, weights = later([*crossed, along, across, weights])
+    sibling = swap(weights, 1)
+
+    def send(pieces, order=(6, 4, 2)):
+        return [pieces[0]] + [swap(piece, bits) for piece, bits in zip(pieces[1:], order)]
+
+    def total(pieces):
         return call(functools.partial(sum_kernel, 4), [shape(CAP, width)], *pieces)[0]
 
     results, returned = [], []
@@ -260,18 +272,17 @@
         blocks = near(crossed[k - 1])
         if k == window - 1:
             (along,) = later([along], *blocks)
-        results.append(expert(both(blocks)))
-        pieces = halve(results[-1])
-        returned.append(turn(gather(pieces), window - k))
-    (corner,) = later([swap(along, 2)], results[-1][5])
-    own_blocks = later(both([mine, across, along, corner]), *pieces)
-    results.append(expert(own_blocks))
-    returned.append(gather(halve(results[-1])))
-    results = results[-1:] + results[:-1]
-    returned = returned[-1:] + returned[:-1]
-    grad_gate, grad_up, grad_down = grads(
-        [r[m] for m in (2, 3, 4) for r in results], [r[m] for m in (0, 1) for r in results]
-    )
+        shared, unit, *pieces = expert(blocks)
+        results.append((shared, unit, swap(shared, 1)))
+        sent = send(pieces)
+        whole_piece = total(sent)
+        returned.append(turn(whole_piece, window - k))
+    corner = swap(along, 2)
+    own = expert([mine, across, along, corner])
+    shared, unit, *own_pieces = later(own, whole_piece)
+    results.append((shared, unit, swap(shared, 1)))
+    grad_gate, grad_up, grad_down = grads(hidden, results)
+    returned = [total(later(send(own_pieces, (2, 4, 6)), grad_gate)), *returned]
     d_tokens = call(
         functools.partial(unpack_kernel, window), shape(*tokens.shape), select, *returned
     )

time: 67.8 us -> 65.4 us (0.965)
  starting transfers between devices: 24.8 us -> 21.2 us
  Pallas kernels: 15.9 us -> 17.2 us
    pallas_call x10 -> x7, Pallas kernels: 8.2 us -> 10.5 us  [call(): pl.pallas_call(kernel, out_shape=out_shape, in_specs=[VMEM] * len(args),...]
    ppermute x22 -> x15, starting transfers between devices: 17.3 us -> 15.2 us  [swap(): return lax.ppermute(a, 'exp', [(i, i ^ bits) for i in range(devices)])]
    ppermute x2, starting transfers between devices: 7.53 us -> 5.96 us  [turn(): lax.ppermute(a, 'exp', [(i, (i + k * TILES) % devices) for i in range(dev...]
    pallas_call x1, Pallas kernels: 4.38 us -> 3.43 us  [grads(): pl.pallas_call(functools.partial(grad_kernel, count), grid=(width // step...]
    ppermute x22 -> x15, waiting for transfers between devices: 17.3 us -> 17.3 us  [swap(): return lax.ppermute(a, 'exp', [(i, i ^ bits) for i in range(devices)])]
  transfers between devices with their start and end apart: 24 -> 17, of which waited for: 10 -> 7; matrix products, arithmetic and copies ran while one was open for 0% -> 0% of each run, Pallas kernels for 12% -> 19%
where the time goes in v3:
time: 65.4 us; the launch traced here: 65.2 us
  waiting for transfers between devices  23.3 us (36%)
  starting transfers between devices  21.2 us (32%)
  Pallas kernels  17.2 us (26%)
  local copies, waits for them, and re-layouts  2.83 us (4%)
  between operations  0.75 us (1%)
    ppermute x15, waiting for transfers between devices, swap(): return lax.ppermute(a, 'exp', [(i, i ^ bits) for i in range(devices)])  17.3 us
    ppermute x15, starting transfers between devices, swap(): return lax.ppermute(a, 'exp', [(i, i ^ bits) for i in range(devices)])  15.2 us
    pallas_call x7, Pallas kernels, call(): pl.pallas_call(kernel, out_shape=out_shape, in_specs=[VMEM] * len(args),...  10.5 us
    ppermute x2, waiting for transfers between devices, turn(): lax.ppermute(a, 'exp', [(i, (i + k * TILES) % devices) for i in range(dev...  6.02 us
    ppermute x2, starting transfers between devices, turn(): lax.ppermute(a, 'exp', [(i, (i + k * TILES) % devices) for i in range(dev...  5.96 us
    pallas_call x1, Pallas kernels, grads(): pl.pallas_call(functools.partial(grad_kernel, count), grid=(width // step...  3.43 us
    pallas_call x1, Pallas kernels, pack(): pl.pallas_call(functools.partial(pack_kernel, window), out_shape=outs, in...  3.31 us
    unnamed x10, local copies, waits for them, and re-layouts  2.83 us
  transfers between devices with their start and end apart: 17, of which 7 were waited for; matrix products, arithmetic and copies ran while one was open for 0% of the time, Pallas kernels for 19%

profile of v3, /device:TPU:0, one launch (start us, length us, event | category | flops | bytes accessed | tf_op | source)
XLA Modules:
  0.0 65.2 jit_solution(12129952051237909157)
XLA Ops:
  0.7 3.3 %shard_map.102 = (bf16[32,128]{1,0:T(8,128)(2,1)}, bf16[32,4096]{1,0:T(8,128)(2,1)}, bf16[32,4096]{1,0:T(8,128)(2,1)}) custom-call(s32[1]{0:T(128)} %bitcast.own_ref, s32[8,128]{1,0:T(8,128)} %bitcast.12, f32[8,128]{1,0:T(8,128)} %bitcast.13, bf16[128,4096]{1,0:T(8,128)(2,1)} %tokens_hbm.1, bf16[128,4096]{1,0:T(8,128)(2,1)} %upstream_hbm.1), custom_call_target="tpu_custom_call" | custom-call | tf_op jit(solution)/shard_map/pallas_call | solution.py:179
  4.0 4.1 %collective-permute-start = (bf16[32,4096]{1,0:T(8,128)(2,1)}, bf16[32,4096]{1,0:T(8,128)(2,1)S(1)}, u32[]{:S(2)}, u32[]{:S(2)}) collective-permute-start(bf16[32,4096]{1,0:T(8,128)(2,1)} %get-tuple-element.42), channel_id=1, source_target_pairs={{0,8},{1,9},{2,10},{3,11},{4,12},{5,13},{6,14},{7,15},{8,0},{9,1},... | collective-permute-start | bytes 786440 | tf_op jit(solution)/shard_map/ppermute | solution.py:236
  8.1 1.6 %collective-permute-start.1 = (bf16[32,4096]{1,0:T(8,128)(2,1)}, bf16[32,4096]{1,0:T(8,128)(2,1)S(1)}, u32[]{:S(2)}, u32[]{:S(2)}) collective-permute-start(bf16[32,4096]{1,0:T(8,128)(2,1)} %get-tuple-element.41.refs_0_), channel_id=1, source_target_pairs={{0,4},{1,5},{2,6},{3,7},{4,0},{5,1},{6,2},{7,3},{8,12},{9,13},{10,... | collective-permute-start | bytes 786440 | tf_op jit(solution)/shard_map/ppermute | solution.py:233
  9.6 1.5 %collective-permute-start.2 = (bf16[32,4096]{1,0:T(8,128)(2,1)}, bf16[32,4096]{1,0:T(8,128)(2,1)S(1)}, u32[]{:S(2)}, u32[]{:S(2)}) collective-permute-start(bf16[32,4096]{1,0:T(8,128)(2,1)} %get-tuple-element.41.refs_0_), channel_id=1, source_target_pairs={{0,2},{1,3},{2,0},{3,1},{4,6},{5,7},{6,4},{7,5},{8,10},{9,11},{10,... | collective-permute-start | bytes 786440 | tf_op jit(solution)/shard_map/ppermute | solution.py:233
  11.2 1.4 %copy-done.1 = bf16[1,192,4096]{2,1,0:T(8,128)(2,1)S(1)} copy-done((bf16[1,192,4096]{2,1,0:T(8,128)(2,1)S(1)}, bf16[1,192,4096]{2,1,0:T(8,128)(2,1)}, u32[]{:S(2)}) %copy-start.1) | copy-done | bytes 1572888
  12.6 1.4 %copy-done.2 = bf16[1,192,4096]{2,1,0:T(8,128)(2,1)S(1)} copy-done((bf16[1,192,4096]{2,1,0:T(8,128)(2,1)S(1)}, bf16[1,192,4096]{2,1,0:T(8,128)(2,1)}, u32[]{:S(2)}) %copy-start.2) | copy-done | bytes 1572888
  14.0 0.3 shard_map.104.refs_4_
  14.3 6.0 %collective-permute-done.source = bf16[32,4096]{1,0:T(8,128)(2,1)S(1)} collective-permute-done((bf16[32,4096]{1,0:T(8,128)(2,1)}, bf16[32,4096]{1,0:T(8,128)(2,1)S(1)}, u32[]{:S(2)}, u32[]{:S(2)}) %collective-permute-start) | collective-permute-done | bytes 262176 | tf_op jit(solution)/shard_map/ppermute | solution.py:236
  20.3 0.2 collective-permute-done.1.refs_2_
  20.5 2.4 %collective-permute-start.3 = (bf16[32,4096]{1,0:T(8,128)(2,1)S(1)}, bf16[32,4096]{1,0:T(8,128)(2,1)S(1)}, u32[]{:S(2)}, u32[]{:S(2)}) collective-permute-start(bf16[32,4096]{1,0:T(8,128)(2,1)S(1)} %shard_map.103.refs_0_), channel_id=1, source_target_pairs={{0,6},{1,7},{2,4},{3,5},{4,2},{5,3},{6,0},{7,1},{8,14},{9,15},{10,... | collective-permute-start | bytes 786440 | tf_op jit(solution)/shard_map/ppermute | solution.py:233
  23.0 0.6 collective-permute-start.4
  23.6 0.5 collective-permute-start.5
  24.0 6.6 %collective-permute-done.3.refs_1_ = bf16[32,4096]{1,0:T(8,128)(2,1)S(1)} collective-permute-done((bf16[32,4096]{1,0:T(8,128)(2,1)S(1)}, bf16[32,4096]{1,0:T(8,128)(2,1)S(1)}, u32[]{:S(2)}, u32[]{:S(2)}) %collective-permute-start.3) | collective-permute-done | bytes 262176 | tf_op jit(solution)/shard_map/ppermute | solution.py:233
  30.6 5.3 %collective-permute-done.4.refs_2_ = bf16[32,4096]{1,0:T(8,128)(2,1)S(1)} collective-permute-done((bf16[32,4096]{1,0:T(8,128)(2,1)S(1)}, bf16[32,4096]{1,0:T(8,128)(2,1)S(1)}, u32[]{:S(2)}, u32[]{:S(2)}) %collective-permute-start.4) | collective-permute-done | bytes 262176 | tf_op jit(solution)/shard_map/ppermute | solution.py:233
  35.9 1.4 %collective-permute-start.6 = (bf16[32,4096]{1,0:T(8,128)(2,1)S(1)}, bf16[32,4096]{1,0:T(8,128)(2,1)S(1)}, u32[]{:S(2)}, u32[]{:S(2)}) collective-permute-start(bf16[32,4096]{1,0:T(8,128)(2,1)S(1)} %collective-permute-done.1.refs_2_), channel_id=1, source_target_pairs={{0,2},{1,3},{2,0},{3,1},{4,6},{5,7},{6,4},{7,5},{8,10},{9,11},{10,... | collective-permute-start | bytes 786440 | tf_op jit(solution)/shard_map/ppermute | solution.py:233
  37.3 4.3 %shard_map.106 = (bf16[192,4096]{1,0:T(8,128)(2,1)S(1)}, bf16[64,768]{1,0:T(8,128)(2,1)S(1)}, bf16[16,4096]{1,0:T(8,128)(2,1)S(1)}, bf16[16,4096]{1,0:T(8,128)(2...) custom-call(bf16[32,4096]{1,0:T(8,128)(2,1)S(1)} %shard_map.103.refs_0_, ...), custom_call_target="tpu_custom_call" | custom-call | tf_op jit(solution)/shard_map/pallas_call | solution.py:155
  41.6 0.7 %collective-permute-start.10 = (bf16[16,4096]{1,0:T(8,128)(2,1)S(1)}, bf16[16,4096]{1,0:T(8,128)(2,1)S(1)}, u32[]{:S(2)}, u32[]{:S(2)}) collective-permute-start(bf16[16,4096]{1,0:T(8,128)(2,1)S(1)} %get-tuple-element.60), channel_id=1, source_target_pairs={{0,2},{1,3},{2,0},{3,1},{4,6},{5,7},{6,4},{7,5},{8,10},{9,11},{10,... | collective-permute-start | bytes 393224 | tf_op jit(solution)/shard_map/ppermute | solution.py:233
  42.3 2.3 %collective-permute-start.8 = (bf16[16,4096]{1,0:T(8,128)(2,1)S(1)}, bf16[16,4096]{1,0:T(8,128)(2,1)S(1)}, u32[]{:S(2)}, u32[]{:S(2)}) collective-permute-start(bf16[16,4096]{1,0:T(8,128)(2,1)S(1)} %get-tuple-element.58), channel_id=1, source_target_pairs={{0,6},{1,7},{2,4},{3,5},{4,2},{5,3},{6,0},{7,1},{8,14},{9,15},{10,... | collective-permute-start | bytes 393224 | tf_op jit(solution)/shard_map/ppermute | solution.py:233
  44.6 0.6 collective-permute-start.9
  45.2 4.3 %shard_map.105 = (bf16[192,4096]{1,0:T(8,128)(2,1)S(1)}, bf16[64,768]{1,0:T(8,128)(2,1)S(1)}, bf16[16,4096]{1,0:T(8,128)(2,1)S(1)}, bf16[16,4096]{1,0:T(8,128)(2...) custom-call(bf16[32,4096]{1,0:T(8,128)(2,1)S(1)} %copy-done.3, ...), custom_call_target="tpu_custom_call" | custom-call | tf_op jit(solution)/shard_map/pallas_call | solution.py:155
  49.5 0.2 collective-permute-done.10.refs_3_
  49.6 1.2 %collective-permute-done.9.refs_2_ = bf16[16,4096]{1,0:T(8,128)(2,1)S(1)} collective-permute-done((bf16[16,4096]{1,0:T(8,128)(2,1)S(1)}, bf16[16,4096]{1,0:T(8,128)(2,1)S(1)}, u32[]{:S(2)}, u32[]{:S(2)}) %collective-permute-start.9) | collective-permute-done | bytes 131104 | tf_op jit(solution)/shard_map/ppermute | solution.py:233
  50.8 0.1 shard_map.107
  50.9 0.1 collective-permute-start.15
  51.0 0.5 collective-permute-start.11
  51.5 1.5 %collective-permute-start.12 = (bf16[16,4096]{1,0:T(8,128)(2,1)S(1)}, bf16[16,4096]{1,0:T(8,128)(2,1)S(1)}, u32[]{:S(2)}, u32[]{:S(2)}) collective-permute-start(bf16[16,4096]{1,0:T(8,128)(2,1)S(1)} %get-tuple-element.63), channel_id=1, source_target_pairs={{0,4},{1,5},{2,6},{3,7},{4,0},{5,1},{6,2},{7,3},{8,12},{9,13},{10,... | collective-permute-start | bytes 393224 | tf_op jit(solution)/shard_map/ppermute | solution.py:233
  53.0 1.5 %collective-permute-start.13 = (bf16[16,4096]{1,0:T(8,128)(2,1)S(1)}, bf16[16,4096]{1,0:T(8,128)(2,1)S(1)}, u32[]{:S(2)}, u32[]{:S(2)}) collective-permute-start(bf16[16,4096]{1,0:T(8,128)(2,1)S(1)} %get-tuple-element.64), channel_id=1, source_target_pairs={{0,6},{1,7},{2,4},{3,5},{4,2},{5,3},{6,0},{7,1},{8,14},{9,15},{10,... | collective-permute-start | bytes 393224 | tf_op jit(solution)/shard_map/ppermute | solution.py:233
  54.6 1.9 %collective-permute-start.16 = (bf16[16,4096]{1,0:T(8,128)(2,1)S(1)}, bf16[16,4096]{1,0:T(8,128)(2,1)S(1)}, u32[]{:S(2)}, u32[]{:S(2)}) collective-permute-start(bf16[16,4096]{1,0:T(8,128)(2,1)S(1)} %shard_map.107), channel_id=1, source_target_pairs={{0,8},{1,9},{2,10},{3,11},{4,12},{5,13},{6,14},{7,15},{8,0},{9,1},... | collective-permute-start | bytes 393224 | tf_op jit(solution)/shard_map/ppermute | solution.py:236
  56.4 3.4 %shard_map.108 = (bf16[192,4096]{1,0:T(8,128)(2,1)}, bf16[192,4096]{1,0:T(8,128)(2,1)}, bf16[192,4096]{1,0:T(8,128)(2,1)}) custom-call(bf16[64,768]{1,0:T(8,128)(2,1)S(1)} %get-tuple-element.65.refs_0_, bf16[192,4096]{1,0:T(8,128)(2,1)S(1)} %collective-permute-done.14.refs_1_.refs_5_, bf16[64,768]{1,0:T(8,128)(2,1)S(1)} %get-tuple-element.67.refs_2_, ...), custom_call_target="tpu_custom_call" | custom-call | tf_op jit(solution)/shard_map/pallas_call | solution.py:215
  59.9 3.8 %collective-permute-done.13.refs_3_ = bf16[16,4096]{1,0:T(8,128)(2,1)S(1)} collective-permute-done((bf16[16,4096]{1,0:T(8,128)(2,1)S(1)}, bf16[16,4096]{1,0:T(8,128)(2,1)S(1)}, u32[]{:S(2)}, u32[]{:S(2)}) %collective-permute-start.13) | collective-permute-done | bytes 131104 | tf_op jit(solution)/shard_map/ppermute | solution.py:233
  63.7 0.1 shard_map.109.refs_0_
  63.8 1.4 %shard_map.110 = bf16[128,4096]{1,0:T(8,128)(2,1)} custom-call(bf16[32,128]{1,0:T(8,128)(2,1)S(1)} %copy-done.4, bf16[16,4096]{1,0:T(8,128)(2,1)S(1)} %shard_map.109.refs_0_, bf16[16,4096]{1,0:T(8,128)(2,1)S(1)} %collective-permute-done.16.refs_1_), custom_call_target="tpu_custom_call" | custom-call | tf_op jit(solution)/shard_map/pallas_call | solution.py:155
  (21 shorter events, 0.1 us)
Async XLA Ops:
  0.6 10.5 %copy-start = (bf16[1,192,4096]{2,1,0:T(8,128)(2,1)S(1)}, bf16[1,192,4096]{2,1,0:T(8,128)(2,1)}, u32[]{:S(2)}) copy-start(bf16[1,192,4096]{2,1,0:T(8,128)(2,1)} %param.11) | copy-start | bytes 4718596
  4.0 16.3 %collective-permute-start = (bf16[32,4096]{1,0:T(8,128)(2,1)}, bf16[32,4096]{1,0:T(8,128)(2,1)S(1)}, u32[]{:S(2)}, u32[]{:S(2)}) collective-permute-start(bf16[32,4096]{1,0:T(8,128)(2,1)} %get-tuple-element.42), channel_id=1, source_target_pairs={{0,8},{1,9},{2,10},{3,11},{4,12},{5,13},{6,14},{7,15},{8,0},{9,1},... | collective-permute-start | bytes 786440 | tf_op jit(solution)/shard_map/ppermute | solution.py:236
  8.1 12.4 %collective-permute-start.1 = (bf16[32,4096]{1,0:T(8,128)(2,1)}, bf16[32,4096]{1,0:T(8,128)(2,1)S(1)}, u32[]{:S(2)}, u32[]{:S(2)}) collective-permute-start(bf16[32,4096]{1,0:T(8,128)(2,1)} %get-tuple-element.41.refs_0_), channel_id=1, source_target_pairs={{0,4},{1,5},{2,6},{3,7},{4,0},{5,1},{6,2},{7,3},{8,12},{9,13},{10,... | collective-permute-start | bytes 786440 | tf_op jit(solution)/shard_map/ppermute | solution.py:233
  9.6 10.9 %collective-permute-start.2 = (bf16[32,4096]{1,0:T(8,128)(2,1)}, bf16[32,4096]{1,0:T(8,128)(2,1)S(1)}, u32[]{:S(2)}, u32[]{:S(2)}) collective-permute-start(bf16[32,4096]{1,0:T(8,128)(2,1)} %get-tuple-element.41.refs_0_), channel_id=1, source_target_pairs={{0,2},{1,3},{2,0},{3,1},{4,6},{5,7},{6,4},{7,5},{8,10},{9,11},{10,... | collective-permute-start | bytes 786440 | tf_op jit(solution)/shard_map/ppermute | solution.py:233
  11.2 1.4 %copy-start.1 = (bf16[1,192,4096]{2,1,0:T(8,128)(2,1)S(1)}, bf16[1,192,4096]{2,1,0:T(8,128)(2,1)}, u32[]{:S(2)}) copy-start(bf16[1,192,4096]{2,1,0:T(8,128)(2,1)} %param.12) | copy-start | bytes 4718596
  12.6 1.4 %copy-start.2 = (bf16[1,192,4096]{2,1,0:T(8,128)(2,1)S(1)}, bf16[1,192,4096]{2,1,0:T(8,128)(2,1)}, u32[]{:S(2)}) copy-start(bf16[1,192,4096]{2,1,0:T(8,128)(2,1)} %param.13) | copy-start | bytes 4718596
  20.3 24.8 %copy-start.3 = (bf16[32,4096]{1,0:T(8,128)(2,1)S(1)}, bf16[32,4096]{1,0:T(8,128)(2,1)}, u32[]{:S(2)}) copy-start(bf16[32,4096]{1,0:T(8,128)(2,1)} %get-tuple-element.41.refs_0_) | copy-start | bytes 786436
  20.5 16.8 %collective-permute-start.7 = (bf16[576,4096]{1,0:T(8,128)(2,1)S(1)}, bf16[576,4096]{1,0:T(8,128)(2,1)S(1)}, u32[]{:S(2)}, u32[]{:S(2)}) collective-permute-start(bf16[576,4096]{1,0:T(8,128)(2,1)S(1)} %shard_map.104.refs_4_), channel_id=1, source_target_pairs={{0,1},{1,0},{2,3},{3,2},{4,5},{5,4},{6,7},{7,6},{8,9},{9,8},{10,11... | collective-permute-start | bytes 14155784 | tf_op jit(solution)/shard_map/ppermute | solution.py:233
  20.5 10.1 %collective-permute-start.3 = (bf16[32,4096]{1,0:T(8,128)(2,1)S(1)}, bf16[32,4096]{1,0:T(8,128)(2,1)S(1)}, u32[]{:S(2)}, u32[]{:S(2)}) collective-permute-start(bf16[32,4096]{1,0:T(8,128)(2,1)S(1)} %shard_map.103.refs_0_), channel_id=1, source_target_pairs={{0,6},{1,7},{2,4},{3,5},{4,2},{5,3},{6,0},{7,1},{8,14},{9,15},{10,... | collective-permute-start | bytes 786440 | tf_op jit(solution)/shard_map/ppermute | solution.py:233
  23.0 12.9 %collective-permute-start.4 = (bf16[32,4096]{1,0:T(8,128)(2,1)S(1)}, bf16[32,4096]{1,0:T(8,128)(2,1)S(1)}, u32[]{:S(2)}, u32[]{:S(2)}) collective-permute-start(bf16[32,4096]{1,0:T(8,128)(2,1)S(1)} %shard_map.103.refs_0_), channel_id=1, source_target_pairs={{0,4},{1,5},{2,6},{3,7},{4,0},{5,1},{6,2},{7,3},{8,12},{9,13},{10,... | collective-permute-start | bytes 786440 | tf_op jit(solution)/shard_map/ppermute | solution.py:233
  23.6 12.3 %collective-permute-start.5 = (bf16[32,4096]{1,0:T(8,128)(2,1)S(1)}, bf16[32,4096]{1,0:T(8,128)(2,1)S(1)}, u32[]{:S(2)}, u32[]{:S(2)}) collective-permute-start(bf16[32,4096]{1,0:T(8,128)(2,1)S(1)} %shard_map.103.refs_0_), channel_id=1, source_target_pairs={{0,2},{1,3},{2,0},{3,1},{4,6},{5,7},{6,4},{7,5},{8,10},{9,11},{10,... | collective-permute-start | bytes 786440 | tf_op jit(solution)/shard_map/ppermute | solution.py:233
  35.9 9.3 %collective-permute-start.6 = (bf16[32,4096]{1,0:T(8,128)(2,1)S(1)}, bf16[32,4096]{1,0:T(8,128)(2,1)S(1)}, u32[]{:S(2)}, u32[]{:S(2)}) collective-permute-start(bf16[32,4096]{1,0:T(8,128)(2,1)S(1)} %collective-permute-done.1.refs_2_), channel_id=1, source_target_pairs={{0,2},{1,3},{2,0},{3,1},{4,6},{5,7},{6,4},{7,5},{8,10},{9,11},{10,... | collective-permute-start | bytes 786440 | tf_op jit(solution)/shard_map/ppermute | solution.py:233
  41.6 8.0 %collective-permute-start.10 = (bf16[16,4096]{1,0:T(8,128)(2,1)S(1)}, bf16[16,4096]{1,0:T(8,128)(2,1)S(1)}, u32[]{:S(2)}, u32[]{:S(2)}) collective-permute-start(bf16[16,4096]{1,0:T(8,128)(2,1)S(1)} %get-tuple-element.60), channel_id=1, source_target_pairs={{0,2},{1,3},{2,0},{3,1},{4,6},{5,7},{6,4},{7,5},{8,10},{9,11},{10,... | collective-permute-start | bytes 393224 | tf_op jit(solution)/shard_map/ppermute | solution.py:233
  42.3 7.3 %collective-permute-start.8 = (bf16[16,4096]{1,0:T(8,128)(2,1)S(1)}, bf16[16,4096]{1,0:T(8,128)(2,1)S(1)}, u32[]{:S(2)}, u32[]{:S(2)}) collective-permute-start(bf16[16,4096]{1,0:T(8,128)(2,1)S(1)} %get-tuple-element.58), channel_id=1, source_target_pairs={{0,6},{1,7},{2,4},{3,5},{4,2},{5,3},{6,0},{7,1},{8,14},{9,15},{10,... | collective-permute-start | bytes 393224 | tf_op jit(solution)/shard_map/ppermute | solution.py:233
  44.6 6.3 %collective-permute-start.9 = (bf16[16,4096]{1,0:T(8,128)(2,1)S(1)}, bf16[16,4096]{1,0:T(8,128)(2,1)S(1)}, u32[]{:S(2)}, u32[]{:S(2)}) collective-permute-start(bf16[16,4096]{1,0:T(8,128)(2,1)S(1)} %get-tuple-element.59), channel_id=1, source_target_pairs={{0,4},{1,5},{2,6},{3,7},{4,0},{5,1},{6,2},{7,3},{8,12},{9,13},{10,... | collective-permute-start | bytes 393224 | tf_op jit(solution)/shard_map/ppermute | solution.py:233
  45.2 9.4 %collective-permute-start.14 = (bf16[192,4096]{1,0:T(8,128)(2,1)S(1)}, bf16[192,4096]{1,0:T(8,128)(2,1)S(1)}, u32[]{:S(2)}, u32[]{:S(2)}) collective-permute-start(bf16[192,4096]{1,0:T(8,128)(2,1)S(1)} %get-tuple-element.66.refs_4_), channel_id=1, source_target_pairs={{0,1},{1,0},{2,3},{3,2},{4,5},{5,4},{6,7},{7,6},{8,9},{9,8},{10,11... | collective-permute-start | bytes 4718600 | tf_op jit(solution)/shard_map/ppermute | solution.py:233
  50.9 5.5 %collective-permute-start.15 = (bf16[192,4096]{1,0:T(8,128)(2,1)S(1)}, bf16[192,4096]{1,0:T(8,128)(2,1)S(1)}, u32[]{:S(2)}, u32[]{:S(2)}) collective-permute-start(bf16[192,4096]{1,0:T(8,128)(2,1)S(1)} %get-tuple-element.68.refs_6_), channel_id=1, source_target_pairs={{0,1},{1,0},{2,3},{3,2},{4,5},{5,4},{6,7},{7,6},{8,9},{9,8},{10,11... | collective-permute-start | bytes 4718600 | tf_op jit(solution)/shard_map/ppermute | solution.py:233
  51.0 8.9 %collective-permute-start.11 = (bf16[16,4096]{1,0:T(8,128)(2,1)S(1)}, bf16[16,4096]{1,0:T(8,128)(2,1)S(1)}, u32[]{:S(2)}, u32[]{:S(2)}) collective-permute-start(bf16[16,4096]{1,0:T(8,128)(2,1)S(1)} %get-tuple-element.62), channel_id=1, source_target_pairs={{0,2},{1,3},{2,0},{3,1},{4,6},{5,7},{6,4},{7,5},{8,10},{9,11},{10,... | collective-permute-start | bytes 393224 | tf_op jit(solution)/shard_map/ppermute | solution.py:233
  51.5 8.3 %collective-permute-start.12 = (bf16[16,4096]{1,0:T(8,128)(2,1)S(1)}, bf16[16,4096]{1,0:T(8,128)(2,1)S(1)}, u32[]{:S(2)}, u32[]{:S(2)}) collective-permute-start(bf16[16,4096]{1,0:T(8,128)(2,1)S(1)} %get-tuple-element.63), channel_id=1, source_target_pairs={{0,4},{1,5},{2,6},{3,7},{4,0},{5,1},{6,2},{7,3},{8,12},{9,13},{10,... | collective-permute-start | bytes 393224 | tf_op jit(solution)/shard_map/ppermute | solution.py:233
  53.0 10.7 %collective-permute-start.13 = (bf16[16,4096]{1,0:T(8,128)(2,1)S(1)}, bf16[16,4096]{1,0:T(8,128)(2,1)S(1)}, u32[]{:S(2)}, u32[]{:S(2)}) collective-permute-start(bf16[16,4096]{1,0:T(8,128)(2,1)S(1)} %get-tuple-element.64), channel_id=1, source_target_pairs={{0,6},{1,7},{2,4},{3,5},{4,2},{5,3},{6,0},{7,1},{8,14},{9,15},{10,... | collective-permute-start | bytes 393224 | tf_op jit(solution)/shard_map/ppermute | solution.py:233
  54.6 9.2 %collective-permute-start.16 = (bf16[16,4096]{1,0:T(8,128)(2,1)S(1)}, bf16[16,4096]{1,0:T(8,128)(2,1)S(1)}, u32[]{:S(2)}, u32[]{:S(2)}) collective-permute-start(bf16[16,4096]{1,0:T(8,128)(2,1)S(1)} %shard_map.107), channel_id=1, source_target_pairs={{0,8},{1,9},{2,10},{3,11},{4,12},{5,13},{6,14},{7,15},{8,0},{9,1},... | collective-permute-start | bytes 393224 | tf_op jit(solution)/shard_map/ppermute | solution.py:236
  56.4 7.4 %copy-start.4 = (bf16[32,128]{1,0:T(8,128)(2,1)S(1)}, bf16[32,128]{1,0:T(8,128)(2,1)}, u32[]{:S(2)}) copy-start(bf16[32,128]{1,0:T(8,128)(2,1)} %get-tuple-element.40.select_ref) | copy-start | bytes 24580

commit v4 on v3

--- a/solution.py
+++ b/solution.py
@@ -39,7 +39,7 @@
         pltpu.make_async_copy(ids_hbm, ids_ref, small.at[0]),
         pltpu.make_async_copy(gate_hbm, gate_ref, small.at[1]),
     ]
-    step = min(STEP, width)
+    step = min(2 * STEP, width)
     copies = []
     for j, at in enumerate(range(0, width, step)):
         cols = pl.ds(at, step)
@@ -142,13 +142,18 @@
 
 
 def unpack_kernel(count, select_ref, *refs):
-    out = refs[-1]
-    width = out.shape[1]
-    step = min(STEP, width)
-    for at in range(0, width, step):
+    rows, (out_hbm, out_ref, done) = refs[:count], refs[count:]
+    width = out_ref.shape[1]
+    step = min(STEP // 2, width)
+    copies = []
+    for j, at in enumerate(range(0, width, step)):
         cols = pl.ds(at, step)
-        rows = jnp.concatenate([refs[k][:, cols] for k in range(count)], axis=0)
-        out[:, cols] = dot(select_ref[...], rows, 0, 0).astype(BF)
+        both = jnp.concatenate([ref[:, cols] for ref in rows], axis=0)
+        out_ref[:, cols] = dot(select_ref[...], both, 0, 0).astype(BF)
+        copies.append(pltpu.make_async_copy(out_ref.at[:, cols], out_hbm.at[:, cols], done.at[j]))
+        copies[-1].start()
+    for copy in copies:
+        copy.wait()
 
 
 def call(kernel, out_shape, *args, mib=24):
@@ -187,7 +192,7 @@
             pltpu.VMEM(tokens.shape, BF),
             pltpu.VMEM(upstream.shape, BF),
             pltpu.SemaphoreType.DMA((2,)),
-            pltpu.SemaphoreType.DMA((2 * (width // min(STEP, width)),)),
+            pltpu.SemaphoreType.DMA((2 * (width // min(2 * STEP, width)),)),
         ],
         compiler_params=params(56),
     )(own, expert_ids, gate_values, tokens, upstream)
@@ -222,6 +227,21 @@
     )(*units, *rows)
 
 
+def unpack(select, pieces):
+    count, width = select.shape[1], pieces[0].shape[1]
+    return pl.pallas_call(
+        functools.partial(unpack_kernel, len(pieces)),
+        out_shape=shape(count, width),
+        in_specs=[VMEM] * (1 + len(pieces)),
+        out_specs=HBM,
+        scratch_shapes=[
+            pltpu.VMEM((count, width), BF),
+            pltpu.SemaphoreType.DMA((width // min(STEP // 2, width),)),
+        ],
+        compiler_params=params(16),
+    )(select, *pieces)
+
+
 def on_device(tokens, upstream, expert_ids, gate_values, w_gate, w_up, w_down):
     devices = lax.axis_size("exp")
     window = devices // TILES
@@ -278,14 +298,12 @@
         whole_piece = total(sent)
         returned.append(turn(whole_piece, window - k))
     corner = swap(along, 2)
-    own = expert([mine, across, along, corner])
+    own = expert([mine, corner, along, across])
     shared, unit, *own_pieces = later(own, whole_piece)
     results.append((shared, unit, swap(shared, 1)))
     grad_gate, grad_up, grad_down = grads(hidden, results)
-    returned = [total(later(send(own_pieces, (2, 4, 6)), grad_gate)), *returned]
-    d_tokens = call(
-        functools.partial(unpack_kernel, window), shape(*tokens.shape), select, *returned
-    )
+    returned = [total(later(send(own_pieces), grad_gate)), *returned]
+    d_tokens = unpack(select, returned)
     return (d_tokens, grad_gate[None], grad_up[None], grad_down[None])
 
 

time: 65.4 us -> 63.5 us (0.971)
  waiting for transfers between devices: 23.3 us -> 22 us
    pallas_call x7 -> x6, Pallas kernels: 10.5 us -> 9.03 us  [call(): pl.pallas_call(kernel, out_shape=out_shape, in_specs=[VMEM] * len(args),...]
    ppermute x15, waiting for transfers between devices: 17.3 us -> 16 us  [swap(): return lax.ppermute(a, 'exp', [(i, i ^ bits) for i in range(devices)])]
    pallas_call x0 -> x1, Pallas kernels: none -> 1.25 us  [unpack(): pl.pallas_call(functools.partial(unpack_kernel, len(pieces)), out_shape=s...]
  transfers between devices with their start and end apart: 17 -> 17, of which waited for: 7 -> 8; matrix products, arithmetic and copies ran while one was open for 0% -> 0% of each run, Pallas kernels for 19% -> 20%
where the time goes in v4:
time: 63.5 us; the launch traced here: 63.4 us
  waiting for transfers between devices  22 us (35%)
  starting transfers between devices  21.2 us (33%)
  Pallas kernels  16.6 us (26%)
  local copies, waits for them, and re-layouts  2.83 us (4%)
  between operations  0.75 us (1%)
    ppermute x15, waiting for transfers between devices, swap(): return lax.ppermute(a, 'exp', [(i, i ^ bits) for i in range(devices)])  16 us
    ppermute x15, starting transfers between devices, swap(): return lax.ppermute(a, 'exp', [(i, i ^ bits) for i in range(devices)])  15.2 us
    pallas_call x6, Pallas kernels, call(): pl.pallas_call(kernel, out_shape=out_shape, in_specs=[VMEM] * len(args),...  9.03 us
    ppermute x2, waiting for transfers between devices, turn(): lax.ppermute(a, 'exp', [(i, (i + k * TILES) % devices) for i in range(dev...  6.02 us
    ppermute x2, starting transfers between devices, turn(): lax.ppermute(a, 'exp', [(i, (i + k * TILES) % devices) for i in range(dev...  5.96 us
    pallas_call x1, Pallas kernels, grads(): pl.pallas_call(functools.partial(grad_kernel, count), grid=(width // step...  3.43 us
    pallas_call x1, Pallas kernels, pack(): pl.pallas_call(functools.partial(pack_kernel, window), out_shape=outs, in...  2.9 us
    unnamed x10, local copies, waits for them, and re-layouts  2.83 us
  transfers between devices with their start and end apart: 17, of which 8 were waited for; matrix products, arithmetic and copies ran while one was open for 0% of the time, Pallas kernels for 20%

profile of v4, /device:TPU:0, one launch (start us, length us, event | category | flops | bytes accessed | tf_op | source)
XLA Modules:
  0.0 63.4 jit_solution(4411400304232712525)
XLA Ops:
  0.7 2.9 %shard_map.102 = (bf16[32,128]{1,0:T(8,128)(2,1)}, bf16[32,4096]{1,0:T(8,128)(2,1)}, bf16[32,4096]{1,0:T(8,128)(2,1)}) custom-call(s32[1]{0:T(128)} %bitcast.own_ref, s32[8,128]{1,0:T(8,128)} %bitcast.12, f32[8,128]{1,0:T(8,128)} %bitcast.13, bf16[128,4096]{1,0:T(8,128)(2,1)} %tokens_hbm.1, bf16[128,4096]{1,0:T(8,128)(2,1)} %upstream_hbm.1), custom_call_target="tpu_custom_call" | custom-call | tf_op jit(solution)/shard_map/pallas_call | solution.py:184
  3.6 4.1 %collective-permute-start = (bf16[32,4096]{1,0:T(8,128)(2,1)}, bf16[32,4096]{1,0:T(8,128)(2,1)S(1)}, u32[]{:S(2)}, u32[]{:S(2)}) collective-permute-start(bf16[32,4096]{1,0:T(8,128)(2,1)} %get-tuple-element.42), channel_id=1, source_target_pairs={{0,8},{1,9},{2,10},{3,11},{4,12},{5,13},{6,14},{7,15},{8,0},{9,1},... | collective-permute-start | bytes 786440 | tf_op jit(solution)/shard_map/ppermute | solution.py:256
  7.7 1.6 %collective-permute-start.1 = (bf16[32,4096]{1,0:T(8,128)(2,1)}, bf16[32,4096]{1,0:T(8,128)(2,1)S(1)}, u32[]{:S(2)}, u32[]{:S(2)}) collective-permute-start(bf16[32,4096]{1,0:T(8,128)(2,1)} %get-tuple-element.41.refs_0_), channel_id=1, source_target_pairs={{0,4},{1,5},{2,6},{3,7},{4,0},{5,1},{6,2},{7,3},{8,12},{9,13},{10,... | collective-permute-start | bytes 786440 | tf_op jit(solution)/shard_map/ppermute | solution.py:253
  9.2 1.5 %collective-permute-start.2 = (bf16[32,4096]{1,0:T(8,128)(2,1)}, bf16[32,4096]{1,0:T(8,128)(2,1)S(1)}, u32[]{:S(2)}, u32[]{:S(2)}) collective-permute-start(bf16[32,4096]{1,0:T(8,128)(2,1)} %get-tuple-element.41.refs_0_), channel_id=1, source_target_pairs={{0,2},{1,3},{2,0},{3,1},{4,6},{5,7},{6,4},{7,5},{8,10},{9,11},{10,... | collective-permute-start | bytes 786440 | tf_op jit(solution)/shard_map/ppermute | solution.py:253
  10.8 1.4 %copy-done.1 = bf16[1,192,4096]{2,1,0:T(8,128)(2,1)S(1)} copy-done((bf16[1,192,4096]{2,1,0:T(8,128)(2,1)S(1)}, bf16[1,192,4096]{2,1,0:T(8,128)(2,1)}, u32[]{:S(2)}) %copy-start.1) | copy-done | bytes 1572888
  12.2 1.4 %copy-done.2 = bf16[1,192,4096]{2,1,0:T(8,128)(2,1)S(1)} copy-done((bf16[1,192,4096]{2,1,0:T(8,128)(2,1)S(1)}, bf16[1,192,4096]{2,1,0:T(8,128)(2,1)}, u32[]{:S(2)}) %copy-start.2) | copy-done | bytes 1572888
  13.6 0.3 shard_map.104.refs_4_
  13.9 6.0 %collective-permute-done.source = bf16[32,4096]{1,0:T(8,128)(2,1)S(1)} collective-permute-done((bf16[32,4096]{1,0:T(8,128)(2,1)}, bf16[32,4096]{1,0:T(8,128)(2,1)S(1)}, u32[]{:S(2)}, u32[]{:S(2)}) %collective-permute-start) | collective-permute-done | bytes 262176 | tf_op jit(solution)/shard_map/ppermute | solution.py:256
  19.9 0.2 collective-permute-done.1.refs_2_
  20.1 2.4 %collective-permute-start.3 = (bf16[32,4096]{1,0:T(8,128)(2,1)S(1)}, bf16[32,4096]{1,0:T(8,128)(2,1)S(1)}, u32[]{:S(2)}, u32[]{:S(2)}) collective-permute-start(bf16[32,4096]{1,0:T(8,128)(2,1)S(1)} %shard_map.103.refs_0_), channel_id=1, source_target_pairs={{0,6},{1,7},{2,4},{3,5},{4,2},{5,3},{6,0},{7,1},{8,14},{9,15},{10,... | collective-permute-start | bytes 786440 | tf_op jit(solution)/shard_map/ppermute | solution.py:253
  22.5 0.6 collective-permute-start.4
  23.2 0.5 collective-permute-start.5
  23.6 6.6 %collective-permute-done.3.refs_1_ = bf16[32,4096]{1,0:T(8,128)(2,1)S(1)} collective-permute-done((bf16[32,4096]{1,0:T(8,128)(2,1)S(1)}, bf16[32,4096]{1,0:T(8,128)(2,1)S(1)}, u32[]{:S(2)}, u32[]{:S(2)}) %collective-permute-start.3) | collective-permute-done | bytes 262176 | tf_op jit(solution)/shard_map/ppermute | solution.py:253
  30.2 5.3 %collective-permute-done.4.refs_2_ = bf16[32,4096]{1,0:T(8,128)(2,1)S(1)} collective-permute-done((bf16[32,4096]{1,0:T(8,128)(2,1)S(1)}, bf16[32,4096]{1,0:T(8,128)(2,1)S(1)}, u32[]{:S(2)}, u32[]{:S(2)}) %collective-permute-start.4) | collective-permute-done | bytes 262176 | tf_op jit(solution)/shard_map/ppermute | solution.py:253
  35.5 1.4 %collective-permute-start.6 = (bf16[32,4096]{1,0:T(8,128)(2,1)S(1)}, bf16[32,4096]{1,0:T(8,128)(2,1)S(1)}, u32[]{:S(2)}, u32[]{:S(2)}) collective-permute-start(bf16[32,4096]{1,0:T(8,128)(2,1)S(1)} %collective-permute-done.1.refs_2_), channel_id=1, source_target_pairs={{0,2},{1,3},{2,0},{3,1},{4,6},{5,7},{6,4},{7,5},{8,10},{9,11},{10,... | collective-permute-start | bytes 786440 | tf_op jit(solution)/shard_map/ppermute | solution.py:253
  36.9 4.3 %shard_map.106 = (bf16[192,4096]{1,0:T(8,128)(2,1)S(1)}, bf16[64,768]{1,0:T(8,128)(2,1)S(1)}, bf16[16,4096]{1,0:T(8,128)(2,1)S(1)}, bf16[16,4096]{1,0:T(8,128)(2...) custom-call(bf16[32,4096]{1,0:T(8,128)(2,1)S(1)} %shard_map.103.refs_0_, ...), custom_call_target="tpu_custom_call" | custom-call | tf_op jit(solution)/shard_map/pallas_call | solution.py:160
  41.2 0.7 %collective-permute-start.10 = (bf16[16,4096]{1,0:T(8,128)(2,1)S(1)}, bf16[16,4096]{1,0:T(8,128)(2,1)S(1)}, u32[]{:S(2)}, u32[]{:S(2)}) collective-permute-start(bf16[16,4096]{1,0:T(8,128)(2,1)S(1)} %get-tuple-element.60), channel_id=1, source_target_pairs={{0,2},{1,3},{2,0},{3,1},{4,6},{5,7},{6,4},{7,5},{8,10},{9,11},{10,... | collective-permute-start | bytes 393224 | tf_op jit(solution)/shard_map/ppermute | solution.py:253
  41.9 2.3 %collective-permute-start.8 = (bf16[16,4096]{1,0:T(8,128)(2,1)S(1)}, bf16[16,4096]{1,0:T(8,128)(2,1)S(1)}, u32[]{:S(2)}, u32[]{:S(2)}) collective-permute-start(bf16[16,4096]{1,0:T(8,128)(2,1)S(1)} %get-tuple-element.58), channel_id=1, source_target_pairs={{0,6},{1,7},{2,4},{3,5},{4,2},{5,3},{6,0},{7,1},{8,14},{9,15},{10,... | collective-permute-start | bytes 393224 | tf_op jit(solution)/shard_map/ppermute | solution.py:253
  44.2 0.6 collective-permute-start.9
  44.8 4.3 %shard_map.105 = (bf16[192,4096]{1,0:T(8,128)(2,1)S(1)}, bf16[64,768]{1,0:T(8,128)(2,1)S(1)}, bf16[16,4096]{1,0:T(8,128)(2,1)S(1)}, bf16[16,4096]{1,0:T(8,128)(2...) custom-call(bf16[32,4096]{1,0:T(8,128)(2,1)S(1)} %copy-done.3, ...), custom_call_target="tpu_custom_call" | custom-call | tf_op jit(solution)/shard_map/pallas_call | solution.py:160
  49.1 0.2 collective-permute-done.10.refs_3_
  49.2 1.2 %collective-permute-done.9.refs_2_ = bf16[16,4096]{1,0:T(8,128)(2,1)S(1)} collective-permute-done((bf16[16,4096]{1,0:T(8,128)(2,1)S(1)}, bf16[16,4096]{1,0:T(8,128)(2,1)S(1)}, u32[]{:S(2)}, u32[]{:S(2)}) %collective-permute-start.9) | collective-permute-done | bytes 131104 | tf_op jit(solution)/shard_map/ppermute | solution.py:253
  50.4 0.1 shard_map.107
  50.5 0.1 collective-permute-start.15
  50.6 1.5 %collective-permute-start.11 = (bf16[16,4096]{1,0:T(8,128)(2,1)S(1)}, bf16[16,4096]{1,0:T(8,128)(2,1)S(1)}, u32[]{:S(2)}, u32[]{:S(2)}) collective-permute-start(bf16[16,4096]{1,0:T(8,128)(2,1)S(1)} %get-tuple-element.62), channel_id=1, source_target_pairs={{0,6},{1,7},{2,4},{3,5},{4,2},{5,3},{6,0},{7,1},{8,14},{9,15},{10,... | collective-permute-start | bytes 393224 | tf_op jit(solution)/shard_map/ppermute | solution.py:253
  52.0 0.5 collective-permute-start.12
  52.6 1.6 %collective-permute-start.13 = (bf16[16,4096]{1,0:T(8,128)(2,1)S(1)}, bf16[16,4096]{1,0:T(8,128)(2,1)S(1)}, u32[]{:S(2)}, u32[]{:S(2)}) collective-permute-start(bf16[16,4096]{1,0:T(8,128)(2,1)S(1)} %get-tuple-element.64), channel_id=1, source_target_pairs={{0,2},{1,3},{2,0},{3,1},{4,6},{5,7},{6,4},{7,5},{8,10},{9,11},{10,... | collective-permute-start | bytes 393224 | tf_op jit(solution)/shard_map/ppermute | solution.py:253
  54.1 1.9 %collective-permute-start.16 = (bf16[16,4096]{1,0:T(8,128)(2,1)S(1)}, bf16[16,4096]{1,0:T(8,128)(2,1)S(1)}, u32[]{:S(2)}, u32[]{:S(2)}) collective-permute-start(bf16[16,4096]{1,0:T(8,128)(2,1)S(1)} %shard_map.107), channel_id=1, source_target_pairs={{0,8},{1,9},{2,10},{3,11},{4,12},{5,13},{6,14},{7,15},{8,0},{9,1},... | collective-permute-start | bytes 393224 | tf_op jit(solution)/shard_map/ppermute | solution.py:256
  56.0 3.4 %shard_map.108 = (bf16[192,4096]{1,0:T(8,128)(2,1)}, bf16[192,4096]{1,0:T(8,128)(2,1)}, bf16[192,4096]{1,0:T(8,128)(2,1)}) custom-call(bf16[64,768]{1,0:T(8,128)(2,1)S(1)} %get-tuple-element.65.refs_0_, bf16[192,4096]{1,0:T(8,128)(2,1)S(1)} %collective-permute-done.14.refs_1_.refs_5_, bf16[64,768]{1,0:T(8,128)(2,1)S(1)} %get-tuple-element.67.refs_2_, ...), custom_call_target="tpu_custom_call" | custom-call | tf_op jit(solution)/shard_map/pallas_call | solution.py:220
  59.4 1.3 %collective-permute-done.11.refs_1_ = bf16[16,4096]{1,0:T(8,128)(2,1)S(1)} collective-permute-done((bf16[16,4096]{1,0:T(8,128)(2,1)S(1)}, bf16[16,4096]{1,0:T(8,128)(2,1)S(1)}, u32[]{:S(2)}, u32[]{:S(2)}) %collective-permute-start.11) | collective-permute-done | bytes 131104 | tf_op jit(solution)/shard_map/ppermute | solution.py:253
  60.7 1.3 %collective-permute-done.12.refs_2_ = bf16[16,4096]{1,0:T(8,128)(2,1)S(1)} collective-permute-done((bf16[16,4096]{1,0:T(8,128)(2,1)S(1)}, bf16[16,4096]{1,0:T(8,128)(2,1)S(1)}, u32[]{:S(2)}, u32[]{:S(2)}) %collective-permute-start.12) | collective-permute-done | bytes 131104 | tf_op jit(solution)/shard_map/ppermute | solution.py:253
  62.1 1.2 %shard_map.110 = bf16[128,4096]{1,0:T(8,128)(2,1)} custom-call(bf16[32,128]{1,0:T(8,128)(2,1)S(1)} %copy-done.4, bf16[16,4096]{1,0:T(8,128)(2,1)S(1)} %shard_map.109.refs_0_, bf16[16,4096]{1,0:T(8,128)(2,1)S(1)} %collective-permute-done.16.refs_1_), custom_call_target="tpu_custom_call" | custom-call | tf_op jit(solution)/shard_map/pallas_call | solution.py:232
  (21 shorter events, 0.1 us)
Async XLA Ops:
  0.6 10.1 %copy-start = (bf16[1,192,4096]{2,1,0:T(8,128)(2,1)S(1)}, bf16[1,192,4096]{2,1,0:T(8,128)(2,1)}, u32[]{:S(2)}) copy-start(bf16[1,192,4096]{2,1,0:T(8,128)(2,1)} %param.11) | copy-start | bytes 4718596
  3.6 16.3 %collective-permute-start = (bf16[32,4096]{1,0:T(8,128)(2,1)}, bf16[32,4096]{1,0:T(8,128)(2,1)S(1)}, u32[]{:S(2)}, u32[]{:S(2)}) collective-permute-start(bf16[32,4096]{1,0:T(8,128)(2,1)} %get-tuple-element.42), channel_id=1, source_target_pairs={{0,8},{1,9},{2,10},{3,11},{4,12},{5,13},{6,14},{7,15},{8,0},{9,1},... | collective-permute-start | bytes 786440 | tf_op jit(solution)/shard_map/ppermute | solution.py:256
  7.7 12.4 %collective-permute-start.1 = (bf16[32,4096]{1,0:T(8,128)(2,1)}, bf16[32,4096]{1,0:T(8,128)(2,1)S(1)}, u32[]{:S(2)}, u32[]{:S(2)}) collective-permute-start(bf16[32,4096]{1,0:T(8,128)(2,1)} %get-tuple-element.41.refs_0_), channel_id=1, source_target_pairs={{0,4},{1,5},{2,6},{3,7},{4,0},{5,1},{6,2},{7,3},{8,12},{9,13},{10,... | collective-permute-start | bytes 786440 | tf_op jit(solution)/shard_map/ppermute | solution.py:253
  9.2 10.9 %collective-permute-start.2 = (bf16[32,4096]{1,0:T(8,128)(2,1)}, bf16[32,4096]{1,0:T(8,128)(2,1)S(1)}, u32[]{:S(2)}, u32[]{:S(2)}) collective-permute-start(bf16[32,4096]{1,0:T(8,128)(2,1)} %get-tuple-element.41.refs_0_), channel_id=1, source_target_pairs={{0,2},{1,3},{2,0},{3,1},{4,6},{5,7},{6,4},{7,5},{8,10},{9,11},{10,... | collective-permute-start | bytes 786440 | tf_op jit(solution)/shard_map/ppermute | solution.py:253
  10.8 1.4 %copy-start.1 = (bf16[1,192,4096]{2,1,0:T(8,128)(2,1)S(1)}, bf16[1,192,4096]{2,1,0:T(8,128)(2,1)}, u32[]{:S(2)}) copy-start(bf16[1,192,4096]{2,1,0:T(8,128)(2,1)} %param.12) | copy-start | bytes 4718596
  12.2 1.4 %copy-start.2 = (bf16[1,192,4096]{2,1,0:T(8,128)(2,1)S(1)}, bf16[1,192,4096]{2,1,0:T(8,128)(2,1)}, u32[]{:S(2)}) copy-start(bf16[1,192,4096]{2,1,0:T(8,128)(2,1)} %param.13) | copy-start | bytes 4718596
  19.9 24.8 %copy-start.3 = (bf16[32,4096]{1,0:T(8,128)(2,1)S(1)}, bf16[32,4096]{1,0:T(8,128)(2,1)}, u32[]{:S(2)}) copy-start(bf16[32,4096]{1,0:T(8,128)(2,1)} %get-tuple-element.41.refs_0_) | copy-start | bytes 786436
  20.1 16.8 %collective-permute-start.7 = (bf16[576,4096]{1,0:T(8,128)(2,1)S(1)}, bf16[576,4096]{1,0:T(8,128)(2,1)S(1)}, u32[]{:S(2)}, u32[]{:S(2)}) collective-permute-start(bf16[576,4096]{1,0:T(8,128)(2,1)S(1)} %shard_map.104.refs_4_), channel_id=1, source_target_pairs={{0,1},{1,0},{2,3},{3,2},{4,5},{5,4},{6,7},{7,6},{8,9},{9,8},{10,11... | collective-permute-start | bytes 14155784 | tf_op jit(solution)/shard_map/ppermute | solution.py:253
  20.1 10.1 %collective-permute-start.3 = (bf16[32,4096]{1,0:T(8,128)(2,1)S(1)}, bf16[32,4096]{1,0:T(8,128)(2,1)S(1)}, u32[]{:S(2)}, u32[]{:S(2)}) collective-permute-start(bf16[32,4096]{1,0:T(8,128)(2,1)S(1)} %shard_map.103.refs_0_), channel_id=1, source_target_pairs={{0,6},{1,7},{2,4},{3,5},{4,2},{5,3},{6,0},{7,1},{8,14},{9,15},{10,... | collective-permute-start | bytes 786440 | tf_op jit(solution)/shard_map/ppermute | solution.py:253
  22.5 12.9 %collective-permute-start.4 = (bf16[32,4096]{1,0:T(8,128)(2,1)S(1)}, bf16[32,4096]{1,0:T(8,128)(2,1)S(1)}, u32[]{:S(2)}, u32[]{:S(2)}) collective-permute-start(bf16[32,4096]{1,0:T(8,128)(2,1)S(1)} %shard_map.103.refs_0_), channel_id=1, source_target_pairs={{0,4},{1,5},{2,6},{3,7},{4,0},{5,1},{6,2},{7,3},{8,12},{9,13},{10,... | collective-permute-start | bytes 786440 | tf_op jit(solution)/shard_map/ppermute | solution.py:253
  23.2 12.3 %collective-permute-start.5 = (bf16[32,4096]{1,0:T(8,128)(2,1)S(1)}, bf16[32,4096]{1,0:T(8,128)(2,1)S(1)}, u32[]{:S(2)}, u32[]{:S(2)}) collective-permute-start(bf16[32,4096]{1,0:T(8,128)(2,1)S(1)} %shard_map.103.refs_0_), channel_id=1, source_target_pairs={{0,2},{1,3},{2,0},{3,1},{4,6},{5,7},{6,4},{7,5},{8,10},{9,11},{10,... | collective-permute-start | bytes 786440 | tf_op jit(solution)/shard_map/ppermute | solution.py:253
  35.5 9.3 %collective-permute-start.6 = (bf16[32,4096]{1,0:T(8,128)(2,1)S(1)}, bf16[32,4096]{1,0:T(8,128)(2,1)S(1)}, u32[]{:S(2)}, u32[]{:S(2)}) collective-permute-start(bf16[32,4096]{1,0:T(8,128)(2,1)S(1)} %collective-permute-done.1.refs_2_), channel_id=1, source_target_pairs={{0,2},{1,3},{2,0},{3,1},{4,6},{5,7},{6,4},{7,5},{8,10},{9,11},{10,... | collective-permute-start | bytes 786440 | tf_op jit(solution)/shard_map/ppermute | solution.py:253
  41.2 8.0 %collective-permute-start.10 = (bf16[16,4096]{1,0:T(8,128)(2,1)S(1)}, bf16[16,4096]{1,0:T(8,128)(2,1)S(1)}, u32[]{:S(2)}, u32[]{:S(2)}) collective-permute-start(bf16[16,4096]{1,0:T(8,128)(2,1)S(1)} %get-tuple-element.60), channel_id=1, source_target_pairs={{0,2},{1,3},{2,0},{3,1},{4,6},{5,7},{6,4},{7,5},{8,10},{9,11},{10,... | collective-permute-start | bytes 393224 | tf_op jit(solution)/shard_map/ppermute | solution.py:253
  41.9 7.3 %collective-permute-start.8 = (bf16[16,4096]{1,0:T(8,128)(2,1)S(1)}, bf16[16,4096]{1,0:T(8,128)(2,1)S(1)}, u32[]{:S(2)}, u32[]{:S(2)}) collective-permute-start(bf16[16,4096]{1,0:T(8,128)(2,1)S(1)} %get-tuple-element.58), channel_id=1, source_target_pairs={{0,6},{1,7},{2,4},{3,5},{4,2},{5,3},{6,0},{7,1},{8,14},{9,15},{10,... | collective-permute-start | bytes 393224 | tf_op jit(solution)/shard_map/ppermute | solution.py:253
  44.2 6.3 %collective-permute-start.9 = (bf16[16,4096]{1,0:T(8,128)(2,1)S(1)}, bf16[16,4096]{1,0:T(8,128)(2,1)S(1)}, u32[]{:S(2)}, u32[]{:S(2)}) collective-permute-start(bf16[16,4096]{1,0:T(8,128)(2,1)S(1)} %get-tuple-element.59), channel_id=1, source_target_pairs={{0,4},{1,5},{2,6},{3,7},{4,0},{5,1},{6,2},{7,3},{8,12},{9,13},{10,... | collective-permute-start | bytes 393224 | tf_op jit(solution)/shard_map/ppermute | solution.py:253
  44.8 9.4 %collective-permute-start.14 = (bf16[192,4096]{1,0:T(8,128)(2,1)S(1)}, bf16[192,4096]{1,0:T(8,128)(2,1)S(1)}, u32[]{:S(2)}, u32[]{:S(2)}) collective-permute-start(bf16[192,4096]{1,0:T(8,128)(2,1)S(1)} %get-tuple-element.66.refs_4_), channel_id=1, source_target_pairs={{0,1},{1,0},{2,3},{3,2},{4,5},{5,4},{6,7},{7,6},{8,9},{9,8},{10,11... | collective-permute-start | bytes 4718600 | tf_op jit(solution)/shard_map/ppermute | solution.py:253
  50.5 5.5 %collective-permute-start.15 = (bf16[192,4096]{1,0:T(8,128)(2,1)S(1)}, bf16[192,4096]{1,0:T(8,128)(2,1)S(1)}, u32[]{:S(2)}, u32[]{:S(2)}) collective-permute-start(bf16[192,4096]{1,0:T(8,128)(2,1)S(1)} %get-tuple-element.68.refs_6_), channel_id=1, source_target_pairs={{0,1},{1,0},{2,3},{3,2},{4,5},{5,4},{6,7},{7,6},{8,9},{9,8},{10,11... | collective-permute-start | bytes 4718600 | tf_op jit(solution)/shard_map/ppermute | solution.py:253
  50.6 10.1 %collective-permute-start.11 = (bf16[16,4096]{1,0:T(8,128)(2,1)S(1)}, bf16[16,4096]{1,0:T(8,128)(2,1)S(1)}, u32[]{:S(2)}, u32[]{:S(2)}) collective-permute-start(bf16[16,4096]{1,0:T(8,128)(2,1)S(1)} %get-tuple-element.62), channel_id=1, source_target_pairs={{0,6},{1,7},{2,4},{3,5},{4,2},{5,3},{6,0},{7,1},{8,14},{9,15},{10,... | collective-permute-start | bytes 393224 | tf_op jit(solution)/shard_map/ppermute | solution.py:253
  52.0 10.0 %collective-permute-start.12 = (bf16[16,4096]{1,0:T(8,128)(2,1)S(1)}, bf16[16,4096]{1,0:T(8,128)(2,1)S(1)}, u32[]{:S(2)}, u32[]{:S(2)}) collective-permute-start(bf16[16,4096]{1,0:T(8,128)(2,1)S(1)} %get-tuple-element.63), channel_id=1, source_target_pairs={{0,4},{1,5},{2,6},{3,7},{4,0},{5,1},{6,2},{7,3},{8,12},{9,13},{10,... | collective-permute-start | bytes 393224 | tf_op jit(solution)/shard_map/ppermute | solution.py:253
  52.6 9.4 %collective-permute-start.13 = (bf16[16,4096]{1,0:T(8,128)(2,1)S(1)}, bf16[16,4096]{1,0:T(8,128)(2,1)S(1)}, u32[]{:S(2)}, u32[]{:S(2)}) collective-permute-start(bf16[16,4096]{1,0:T(8,128)(2,1)S(1)} %get-tuple-element.64), channel_id=1, source_target_pairs={{0,2},{1,3},{2,0},{3,1},{4,6},{5,7},{6,4},{7,5},{8,10},{9,11},{10,... | collective-permute-start | bytes 393224 | tf_op jit(solution)/shard_map/ppermute | solution.py:253
  54.1 7.9 %collective-permute-start.16 = (bf16[16,4096]{1,0:T(8,128)(2,1)S(1)}, bf16[16,4096]{1,0:T(8,128)(2,1)S(1)}, u32[]{:S(2)}, u32[]{:S(2)}) collective-permute-start(bf16[16,4096]{1,0:T(8,128)(2,1)S(1)} %shard_map.107), channel_id=1, source_target_pairs={{0,8},{1,9},{2,10},{3,11},{4,12},{5,13},{6,14},{7,15},{8,0},{9,1},... | collective-permute-start | bytes 393224 | tf_op jit(solution)/shard_map/ppermute | solution.py:256
  56.0 6.1 %copy-start.4 = (bf16[32,128]{1,0:T(8,128)(2,1)S(1)}, bf16[32,128]{1,0:T(8,128)(2,1)}, u32[]{:S(2)}) copy-start(bf16[32,128]{1,0:T(8,128)(2,1)} %get-tuple-element.40.select_ref) | copy-start | bytes 24580

commit v5 on v4

--- a/solution.py
+++ b/solution.py
@@ -90,27 +90,28 @@
 
 
 def expert_kernel(count, hidden, *refs):
-    blocks, weights = refs[:count], refs[count : count + 2]
-    shared_ref, unit_ref, *parts = refs[count + 2 :]
-    rows = count * CAP
+    blocks, (turned_ref, mine_ref, other_ref, shared_ref, unit_ref, *parts) = refs[:count], refs[count:]
+    rows, both = count * CAP, 2 * hidden
     for j, block in enumerate(blocks):
         shared_ref[j * CAP : (j + 1) * CAP, :] = block[:CAP, :]
         shared_ref[rows + j * CAP : rows + (j + 1) * CAP, :] = block[CAP:, :]
-    x, z = shared_ref[:rows, :], shared_ref[rows : 2 * rows, :]
+    pre = dot(shared_ref[:rows, :], turned_ref[:, : 2 * both], 1, 0)
+    d_hidden = dot(shared_ref[rows : 2 * rows, :], turned_ref[:, 2 * both :], 1, 0)
+    pre_gate, pre_up = pre[:, :both], pre[:, both:]
+    sigma = 1.0 / (1.0 + jnp.exp(-pre_gate))
+    active = pre_gate * sigma
+    d_gate = (d_hidden * pre_up * sigma * (1.0 + pre_gate * (1.0 - sigma))).astype(BF)
+    d_up = (d_hidden * active).astype(BF)
+    units = (d_gate, d_up, (active * pre_up).astype(BF))
     terms = []
-    for ref, unit_rows, out in ((weights[0], 0, unit_ref), (weights[1], 2 * rows, shared_ref)):
-        pre_gate = dot(x, ref[:hidden, :], 1, 1)
-        pre_up = dot(x, ref[hidden : 2 * hidden, :], 1, 1)
-        d_hidden = dot(z, ref[2 * hidden :, :], 1, 1)
-        sigma = 1.0 / (1.0 + jnp.exp(-pre_gate))
-        active = pre_gate * sigma
-        d_gate = (d_hidden * pre_up * sigma * (1.0 + pre_gate * (1.0 - sigma))).astype(BF)
-        d_up = (d_hidden * active).astype(BF)
-        for m, unit in enumerate((d_gate, d_up, (active * pre_up).astype(BF))):
-            at = m * padded(hidden)
-            out[unit_rows : unit_rows + rows, at : at + hidden] = unit
-        terms += [(d_gate, ref, 0), (d_up, ref, hidden)]
-    width = x.shape[1]
+    for m, unit in enumerate(units):
+        at = m * padded(hidden)
+        own, sibling = unit[:, :hidden], unit[:, hidden:]
+        unit_ref[:, at : at + hidden] = own
+        shared_ref[2 * rows :, at : at + hidden] = sibling
+        if m < 2:
+            terms += [(own, mine_ref, m * hidden), (sibling, other_ref, m * hidden)]
+    width = shared_ref.shape[1]
     step = min(STEP, width)
     for at in range(0, width, step):
         cols = pl.ds(at, step)
@@ -202,6 +203,17 @@
     out[...] = source[...]
 
 
+def turn_kernel(mine_ref, other_ref, out_ref):
+    hidden, width = mine_ref.shape[0] // 3, mine_ref.shape[1]
+    step = min(STEP // 2, width)
+    for m in range(3):
+        part = slice(m * hidden, (m + 1) * hidden)
+        for at in range(0, width, step):
+            cols = pl.ds(at, step)
+            rows = jnp.concatenate([mine_ref[part, cols], other_ref[part, cols]], axis=0)
+            out_ref[at : at + step, 2 * m * hidden : 2 * (m + 1) * hidden] = rows.T
+
+
 def fetch_kernel(gate_ref, up_ref, down_ref, out_ref):
     rows = gate_ref.shape[0]
     for m, ref in enumerate((gate_ref, up_ref, down_ref)):
@@ -256,7 +268,7 @@
         return lax.ppermute(a, "exp", [(i, (i + k * TILES) % devices) for i in range(devices)])
 
     def near(block):
-        return [block] + [swap(block, bits) for bits in (6, 4, 2)]
+        return [block] + [swap(block, bits) for bits in (4, 2, 6)]
 
     def later(values, *first):
         count = len(values)
@@ -267,7 +279,7 @@
         return call(
             functools.partial(expert_kernel, len(blocks), hidden),
             [shape(3 * rows, width), shape(rows, 3 * padded(hidden))] + [shape(CAP, width)] * len(blocks),
-            *blocks, weights, sibling,
+            *blocks, turned, weights, sibling,
         )
 
     select, *packed = pack(window, own, expert_ids.T, gate_values.T, tokens, upstream)
@@ -280,29 +292,31 @@
     crossed = [call(copy_kernel, shape(*c.shape), c, mib=4) for c in crossed]
     *crossed, along, across, weights = later([*crossed, along, across, weights])
     sibling = swap(weights, 1)
-
-    def send(pieces, order=(6, 4, 2)):
+    turned = call(turn_kernel, shape(width, 6 * hidden), weights, sibling)
+
+    def send(pieces, order=(4, 2, 6)):
         return [pieces[0]] + [swap(piece, bits) for piece, bits in zip(pieces[1:], order)]
 
     def total(pieces):
         return call(functools.partial(sum_kernel, 4), [shape(CAP, width)], *pieces)[0]
 
-    results, returned = [], []
+    results, sent, returned = [], [], []
     for k in range(1, window):
         blocks = near(crossed[k - 1])
         if k == window - 1:
-            (along,) = later([along], *blocks)
+            (along,) = later([along], *blocks, turned)
         shared, unit, *pieces = expert(blocks)
         results.append((shared, unit, swap(shared, 1)))
-        sent = send(pieces)
-        whole_piece = total(sent)
+        sent.append(send(pieces))
+    corner = swap(along, 2)
+    own = expert([mine, along, corner, across])
+    for k in range(1, window):
+        whole_piece = total(later(sent[k - 1], own[1]))
         returned.append(turn(whole_piece, window - k))
-    corner = swap(along, 2)
-    own = expert([mine, corner, along, across])
     shared, unit, *own_pieces = later(own, whole_piece)
     results.append((shared, unit, swap(shared, 1)))
     grad_gate, grad_up, grad_down = grads(hidden, results)
-    returned = [total(later(send(own_pieces), grad_gate)), *returned]
+    returned = [total(later(send(own_pieces, (4, 6, 2)), grad_gate)), *returned]
     d_tokens = unpack(select, returned)
     return (d_tokens, grad_gate[None], grad_up[None], grad_down[None])
 

time: 63.5 us -> 63 us (level)
  waiting for transfers between devices: 22 us -> 21 us
    ppermute x15, waiting for transfers between devices: 16 us -> 14.9 us  [swap(): return lax.ppermute(a, 'exp', [(i, i ^ bits) for i in range(devices)])]
    pallas_call x6 -> x7, Pallas kernels: 9.03 us -> 9.04 us  [call(): pl.pallas_call(kernel, out_shape=out_shape, in_specs=[VMEM] * len(args),...]
  transfers between devices with their start and end apart: 17 -> 17, of which waited for: 8 -> 7; matrix products, arithmetic and copies ran while one was open for 0% -> 0% of each run, Pallas kernels for 20% -> 20%
where the time goes in v5:
time: 63 us; the launch traced here: 62.9 us
  starting transfers between devices  21.7 us (34%)
  waiting for transfers between devices  21 us (33%)
  Pallas kernels  16.6 us (26%)
  local copies, waits for them, and re-layouts  2.83 us (4%)
  between operations  0.77 us (1%)
    ppermute x15, starting transfers between devices, swap(): return lax.ppermute(a, 'exp', [(i, i ^ bits) for i in range(devices)])  15.3 us
    ppermute x15, waiting for transfers between devices, swap(): return lax.ppermute(a, 'exp', [(i, i ^ bits) for i in range(devices)])  14.9 us
    pallas_call x7, Pallas kernels, call(): pl.pallas_call(kernel, out_shape=out_shape, in_specs=[VMEM] * len(args),...  9.04 us
    ppermute x2, starting transfers between devices, turn(): lax.ppermute(a, 'exp', [(i, (i + k * TILES) % devices) for i in range(dev...  6.36 us
    ppermute x2, waiting for transfers between devices, turn(): lax.ppermute(a, 'exp', [(i, (i + k * TILES) % devices) for i in range(dev...  6.02 us
    pallas_call x1, Pallas kernels, grads(): pl.pallas_call(functools.partial(grad_kernel, count), grid=(width // step...  3.44 us
    pallas_call x1, Pallas kernels, pack(): pl.pallas_call(functools.partial(pack_kernel, window), out_shape=outs, in...  2.9 us
    unnamed x10, local copies, waits for them, and re-layouts  2.83 us
  transfers between devices with their start and end apart: 17, of which 7 were waited for; matrix products, arithmetic and copies ran while one was open for 0% of the time, Pallas kernels for 20%

profile of v5, /device:TPU:0, one launch (start us, length us, event | category | flops | bytes accessed | tf_op | source)
XLA Modules:
  0.0 62.9 jit_solution(5162253459915130943)
XLA Ops:
  0.7 2.9 %shard_map.102 = (bf16[32,128]{1,0:T(8,128)(2,1)}, bf16[32,4096]{1,0:T(8,128)(2,1)}, bf16[32,4096]{1,0:T(8,128)(2,1)}) custom-call(s32[1]{0:T(128)} %bitcast.own_ref, s32[8,128]{1,0:T(8,128)} %bitcast.12, f32[8,128]{1,0:T(8,128)} %bitcast.13, bf16[128,4096]{1,0:T(8,128)(2,1)} %tokens_hbm.1, bf16[128,4096]{1,0:T(8,128)(2,1)} %upstream_hbm.1), custom_call_target="tpu_custom_call" | custom-call | tf_op jit(solution)/shard_map/pallas_call | solution.py:185
  3.6 4.1 %collective-permute-start = (bf16[32,4096]{1,0:T(8,128)(2,1)}, bf16[32,4096]{1,0:T(8,128)(2,1)S(1)}, u32[]{:S(2)}, u32[]{:S(2)}) collective-permute-start(bf16[32,4096]{1,0:T(8,128)(2,1)} %get-tuple-element.46), channel_id=1, source_target_pairs={{0,8},{1,9},{2,10},{3,11},{4,12},{5,13},{6,14},{7,15},{8,0},{9,1},... | collective-permute-start | bytes 786440 | tf_op jit(solution)/shard_map/ppermute | solution.py:268
  7.7 1.6 %collective-permute-start.1 = (bf16[32,4096]{1,0:T(8,128)(2,1)}, bf16[32,4096]{1,0:T(8,128)(2,1)S(1)}, u32[]{:S(2)}, u32[]{:S(2)}) collective-permute-start(bf16[32,4096]{1,0:T(8,128)(2,1)} %get-tuple-element.45.refs_0_), channel_id=1, source_target_pairs={{0,4},{1,5},{2,6},{3,7},{4,0},{5,1},{6,2},{7,3},{8,12},{9,13},{10,... | collective-permute-start | bytes 786440 | tf_op jit(solution)/shard_map/ppermute | solution.py:265
  9.2 1.5 %collective-permute-start.2 = (bf16[32,4096]{1,0:T(8,128)(2,1)}, bf16[32,4096]{1,0:T(8,128)(2,1)S(1)}, u32[]{:S(2)}, u32[]{:S(2)}) collective-permute-start(bf16[32,4096]{1,0:T(8,128)(2,1)} %get-tuple-element.45.refs_0_), channel_id=1, source_target_pairs={{0,2},{1,3},{2,0},{3,1},{4,6},{5,7},{6,4},{7,5},{8,10},{9,11},{10,... | collective-permute-start | bytes 786440 | tf_op jit(solution)/shard_map/ppermute | solution.py:265
  10.8 1.4 %copy-done.1 = bf16[1,192,4096]{2,1,0:T(8,128)(2,1)S(1)} copy-done((bf16[1,192,4096]{2,1,0:T(8,128)(2,1)S(1)}, bf16[1,192,4096]{2,1,0:T(8,128)(2,1)}, u32[]{:S(2)}) %copy-start.1) | copy-done | bytes 1572888
  12.2 1.4 %copy-done.2 = bf16[1,192,4096]{2,1,0:T(8,128)(2,1)S(1)} copy-done((bf16[1,192,4096]{2,1,0:T(8,128)(2,1)S(1)}, bf16[1,192,4096]{2,1,0:T(8,128)(2,1)}, u32[]{:S(2)}) %copy-start.2) | copy-done | bytes 1572888
  13.6 0.3 shard_map.104.mine_ref.refs_5_
  13.9 6.0 %collective-permute-done.source = bf16[32,4096]{1,0:T(8,128)(2,1)S(1)} collective-permute-done((bf16[32,4096]{1,0:T(8,128)(2,1)}, bf16[32,4096]{1,0:T(8,128)(2,1)S(1)}, u32[]{:S(2)}, u32[]{:S(2)}) %collective-permute-start) | collective-permute-done | bytes 262176 | tf_op jit(solution)/shard_map/ppermute | solution.py:268
  19.9 0.2 collective-permute-done.1.refs_1_
  20.1 1.5 %collective-permute-start.3 = (bf16[32,4096]{1,0:T(8,128)(2,1)S(1)}, bf16[32,4096]{1,0:T(8,128)(2,1)S(1)}, u32[]{:S(2)}, u32[]{:S(2)}) collective-permute-start(bf16[32,4096]{1,0:T(8,128)(2,1)S(1)} %shard_map.103.refs_0_), channel_id=1, source_target_pairs={{0,4},{1,5},{2,6},{3,7},{4,0},{5,1},{6,2},{7,3},{8,12},{9,13},{10,... | collective-permute-start | bytes 786440 | tf_op jit(solution)/shard_map/ppermute | solution.py:265
  21.6 1.5 %collective-permute-start.4 = (bf16[32,4096]{1,0:T(8,128)(2,1)S(1)}, bf16[32,4096]{1,0:T(8,128)(2,1)S(1)}, u32[]{:S(2)}, u32[]{:S(2)}) collective-permute-start(bf16[32,4096]{1,0:T(8,128)(2,1)S(1)} %shard_map.103.refs_0_), channel_id=1, source_target_pairs={{0,2},{1,3},{2,0},{3,1},{4,6},{5,7},{6,4},{7,5},{8,10},{9,11},{10,... | collective-permute-start | bytes 786440 | tf_op jit(solution)/shard_map/ppermute | solution.py:265
  23.1 0.5 collective-permute-start.5
  23.6 4.4 %collective-permute-done.6.other_ref.refs_6_ = bf16[576,4096]{1,0:T(8,128)(2,1)S(1)} collective-permute-done((bf16[576,4096]{1,0:T(8,128)(2,1)S(1)}, bf16[576,4096]{1,0:T(8,128)(2,1)S(1)}, u32[]{:S(2)}, u32[]{:S(2)}) %collective-permute-start.6) | collective-permute-done | bytes 4718624 | tf_op jit(solution)/shard_map/ppermute | solution.py:265
  28.0 2.5 %shard_map.105.refs_4_ = bf16[4096,1152]{1,0:T(8,128)(2,1)S(1)} custom-call(bf16[576,4096]{1,0:T(8,128)(2,1)S(1)} %shard_map.104.mine_ref.refs_5_, bf16[576,4096]{1,0:T(8,128)(2,1)S(1)} %collective-permute-done.6.other_ref.refs_6_), custom_call_target="tpu_custom_call" | custom-call | tf_op jit(solution)/shard_map/pallas_call | solution.py:161
  30.5 5.1 %collective-permute-done.4.refs_2_ = bf16[32,4096]{1,0:T(8,128)(2,1)S(1)} collective-permute-done((bf16[32,4096]{1,0:T(8,128)(2,1)S(1)}, bf16[32,4096]{1,0:T(8,128)(2,1)S(1)}, u32[]{:S(2)}, u32[]{:S(2)}) %collective-permute-start.4) | collective-permute-done | bytes 262176 | tf_op jit(solution)/shard_map/ppermute | solution.py:265
  35.7 1.5 %collective-permute-start.7 = (bf16[32,4096]{1,0:T(8,128)(2,1)S(1)}, bf16[32,4096]{1,0:T(8,128)(2,1)S(1)}, u32[]{:S(2)}, u32[]{:S(2)}) collective-permute-start(bf16[32,4096]{1,0:T(8,128)(2,1)S(1)} %collective-permute-done.1.refs_1_), channel_id=1, source_target_pairs={{0,2},{1,3},{2,0},{3,1},{4,6},{5,7},{6,4},{7,5},{8,10},{9,11},{10,... | collective-permute-start | bytes 786440 | tf_op jit(solution)/shard_map/ppermute | solution.py:265
  37.2 3.1 %shard_map.107 = (bf16[192,4096]{1,0:T(8,128)(2,1)S(1)}, bf16[64,768]{1,0:T(8,128)(2,1)S(1)}, bf16[16,4096]{1,0:T(8,128)(2,1)S(1)}, bf16[16,4096]{1,0:T(8,128)(2...) custom-call(bf16[32,4096]{1,0:T(8,128)(2,1)S(1)} %shard_map.103.refs_0_, ...), custom_call_target="tpu_custom_call" | custom-call | tf_op jit(solution)/shard_map/pallas_call | solution.py:161
  40.2 0.7 %collective-permute-start.8 = (bf16[16,4096]{1,0:T(8,128)(2,1)S(1)}, bf16[16,4096]{1,0:T(8,128)(2,1)S(1)}, u32[]{:S(2)}, u32[]{:S(2)}) collective-permute-start(bf16[16,4096]{1,0:T(8,128)(2,1)S(1)} %get-tuple-element.62), channel_id=1, source_target_pairs={{0,4},{1,5},{2,6},{3,7},{4,0},{5,1},{6,2},{7,3},{8,12},{9,13},{10,... | collective-permute-start | bytes 393224 | tf_op jit(solution)/shard_map/ppermute | solution.py:265
  40.9 1.1 %collective-permute-start.9 = (bf16[16,4096]{1,0:T(8,128)(2,1)S(1)}, bf16[16,4096]{1,0:T(8,128)(2,1)S(1)}, u32[]{:S(2)}, u32[]{:S(2)}) collective-permute-start(bf16[16,4096]{1,0:T(8,128)(2,1)S(1)} %get-tuple-element.63), channel_id=1, source_target_pairs={{0,2},{1,3},{2,0},{3,1},{4,6},{5,7},{6,4},{7,5},{8,10},{9,11},{10,... | collective-permute-start | bytes 393224 | tf_op jit(solution)/shard_map/ppermute | solution.py:265
  42.0 1.7 %collective-permute-start.10 = (bf16[16,4096]{1,0:T(8,128)(2,1)S(1)}, bf16[16,4096]{1,0:T(8,128)(2,1)S(1)}, u32[]{:S(2)}, u32[]{:S(2)}) collective-permute-start(bf16[16,4096]{1,0:T(8,128)(2,1)S(1)} %get-tuple-element.64), channel_id=1, source_target_pairs={{0,6},{1,7},{2,4},{3,5},{4,2},{5,3},{6,0},{7,1},{8,14},{9,15},{10,... | collective-permute-start | bytes 393224 | tf_op jit(solution)/shard_map/ppermute | solution.py:265
  43.8 0.6 %collective-permute-done.7.refs_2_ = bf16[32,4096]{1,0:T(8,128)(2,1)S(1)} collective-permute-done((bf16[32,4096]{1,0:T(8,128)(2,1)S(1)}, bf16[32,4096]{1,0:T(8,128)(2,1)S(1)}, u32[]{:S(2)}, u32[]{:S(2)}) %collective-permute-start.7) | collective-permute-done | bytes 262176 | tf_op jit(solution)/shard_map/ppermute | solution.py:265
  44.4 3.1 %shard_map.106 = (bf16[192,4096]{1,0:T(8,128)(2,1)S(1)}, bf16[64,768]{1,0:T(8,128)(2,1)S(1)}, bf16[16,4096]{1,0:T(8,128)(2,1)S(1)}, bf16[16,4096]{1,0:T(8,128)(2...) custom-call(bf16[32,4096]{1,0:T(8,128)(2,1)S(1)} %copy-done.3, ...), custom_call_target="tpu_custom_call" | custom-call | tf_op jit(solution)/shard_map/pallas_call | solution.py:161
  47.5 1.5 %collective-permute-done.9.refs_2_ = bf16[16,4096]{1,0:T(8,128)(2,1)S(1)} collective-permute-done((bf16[16,4096]{1,0:T(8,128)(2,1)S(1)}, bf16[16,4096]{1,0:T(8,128)(2,1)S(1)}, u32[]{:S(2)}, u32[]{:S(2)}) %collective-permute-start.9) | collective-permute-done | bytes 131104 | tf_op jit(solution)/shard_map/ppermute | solution.py:265
  49.0 0.1 shard_map.108
  49.1 0.1 collective-permute-start.15
  49.2 1.5 %collective-permute-start.11 = (bf16[16,4096]{1,0:T(8,128)(2,1)S(1)}, bf16[16,4096]{1,0:T(8,128)(2,1)S(1)}, u32[]{:S(2)}, u32[]{:S(2)}) collective-permute-start(bf16[16,4096]{1,0:T(8,128)(2,1)S(1)} %get-tuple-element.70), channel_id=1, source_target_pairs={{0,4},{1,5},{2,6},{3,7},{4,0},{5,1},{6,2},{7,3},{8,12},{9,13},{10,... | collective-permute-start | bytes 393224 | tf_op jit(solution)/shard_map/ppermute | solution.py:265
  50.7 1.4 %collective-permute-start.12 = (bf16[16,4096]{1,0:T(8,128)(2,1)S(1)}, bf16[16,4096]{1,0:T(8,128)(2,1)S(1)}, u32[]{:S(2)}, u32[]{:S(2)}) collective-permute-start(bf16[16,4096]{1,0:T(8,128)(2,1)S(1)} %get-tuple-element.71), channel_id=1, source_target_pairs={{0,6},{1,7},{2,4},{3,5},{4,2},{5,3},{6,0},{7,1},{8,14},{9,15},{10,... | collective-permute-start | bytes 393224 | tf_op jit(solution)/shard_map/ppermute | solution.py:265
  52.1 0.6 %collective-permute-start.13 = (bf16[16,4096]{1,0:T(8,128)(2,1)S(1)}, bf16[16,4096]{1,0:T(8,128)(2,1)S(1)}, u32[]{:S(2)}, u32[]{:S(2)}) collective-permute-start(bf16[16,4096]{1,0:T(8,128)(2,1)S(1)} %get-tuple-element.72), channel_id=1, source_target_pairs={{0,2},{1,3},{2,0},{3,1},{4,6},{5,7},{6,4},{7,5},{8,10},{9,11},{10,... | collective-permute-start | bytes 393224 | tf_op jit(solution)/shard_map/ppermute | solution.py:265
  52.7 2.3 %collective-permute-start.16 = (bf16[16,4096]{1,0:T(8,128)(2,1)S(1)}, bf16[16,4096]{1,0:T(8,128)(2,1)S(1)}, u32[]{:S(2)}, u32[]{:S(2)}) collective-permute-start(bf16[16,4096]{1,0:T(8,128)(2,1)S(1)} %shard_map.108), channel_id=1, source_target_pairs={{0,8},{1,9},{2,10},{3,11},{4,12},{5,13},{6,14},{7,15},{8,0},{9,1},... | collective-permute-start | bytes 393224 | tf_op jit(solution)/shard_map/ppermute | solution.py:268
  55.0 3.4 %shard_map.109 = (bf16[192,4096]{1,0:T(8,128)(2,1)}, bf16[192,4096]{1,0:T(8,128)(2,1)}, bf16[192,4096]{1,0:T(8,128)(2,1)}) custom-call(bf16[64,768]{1,0:T(8,128)(2,1)S(1)} %get-tuple-element.73.refs_0_, bf16[192,4096]{1,0:T(8,128)(2,1)S(1)} %collective-permute-done.14.refs_1_.refs_5_, bf16[64,768]{1,0:T(8,128)(2,1)S(1)} %get-tuple-element.75.refs_2_, ...), custom_call_target="tpu_custom_call" | custom-call | tf_op jit(solution)/shard_map/pallas_call | solution.py:232
  58.5 3.1 %collective-permute-done.12.refs_2_ = bf16[16,4096]{1,0:T(8,128)(2,1)S(1)} collective-permute-done((bf16[16,4096]{1,0:T(8,128)(2,1)S(1)}, bf16[16,4096]{1,0:T(8,128)(2,1)S(1)}, u32[]{:S(2)}, u32[]{:S(2)}) %collective-permute-start.12) | collective-permute-done | bytes 131104 | tf_op jit(solution)/shard_map/ppermute | solution.py:265
  61.6 1.2 %shard_map.111 = bf16[128,4096]{1,0:T(8,128)(2,1)} custom-call(bf16[32,128]{1,0:T(8,128)(2,1)S(1)} %copy-done.4, bf16[16,4096]{1,0:T(8,128)(2,1)S(1)} %shard_map.110.refs_0_, bf16[16,4096]{1,0:T(8,128)(2,1)S(1)} %collective-permute-done.16.refs_1_), custom_call_target="tpu_custom_call" | custom-call | tf_op jit(solution)/shard_map/pallas_call | solution.py:244
  (22 shorter events, 0.1 us)
Async XLA Ops:
  0.6 10.1 %copy-start = (bf16[1,192,4096]{2,1,0:T(8,128)(2,1)S(1)}, bf16[1,192,4096]{2,1,0:T(8,128)(2,1)}, u32[]{:S(2)}) copy-start(bf16[1,192,4096]{2,1,0:T(8,128)(2,1)} %param.11) | copy-start | bytes 4718596
  3.6 16.3 %collective-permute-start = (bf16[32,4096]{1,0:T(8,128)(2,1)}, bf16[32,4096]{1,0:T(8,128)(2,1)S(1)}, u32[]{:S(2)}, u32[]{:S(2)}) collective-permute-start(bf16[32,4096]{1,0:T(8,128)(2,1)} %get-tuple-element.46), channel_id=1, source_target_pairs={{0,8},{1,9},{2,10},{3,11},{4,12},{5,13},{6,14},{7,15},{8,0},{9,1},... | collective-permute-start | bytes 786440 | tf_op jit(solution)/shard_map/ppermute | solution.py:268
  7.7 12.4 %collective-permute-start.1 = (bf16[32,4096]{1,0:T(8,128)(2,1)}, bf16[32,4096]{1,0:T(8,128)(2,1)S(1)}, u32[]{:S(2)}, u32[]{:S(2)}) collective-permute-start(bf16[32,4096]{1,0:T(8,128)(2,1)} %get-tuple-element.45.refs_0_), channel_id=1, source_target_pairs={{0,4},{1,5},{2,6},{3,7},{4,0},{5,1},{6,2},{7,3},{8,12},{9,13},{10,... | collective-permute-start | bytes 786440 | tf_op jit(solution)/shard_map/ppermute | solution.py:265
  9.2 10.9 %collective-permute-start.2 = (bf16[32,4096]{1,0:T(8,128)(2,1)}, bf16[32,4096]{1,0:T(8,128)(2,1)S(1)}, u32[]{:S(2)}, u32[]{:S(2)}) collective-permute-start(bf16[32,4096]{1,0:T(8,128)(2,1)} %get-tuple-element.45.refs_0_), channel_id=1, source_target_pairs={{0,2},{1,3},{2,0},{3,1},{4,6},{5,7},{6,4},{7,5},{8,10},{9,11},{10,... | collective-permute-start | bytes 786440 | tf_op jit(solution)/shard_map/ppermute | solution.py:265
  10.8 1.4 %copy-start.1 = (bf16[1,192,4096]{2,1,0:T(8,128)(2,1)S(1)}, bf16[1,192,4096]{2,1,0:T(8,128)(2,1)}, u32[]{:S(2)}) copy-start(bf16[1,192,4096]{2,1,0:T(8,128)(2,1)} %param.12) | copy-start | bytes 4718596
  12.2 1.4 %copy-start.2 = (bf16[1,192,4096]{2,1,0:T(8,128)(2,1)S(1)}, bf16[1,192,4096]{2,1,0:T(8,128)(2,1)}, u32[]{:S(2)}) copy-start(bf16[1,192,4096]{2,1,0:T(8,128)(2,1)} %param.13) | copy-start | bytes 4718596
  20.1 7.9 %collective-permute-start.6 = (bf16[576,4096]{1,0:T(8,128)(2,1)S(1)}, bf16[576,4096]{1,0:T(8,128)(2,1)S(1)}, u32[]{:S(2)}, u32[]{:S(2)}) collective-permute-start(bf16[576,4096]{1,0:T(8,128)(2,1)S(1)} %shard_map.104.mine_ref.refs_5_), channel_id=1, source_target_pairs={{0,1},{1,0},{2,3},{3,2},{4,5},{5,4},{6,7},{7,6},{8,9},{9,8},{10,11... | collective-permute-start | bytes 14155784 | tf_op jit(solution)/shard_map/ppermute | solution.py:265
  20.1 10.4 %collective-permute-start.3 = (bf16[32,4096]{1,0:T(8,128)(2,1)S(1)}, bf16[32,4096]{1,0:T(8,128)(2,1)S(1)}, u32[]{:S(2)}, u32[]{:S(2)}) collective-permute-start(bf16[32,4096]{1,0:T(8,128)(2,1)S(1)} %shard_map.103.refs_0_), channel_id=1, source_target_pairs={{0,4},{1,5},{2,6},{3,7},{4,0},{5,1},{6,2},{7,3},{8,12},{9,13},{10,... | collective-permute-start | bytes 786440 | tf_op jit(solution)/shard_map/ppermute | solution.py:265
  21.6 14.1 %collective-permute-start.4 = (bf16[32,4096]{1,0:T(8,128)(2,1)S(1)}, bf16[32,4096]{1,0:T(8,128)(2,1)S(1)}, u32[]{:S(2)}, u32[]{:S(2)}) collective-permute-start(bf16[32,4096]{1,0:T(8,128)(2,1)S(1)} %shard_map.103.refs_0_), channel_id=1, source_target_pairs={{0,2},{1,3},{2,0},{3,1},{4,6},{5,7},{6,4},{7,5},{8,10},{9,11},{10,... | collective-permute-start | bytes 786440 | tf_op jit(solution)/shard_map/ppermute | solution.py:265
  23.1 12.5 %collective-permute-start.5 = (bf16[32,4096]{1,0:T(8,128)(2,1)S(1)}, bf16[32,4096]{1,0:T(8,128)(2,1)S(1)}, u32[]{:S(2)}, u32[]{:S(2)}) collective-permute-start(bf16[32,4096]{1,0:T(8,128)(2,1)S(1)} %shard_map.103.refs_0_), channel_id=1, source_target_pairs={{0,6},{1,7},{2,4},{3,5},{4,2},{5,3},{6,0},{7,1},{8,14},{9,15},{10,... | collective-permute-start | bytes 786440 | tf_op jit(solution)/shard_map/ppermute | solution.py:265
  30.5 13.9 %copy-start.3 = (bf16[32,4096]{1,0:T(8,128)(2,1)S(1)}, bf16[32,4096]{1,0:T(8,128)(2,1)}, u32[]{:S(2)}) copy-start(bf16[32,4096]{1,0:T(8,128)(2,1)} %get-tuple-element.45.refs_0_) | copy-start | bytes 786436
  35.7 8.8 %collective-permute-start.7 = (bf16[32,4096]{1,0:T(8,128)(2,1)S(1)}, bf16[32,4096]{1,0:T(8,128)(2,1)S(1)}, u32[]{:S(2)}, u32[]{:S(2)}) collective-permute-start(bf16[32,4096]{1,0:T(8,128)(2,1)S(1)} %collective-permute-done.1.refs_1_), channel_id=1, source_target_pairs={{0,2},{1,3},{2,0},{3,1},{4,6},{5,7},{6,4},{7,5},{8,10},{9,11},{10,... | collective-permute-start | bytes 786440 | tf_op jit(solution)/shard_map/ppermute | solution.py:265
  40.2 7.3 %collective-permute-start.8 = (bf16[16,4096]{1,0:T(8,128)(2,1)S(1)}, bf16[16,4096]{1,0:T(8,128)(2,1)S(1)}, u32[]{:S(2)}, u32[]{:S(2)}) collective-permute-start(bf16[16,4096]{1,0:T(8,128)(2,1)S(1)} %get-tuple-element.62), channel_id=1, source_target_pairs={{0,4},{1,5},{2,6},{3,7},{4,0},{5,1},{6,2},{7,3},{8,12},{9,13},{10,... | collective-permute-start | bytes 393224 | tf_op jit(solution)/shard_map/ppermute | solution.py:265
  40.9 8.1 %collective-permute-start.9 = (bf16[16,4096]{1,0:T(8,128)(2,1)S(1)}, bf16[16,4096]{1,0:T(8,128)(2,1)S(1)}, u32[]{:S(2)}, u32[]{:S(2)}) collective-permute-start(bf16[16,4096]{1,0:T(8,128)(2,1)S(1)} %get-tuple-element.63), channel_id=1, source_target_pairs={{0,2},{1,3},{2,0},{3,1},{4,6},{5,7},{6,4},{7,5},{8,10},{9,11},{10,... | collective-permute-start | bytes 393224 | tf_op jit(solution)/shard_map/ppermute | solution.py:265
  42.0 7.0 %collective-permute-start.10 = (bf16[16,4096]{1,0:T(8,128)(2,1)S(1)}, bf16[16,4096]{1,0:T(8,128)(2,1)S(1)}, u32[]{:S(2)}, u32[]{:S(2)}) collective-permute-start(bf16[16,4096]{1,0:T(8,128)(2,1)S(1)} %get-tuple-element.64), channel_id=1, source_target_pairs={{0,6},{1,7},{2,4},{3,5},{4,2},{5,3},{6,0},{7,1},{8,14},{9,15},{10,... | collective-permute-start | bytes 393224 | tf_op jit(solution)/shard_map/ppermute | solution.py:265
  43.8 9.0 %collective-permute-start.14 = (bf16[192,4096]{1,0:T(8,128)(2,1)S(1)}, bf16[192,4096]{1,0:T(8,128)(2,1)S(1)}, u32[]{:S(2)}, u32[]{:S(2)}) collective-permute-start(bf16[192,4096]{1,0:T(8,128)(2,1)S(1)} %get-tuple-element.74.refs_4_), channel_id=1, source_target_pairs={{0,1},{1,0},{2,3},{3,2},{4,5},{5,4},{6,7},{7,6},{8,9},{9,8},{10,11... | collective-permute-start | bytes 4718600 | tf_op jit(solution)/shard_map/ppermute | solution.py:265
  49.1 5.9 %collective-permute-start.15 = (bf16[192,4096]{1,0:T(8,128)(2,1)S(1)}, bf16[192,4096]{1,0:T(8,128)(2,1)S(1)}, u32[]{:S(2)}, u32[]{:S(2)}) collective-permute-start(bf16[192,4096]{1,0:T(8,128)(2,1)S(1)} %get-tuple-element.76.refs_6_), channel_id=1, source_target_pairs={{0,1},{1,0},{2,3},{3,2},{4,5},{5,4},{6,7},{7,6},{8,9},{9,8},{10,11... | collective-permute-start | bytes 4718600 | tf_op jit(solution)/shard_map/ppermute | solution.py:265
  49.2 9.3 %collective-permute-start.11 = (bf16[16,4096]{1,0:T(8,128)(2,1)S(1)}, bf16[16,4096]{1,0:T(8,128)(2,1)S(1)}, u32[]{:S(2)}, u32[]{:S(2)}) collective-permute-start(bf16[16,4096]{1,0:T(8,128)(2,1)S(1)} %get-tuple-element.70), channel_id=1, source_target_pairs={{0,4},{1,5},{2,6},{3,7},{4,0},{5,1},{6,2},{7,3},{8,12},{9,13},{10,... | collective-permute-start | bytes 393224 | tf_op jit(solution)/shard_map/ppermute | solution.py:265
  50.7 10.9 %collective-permute-start.12 = (bf16[16,4096]{1,0:T(8,128)(2,1)S(1)}, bf16[16,4096]{1,0:T(8,128)(2,1)S(1)}, u32[]{:S(2)}, u32[]{:S(2)}) collective-permute-start(bf16[16,4096]{1,0:T(8,128)(2,1)S(1)} %get-tuple-element.71), channel_id=1, source_target_pairs={{0,6},{1,7},{2,4},{3,5},{4,2},{5,3},{6,0},{7,1},{8,14},{9,15},{10,... | collective-permute-start | bytes 393224 | tf_op jit(solution)/shard_map/ppermute | solution.py:265
  52.1 9.4 %collective-permute-start.13 = (bf16[16,4096]{1,0:T(8,128)(2,1)S(1)}, bf16[16,4096]{1,0:T(8,128)(2,1)S(1)}, u32[]{:S(2)}, u32[]{:S(2)}) collective-permute-start(bf16[16,4096]{1,0:T(8,128)(2,1)S(1)} %get-tuple-element.72), channel_id=1, source_target_pairs={{0,2},{1,3},{2,0},{3,1},{4,6},{5,7},{6,4},{7,5},{8,10},{9,11},{10,... | collective-permute-start | bytes 393224 | tf_op jit(solution)/shard_map/ppermute | solution.py:265
  52.7 8.9 %collective-permute-start.16 = (bf16[16,4096]{1,0:T(8,128)(2,1)S(1)}, bf16[16,4096]{1,0:T(8,128)(2,1)S(1)}, u32[]{:S(2)}, u32[]{:S(2)}) collective-permute-start(bf16[16,4096]{1,0:T(8,128)(2,1)S(1)} %shard_map.108), channel_id=1, source_target_pairs={{0,8},{1,9},{2,10},{3,11},{4,12},{5,13},{6,14},{7,15},{8,0},{9,1},... | collective-permute-start | bytes 393224 | tf_op jit(solution)/shard_map/ppermute | solution.py:268
  55.0 6.6 %copy-start.4 = (bf16[32,128]{1,0:T(8,128)(2,1)S(1)}, bf16[32,128]{1,0:T(8,128)(2,1)}, u32[]{:S(2)}) copy-start(bf16[32,128]{1,0:T(8,128)(2,1)} %get-tuple-element.44.select_ref) | copy-start | bytes 24580

commit v6 on v5

--- a/solution.py
+++ b/solution.py
@@ -203,20 +203,22 @@
     out[...] = source[...]
 
 
-def turn_kernel(mine_ref, other_ref, out_ref):
-    hidden, width = mine_ref.shape[0] // 3, mine_ref.shape[1]
+def turn_kernel(*refs):
+    mine, other, out_ref = refs[:2], refs[2:4], refs[4]
+    hidden, width = mine[1].shape
     step = min(STEP // 2, width)
     for m in range(3):
-        part = slice(m * hidden, (m + 1) * hidden)
+        part = slice((m % 2) * hidden, (m % 2 + 1) * hidden)
         for at in range(0, width, step):
             cols = pl.ds(at, step)
-            rows = jnp.concatenate([mine_ref[part, cols], other_ref[part, cols]], axis=0)
+            rows = jnp.concatenate([pair[m // 2][part, cols] for pair in (mine, other)], axis=0)
             out_ref[at : at + step, 2 * m * hidden : 2 * (m + 1) * hidden] = rows.T
 
 
-def fetch_kernel(gate_ref, up_ref, down_ref, out_ref):
-    rows = gate_ref.shape[0]
-    for m, ref in enumerate((gate_ref, up_ref, down_ref)):
+def fetch_kernel(*refs):
+    *sources, out_ref = refs
+    rows = sources[0].shape[0]
+    for m, ref in enumerate(sources):
         out_ref[m * rows : (m + 1) * rows, :] = ref[...]
 
 
@@ -279,20 +281,22 @@
         return call(
             functools.partial(expert_kernel, len(blocks), hidden),
             [shape(3 * rows, width), shape(rows, 3 * padded(hidden))] + [shape(CAP, width)] * len(blocks),
-            *blocks, turned, weights, sibling,
+            *blocks, turned, weights[0], sibling[0],
         )
 
     select, *packed = pack(window, own, expert_ids.T, gate_values.T, tokens, upstream)
     crossed = [turn(packed[k], k) for k in range(1, window)]
     mine = packed[0]
     along, across = swap(mine, 4), swap(mine, 2)
-    weights = call(
-        fetch_kernel, shape(3 * hidden, width), *later([w_gate[0], w_up[0], w_down[0]], select)
-    )
+    gate, up, down = later([w_gate[0], w_up[0], w_down[0]], select)
+    weights = [
+        call(fetch_kernel, shape(2 * hidden, width), gate, up),
+        call(fetch_kernel, shape(hidden, width), down),
+    ]
     crossed = [call(copy_kernel, shape(*c.shape), c, mib=4) for c in crossed]
-    *crossed, along, across, weights = later([*crossed, along, across, weights])
-    sibling = swap(weights, 1)
-    turned = call(turn_kernel, shape(width, 6 * hidden), weights, sibling)
+    *crossed, along, across, weights[0], weights[1] = later([*crossed, along, across, *weights])
+    sibling = [swap(w, 1) for w in weights]
+    turned = call(turn_kernel, shape(width, 6 * hidden), *weights, *sibling)
 
     def send(pieces, order=(4, 2, 6)):
         return [pieces[0]] + [swap(piece, bits) for piece, bits in zip(pieces[1:], order)]

time: 63 us -> 61.8 us (0.981)
  local copies, waits for them, and re-layouts: 2.83 us -> 1.79 us
  waiting for transfers between devices: 21 us -> 20 us
  starting transfers between devices: 21.7 us -> 22.4 us
    ppermute x15 -> x16, waiting for transfers between devices: 14.9 us -> 13 us  [swap(): return lax.ppermute(a, 'exp', [(i, i ^ bits) for i in range(devices)])]
    unnamed x10, local copies, waits for them, and re-layouts: 2.83 us -> 1.79 us
    ppermute x2, waiting for transfers between devices: 6.02 us -> 7.06 us  [turn(): lax.ppermute(a, 'exp', [(i, (i + k * TILES) % devices) for i in range(dev...]
    ppermute x15 -> x16, starting transfers between devices: 15.3 us -> 15.8 us  [swap(): return lax.ppermute(a, 'exp', [(i, i ^ bits) for i in range(devices)])]
    pallas_call x7 -> x8, Pallas kernels: 9.04 us -> 9.04 us  [call(): pl.pallas_call(kernel, out_shape=out_shape, in_specs=[VMEM] * len(args),...]
  transfers between devices with their start and end apart: 17 -> 18, of which waited for: 7 -> 7; matrix products, arithmetic and copies ran while one was open for 0% -> 0% of each run, Pallas kernels for 20% -> 20%
where the time goes in v6:
time: 61.8 us; the launch traced here: 61.6 us
  starting transfers between devices  22.4 us (36%)
  waiting for transfers between devices  20 us (32%)
  Pallas kernels  16.6 us (27%)
  local copies, waits for them, and re-layouts  1.79 us (3%)
  between operations  0.77 us (1%)
    ppermute x16, starting transfers between devices, swap(): return lax.ppermute(a, 'exp', [(i, i ^ bits) for i in range(devices)])  15.8 us
    ppermute x16, waiting for transfers between devices, swap(): return lax.ppermute(a, 'exp', [(i, i ^ bits) for i in range(devices)])  13 us
    pallas_call x8, Pallas kernels, call(): pl.pallas_call(kernel, out_shape=out_shape, in_specs=[VMEM] * len(args),...  9.04 us
    ppermute x2, waiting for transfers between devices, turn(): lax.ppermute(a, 'exp', [(i, (i + k * TILES) % devices) for i in range(dev...  7.06 us
    ppermute x2, starting transfers between devices, turn(): lax.ppermute(a, 'exp', [(i, (i + k * TILES) % devices) for i in range(dev...  6.64 us
    pallas_call x1, Pallas kernels, grads(): pl.pallas_call(functools.partial(grad_kernel, count), grid=(width // step...  3.43 us
    pallas_call x1, Pallas kernels, pack(): pl.pallas_call(functools.partial(pack_kernel, window), out_shape=outs, in...  2.9 us
    unnamed x10, local copies, waits for them, and re-layouts  1.79 us
  transfers between devices with their start and end apart: 18, of which 7 were waited for; matrix products, arithmetic and copies ran while one was open for 0% of the time, Pallas kernels for 20%

profile of v6, /device:TPU:0, one launch (start us, length us, event | category | flops | bytes accessed | tf_op | source)
XLA Modules:
  0.0 61.6 jit_solution(10304849034324873526)
XLA Ops:
  0.7 2.9 %shard_map.102 = (bf16[32,128]{1,0:T(8,128)(2,1)}, bf16[32,4096]{1,0:T(8,128)(2,1)}, bf16[32,4096]{1,0:T(8,128)(2,1)}) custom-call(s32[1]{0:T(128)} %bitcast.own_ref, s32[8,128]{1,0:T(8,128)} %bitcast.12, f32[8,128]{1,0:T(8,128)} %bitcast.13, bf16[128,4096]{1,0:T(8,128)(2,1)} %tokens_hbm.1, bf16[128,4096]{1,0:T(8,128)(2,1)} %upstream_hbm.1), custom_call_target="tpu_custom_call" | custom-call | tf_op jit(solution)/shard_map/pallas_call | solution.py:185
  3.6 4.1 %collective-permute-start = (bf16[32,4096]{1,0:T(8,128)(2,1)}, bf16[32,4096]{1,0:T(8,128)(2,1)S(1)}, u32[]{:S(2)}, u32[]{:S(2)}) collective-permute-start(bf16[32,4096]{1,0:T(8,128)(2,1)} %get-tuple-element.47), channel_id=1, source_target_pairs={{0,8},{1,9},{2,10},{3,11},{4,12},{5,13},{6,14},{7,15},{8,0},{9,1},... | collective-permute-start | bytes 786440 | tf_op jit(solution)/shard_map/ppermute | solution.py:270
  7.7 1.6 %collective-permute-start.1 = (bf16[32,4096]{1,0:T(8,128)(2,1)}, bf16[32,4096]{1,0:T(8,128)(2,1)S(1)}, u32[]{:S(2)}, u32[]{:S(2)}) collective-permute-start(bf16[32,4096]{1,0:T(8,128)(2,1)} %get-tuple-element.46.refs_0_), channel_id=1, source_target_pairs={{0,4},{1,5},{2,6},{3,7},{4,0},{5,1},{6,2},{7,3},{8,12},{9,13},{10,... | collective-permute-start | bytes 786440 | tf_op jit(solution)/shard_map/ppermute | solution.py:267
  9.2 1.5 %collective-permute-start.2 = (bf16[32,4096]{1,0:T(8,128)(2,1)}, bf16[32,4096]{1,0:T(8,128)(2,1)S(1)}, u32[]{:S(2)}, u32[]{:S(2)}) collective-permute-start(bf16[32,4096]{1,0:T(8,128)(2,1)} %get-tuple-element.46.refs_0_), channel_id=1, source_target_pairs={{0,2},{1,3},{2,0},{3,1},{4,6},{5,7},{6,4},{7,5},{8,10},{9,11},{10,... | collective-permute-start | bytes 786440 | tf_op jit(solution)/shard_map/ppermute | solution.py:267
  10.8 0.1 shard_map.105.refs_1_
  10.9 1.3 %copy-done.1 = bf16[1,192,4096]{2,1,0:T(8,128)(2,1)S(1)} copy-done((bf16[1,192,4096]{2,1,0:T(8,128)(2,1)S(1)}, bf16[1,192,4096]{2,1,0:T(8,128)(2,1)}, u32[]{:S(2)}) %copy-start.1) | copy-done | bytes 1572888
  12.2 0.5 copy-done.2
  12.6 0.2 shard_map.104.refs_0_.refs_5_
  12.9 7.1 %collective-permute-done.source = bf16[32,4096]{1,0:T(8,128)(2,1)S(1)} collective-permute-done((bf16[32,4096]{1,0:T(8,128)(2,1)}, bf16[32,4096]{1,0:T(8,128)(2,1)S(1)}, u32[]{:S(2)}, u32[]{:S(2)}) %collective-permute-start) | collective-permute-done | bytes 262176 | tf_op jit(solution)/shard_map/ppermute | solution.py:270
  19.9 0.2 collective-permute-done.1.refs_1_
  20.1 0.5 collective-permute-start.7
  20.6 1.5 %collective-permute-start.3 = (bf16[32,4096]{1,0:T(8,128)(2,1)S(1)}, bf16[32,4096]{1,0:T(8,128)(2,1)S(1)}, u32[]{:S(2)}, u32[]{:S(2)}) collective-permute-start(bf16[32,4096]{1,0:T(8,128)(2,1)S(1)} %shard_map.103.refs_0_), channel_id=1, source_target_pairs={{0,4},{1,5},{2,6},{3,7},{4,0},{5,1},{6,2},{7,3},{8,12},{9,13},{10,... | collective-permute-start | bytes 786440 | tf_op jit(solution)/shard_map/ppermute | solution.py:267
  22.1 1.5 %collective-permute-start.4 = (bf16[32,4096]{1,0:T(8,128)(2,1)S(1)}, bf16[32,4096]{1,0:T(8,128)(2,1)S(1)}, u32[]{:S(2)}, u32[]{:S(2)}) collective-permute-start(bf16[32,4096]{1,0:T(8,128)(2,1)S(1)} %shard_map.103.refs_0_), channel_id=1, source_target_pairs={{0,2},{1,3},{2,0},{3,1},{4,6},{5,7},{6,4},{7,5},{8,10},{9,11},{10,... | collective-permute-start | bytes 786440 | tf_op jit(solution)/shard_map/ppermute | solution.py:267
  23.6 0.5 collective-permute-start.5
  24.1 3.9 %collective-permute-done.7.refs_3_ = bf16[192,4096]{1,0:T(8,128)(2,1)S(1)} collective-permute-done((bf16[192,4096]{1,0:T(8,128)(2,1)S(1)}, bf16[192,4096]{1,0:T(8,128)(2,1)S(1)}, u32[]{:S(2)}, u32[]{:S(2)}) %collective-permute-start.7) | collective-permute-done | bytes 1572896 | tf_op jit(solution)/shard_map/ppermute | solution.py:267
  28.0 2.5 %shard_map.106.refs_4_ = bf16[4096,1152]{1,0:T(8,128)(2,1)S(1)} custom-call(bf16[384,4096]{1,0:T(8,128)(2,1)S(1)} %shard_map.104.refs_0_.refs_5_, bf16[192,4096]{1,0:T(8,128)(2,1)S(1)} %shard_map.105.refs_1_, bf16[384,4096]{1,0:T(8,128)(2,1)S(1)} %collective-permute-done.6.refs_2_.refs_6_, bf16[192,4096]{1,0:T(8,128)(2,1)S(1)} %collective-permute-done.7.refs_3_), custom_call_target="tpu_custom_call" | custom-call | tf_op jit(solution)/shard_map/pallas_call | solution.py:161
  30.5 5.1 %collective-permute-done.4.refs_2_ = bf16[32,4096]{1,0:T(8,128)(2,1)S(1)} collective-permute-done((bf16[32,4096]{1,0:T(8,128)(2,1)S(1)}, bf16[32,4096]{1,0:T(8,128)(2,1)S(1)}, u32[]{:S(2)}, u32[]{:S(2)}) %collective-permute-start.4) | collective-permute-done | bytes 262176 | tf_op jit(solution)/shard_map/ppermute | solution.py:267
  35.7 1.5 %collective-permute-start.8 = (bf16[32,4096]{1,0:T(8,128)(2,1)S(1)}, bf16[32,4096]{1,0:T(8,128)(2,1)S(1)}, u32[]{:S(2)}, u32[]{:S(2)}) collective-permute-start(bf16[32,4096]{1,0:T(8,128)(2,1)S(1)} %collective-permute-done.1.refs_1_), channel_id=1, source_target_pairs={{0,2},{1,3},{2,0},{3,1},{4,6},{5,7},{6,4},{7,5},{8,10},{9,11},{10,... | collective-permute-start | bytes 786440 | tf_op jit(solution)/shard_map/ppermute | solution.py:267
  37.2 3.0 %shard_map.108 = (bf16[192,4096]{1,0:T(8,128)(2,1)S(1)}, bf16[64,768]{1,0:T(8,128)(2,1)S(1)}, bf16[16,4096]{1,0:T(8,128)(2,1)S(1)}, bf16[16,4096]{1,0:T(8,128)(2...) custom-call(bf16[32,4096]{1,0:T(8,128)(2,1)S(1)} %shard_map.103.refs_0_, ...), custom_call_target="tpu_custom_call" | custom-call | tf_op jit(solution)/shard_map/pallas_call | solution.py:161
  40.2 0.7 %collective-permute-start.9 = (bf16[16,4096]{1,0:T(8,128)(2,1)S(1)}, bf16[16,4096]{1,0:T(8,128)(2,1)S(1)}, u32[]{:S(2)}, u32[]{:S(2)}) collective-permute-start(bf16[16,4096]{1,0:T(8,128)(2,1)S(1)} %get-tuple-element.64), channel_id=1, source_target_pairs={{0,4},{1,5},{2,6},{3,7},{4,0},{5,1},{6,2},{7,3},{8,12},{9,13},{10,... | collective-permute-start | bytes 393224 | tf_op jit(solution)/shard_map/ppermute | solution.py:267
  40.9 1.1 %collective-permute-start.10 = (bf16[16,4096]{1,0:T(8,128)(2,1)S(1)}, bf16[16,4096]{1,0:T(8,128)(2,1)S(1)}, u32[]{:S(2)}, u32[]{:S(2)}) collective-permute-start(bf16[16,4096]{1,0:T(8,128)(2,1)S(1)} %get-tuple-element.65), channel_id=1, source_target_pairs={{0,2},{1,3},{2,0},{3,1},{4,6},{5,7},{6,4},{7,5},{8,10},{9,11},{10,... | collective-permute-start | bytes 393224 | tf_op jit(solution)/shard_map/ppermute | solution.py:267
  42.0 1.8 %collective-permute-start.11 = (bf16[16,4096]{1,0:T(8,128)(2,1)S(1)}, bf16[16,4096]{1,0:T(8,128)(2,1)S(1)}, u32[]{:S(2)}, u32[]{:S(2)}) collective-permute-start(bf16[16,4096]{1,0:T(8,128)(2,1)S(1)} %get-tuple-element.66), channel_id=1, source_target_pairs={{0,6},{1,7},{2,4},{3,5},{4,2},{5,3},{6,0},{7,1},{8,14},{9,15},{10,... | collective-permute-start | bytes 393224 | tf_op jit(solution)/shard_map/ppermute | solution.py:267
  43.8 0.3 collective-permute-done.8.refs_2_
  44.1 3.1 %shard_map.107 = (bf16[192,4096]{1,0:T(8,128)(2,1)S(1)}, bf16[64,768]{1,0:T(8,128)(2,1)S(1)}, bf16[16,4096]{1,0:T(8,128)(2,1)S(1)}, bf16[16,4096]{1,0:T(8,128)(2...) custom-call(bf16[32,4096]{1,0:T(8,128)(2,1)S(1)} %copy-done.3, ...), custom_call_target="tpu_custom_call" | custom-call | tf_op jit(solution)/shard_map/pallas_call | solution.py:161
  47.2 1.3 %collective-permute-done.10.refs_2_ = bf16[16,4096]{1,0:T(8,128)(2,1)S(1)} collective-permute-done((bf16[16,4096]{1,0:T(8,128)(2,1)S(1)}, bf16[16,4096]{1,0:T(8,128)(2,1)S(1)}, u32[]{:S(2)}, u32[]{:S(2)}) %collective-permute-start.10) | collective-permute-done | bytes 131104 | tf_op jit(solution)/shard_map/ppermute | solution.py:267
  48.7 1.7 %collective-permute-start.12 = (bf16[16,4096]{1,0:T(8,128)(2,1)S(1)}, bf16[16,4096]{1,0:T(8,128)(2,1)S(1)}, u32[]{:S(2)}, u32[]{:S(2)}) collective-permute-start(bf16[16,4096]{1,0:T(8,128)(2,1)S(1)} %get-tuple-element.72), channel_id=1, source_target_pairs={{0,4},{1,5},{2,6},{3,7},{4,0},{5,1},{6,2},{7,3},{8,12},{9,13},{10,... | collective-permute-start | bytes 393224 | tf_op jit(solution)/shard_map/ppermute | solution.py:267
  50.4 0.5 collective-permute-start.13
  50.8 1.4 %collective-permute-start.14 = (bf16[16,4096]{1,0:T(8,128)(2,1)S(1)}, bf16[16,4096]{1,0:T(8,128)(2,1)S(1)}, u32[]{:S(2)}, u32[]{:S(2)}) collective-permute-start(bf16[16,4096]{1,0:T(8,128)(2,1)S(1)} %get-tuple-element.74), channel_id=1, source_target_pairs={{0,2},{1,3},{2,0},{3,1},{4,6},{5,7},{6,4},{7,5},{8,10},{9,11},{10,... | collective-permute-start | bytes 393224 | tf_op jit(solution)/shard_map/ppermute | solution.py:267
  52.2 2.5 %collective-permute-start.17 = (bf16[16,4096]{1,0:T(8,128)(2,1)S(1)}, bf16[16,4096]{1,0:T(8,128)(2,1)S(1)}, u32[]{:S(2)}, u32[]{:S(2)}) collective-permute-start(bf16[16,4096]{1,0:T(8,128)(2,1)S(1)} %shard_map.109), channel_id=1, source_target_pairs={{0,8},{1,9},{2,10},{3,11},{4,12},{5,13},{6,14},{7,15},{8,0},{9,1},... | collective-permute-start | bytes 393224 | tf_op jit(solution)/shard_map/ppermute | solution.py:270
  54.8 3.4 %shard_map.110 = (bf16[192,4096]{1,0:T(8,128)(2,1)}, bf16[192,4096]{1,0:T(8,128)(2,1)}, bf16[192,4096]{1,0:T(8,128)(2,1)}) custom-call(bf16[64,768]{1,0:T(8,128)(2,1)S(1)} %get-tuple-element.75.refs_0_, bf16[192,4096]{1,0:T(8,128)(2,1)S(1)} %collective-permute-done.15.refs_1_.refs_5_, bf16[64,768]{1,0:T(8,128)(2,1)S(1)} %get-tuple-element.77.refs_2_, ...), custom_call_target="tpu_custom_call" | custom-call | tf_op jit(solution)/shard_map/pallas_call | solution.py:234
  58.2 2.1 %collective-permute-done.13.refs_2_ = bf16[16,4096]{1,0:T(8,128)(2,1)S(1)} collective-permute-done((bf16[16,4096]{1,0:T(8,128)(2,1)S(1)}, bf16[16,4096]{1,0:T(8,128)(2,1)S(1)}, u32[]{:S(2)}, u32[]{:S(2)}) %collective-permute-start.13) | collective-permute-done | bytes 131104 | tf_op jit(solution)/shard_map/ppermute | solution.py:267
  60.4 1.2 %shard_map.112 = bf16[128,4096]{1,0:T(8,128)(2,1)} custom-call(bf16[32,128]{1,0:T(8,128)(2,1)S(1)} %copy-done.4, bf16[16,4096]{1,0:T(8,128)(2,1)S(1)} %shard_map.111.refs_0_, bf16[16,4096]{1,0:T(8,128)(2,1)S(1)} %collective-permute-done.17.refs_1_), custom_call_target="tpu_custom_call" | custom-call | tf_op jit(solution)/shard_map/pallas_call | solution.py:246
  (25 shorter events, 0.3 us)
Async XLA Ops:
  0.6 10.1 %copy-start = (bf16[1,192,4096]{2,1,0:T(8,128)(2,1)S(1)}, bf16[1,192,4096]{2,1,0:T(8,128)(2,1)}, u32[]{:S(2)}) copy-start(bf16[1,192,4096]{2,1,0:T(8,128)(2,1)} %param.13) | copy-start | bytes 4718596
  3.6 16.3 %collective-permute-start = (bf16[32,4096]{1,0:T(8,128)(2,1)}, bf16[32,4096]{1,0:T(8,128)(2,1)S(1)}, u32[]{:S(2)}, u32[]{:S(2)}) collective-permute-start(bf16[32,4096]{1,0:T(8,128)(2,1)} %get-tuple-element.47), channel_id=1, source_target_pairs={{0,8},{1,9},{2,10},{3,11},{4,12},{5,13},{6,14},{7,15},{8,0},{9,1},... | collective-permute-start | bytes 786440 | tf_op jit(solution)/shard_map/ppermute | solution.py:270
  7.7 12.4 %collective-permute-start.1 = (bf16[32,4096]{1,0:T(8,128)(2,1)}, bf16[32,4096]{1,0:T(8,128)(2,1)S(1)}, u32[]{:S(2)}, u32[]{:S(2)}) collective-permute-start(bf16[32,4096]{1,0:T(8,128)(2,1)} %get-tuple-element.46.refs_0_), channel_id=1, source_target_pairs={{0,4},{1,5},{2,6},{3,7},{4,0},{5,1},{6,2},{7,3},{8,12},{9,13},{10,... | collective-permute-start | bytes 786440 | tf_op jit(solution)/shard_map/ppermute | solution.py:267
  9.2 10.9 %collective-permute-start.2 = (bf16[32,4096]{1,0:T(8,128)(2,1)}, bf16[32,4096]{1,0:T(8,128)(2,1)S(1)}, u32[]{:S(2)}, u32[]{:S(2)}) collective-permute-start(bf16[32,4096]{1,0:T(8,128)(2,1)} %get-tuple-element.46.refs_0_), channel_id=1, source_target_pairs={{0,2},{1,3},{2,0},{3,1},{4,6},{5,7},{6,4},{7,5},{8,10},{9,11},{10,... | collective-permute-start | bytes 786440 | tf_op jit(solution)/shard_map/ppermute | solution.py:267
  10.8 1.4 %copy-start.1 = (bf16[1,192,4096]{2,1,0:T(8,128)(2,1)S(1)}, bf16[1,192,4096]{2,1,0:T(8,128)(2,1)}, u32[]{:S(2)}) copy-start(bf16[1,192,4096]{2,1,0:T(8,128)(2,1)} %param.11) | copy-start | bytes 4718596
  10.8 1.9 %copy-start.2 = (bf16[1,192,4096]{2,1,0:T(8,128)(2,1)S(1)}, bf16[1,192,4096]{2,1,0:T(8,128)(2,1)}, u32[]{:S(2)}) copy-start(bf16[1,192,4096]{2,1,0:T(8,128)(2,1)} %param.12) | copy-start | bytes 4718596
  20.1 7.9 %collective-permute-start.6 = (bf16[384,4096]{1,0:T(8,128)(2,1)S(1)}, bf16[384,4096]{1,0:T(8,128)(2,1)S(1)}, u32[]{:S(2)}, u32[]{:S(2)}) collective-permute-start(bf16[384,4096]{1,0:T(8,128)(2,1)S(1)} %shard_map.104.refs_0_.refs_5_), channel_id=1, source_target_pairs={{0,1},{1,0},{2,3},{3,2},{4,5},{5,4},{6,7},{7,6},{8,9},{9,8},{10,11... | collective-permute-start | bytes 9437192 | tf_op jit(solution)/shard_map/ppermute | solution.py:267
  20.1 7.9 %collective-permute-start.7 = (bf16[192,4096]{1,0:T(8,128)(2,1)S(1)}, bf16[192,4096]{1,0:T(8,128)(2,1)S(1)}, u32[]{:S(2)}, u32[]{:S(2)}) collective-permute-start(bf16[192,4096]{1,0:T(8,128)(2,1)S(1)} %shard_map.105.refs_1_), channel_id=1, source_target_pairs={{0,1},{1,0},{2,3},{3,2},{4,5},{5,4},{6,7},{7,6},{8,9},{9,8},{10,11... | collective-permute-start | bytes 4718600 | tf_op jit(solution)/shard_map/ppermute | solution.py:267
  20.6 9.9 %collective-permute-start.3 = (bf16[32,4096]{1,0:T(8,128)(2,1)S(1)}, bf16[32,4096]{1,0:T(8,128)(2,1)S(1)}, u32[]{:S(2)}, u32[]{:S(2)}) collective-permute-start(bf16[32,4096]{1,0:T(8,128)(2,1)S(1)} %shard_map.103.refs_0_), channel_id=1, source_target_pairs={{0,4},{1,5},{2,6},{3,7},{4,0},{5,1},{6,2},{7,3},{8,12},{9,13},{10,... | collective-permute-start | bytes 786440 | tf_op jit(solution)/shard_map/ppermute | solution.py:267
  22.1 13.6 %collective-permute-start.4 = (bf16[32,4096]{1,0:T(8,128)(2,1)S(1)}, bf16[32,4096]{1,0:T(8,128)(2,1)S(1)}, u32[]{:S(2)}, u32[]{:S(2)}) collective-permute-start(bf16[32,4096]{1,0:T(8,128)(2,1)S(1)} %shard_map.103.refs_0_), channel_id=1, source_target_pairs={{0,2},{1,3},{2,0},{3,1},{4,6},{5,7},{6,4},{7,5},{8,10},{9,11},{10,... | collective-permute-start | bytes 786440 | tf_op jit(solution)/shard_map/ppermute | solution.py:267
  23.6 12.0 %collective-permute-start.5 = (bf16[32,4096]{1,0:T(8,128)(2,1)S(1)}, bf16[32,4096]{1,0:T(8,128)(2,1)S(1)}, u32[]{:S(2)}, u32[]{:S(2)}) collective-permute-start(bf16[32,4096]{1,0:T(8,128)(2,1)S(1)} %shard_map.103.refs_0_), channel_id=1, source_target_pairs={{0,6},{1,7},{2,4},{3,5},{4,2},{5,3},{6,0},{7,1},{8,14},{9,15},{10,... | collective-permute-start | bytes 786440 | tf_op jit(solution)/shard_map/ppermute | solution.py:267
  30.5 13.6 %copy-start.3 = (bf16[32,4096]{1,0:T(8,128)(2,1)S(1)}, bf16[32,4096]{1,0:T(8,128)(2,1)}, u32[]{:S(2)}) copy-start(bf16[32,4096]{1,0:T(8,128)(2,1)} %get-tuple-element.46.refs_0_) | copy-start | bytes 786436
  35.7 8.5 %collective-permute-start.8 = (bf16[32,4096]{1,0:T(8,128)(2,1)S(1)}, bf16[32,4096]{1,0:T(8,128)(2,1)S(1)}, u32[]{:S(2)}, u32[]{:S(2)}) collective-permute-start(bf16[32,4096]{1,0:T(8,128)(2,1)S(1)} %collective-permute-done.1.refs_1_), channel_id=1, source_target_pairs={{0,2},{1,3},{2,0},{3,1},{4,6},{5,7},{6,4},{7,5},{8,10},{9,11},{10,... | collective-permute-start | bytes 786440 | tf_op jit(solution)/shard_map/ppermute | solution.py:267
  40.2 7.0 %collective-permute-start.9 = (bf16[16,4096]{1,0:T(8,128)(2,1)S(1)}, bf16[16,4096]{1,0:T(8,128)(2,1)S(1)}, u32[]{:S(2)}, u32[]{:S(2)}) collective-permute-start(bf16[16,4096]{1,0:T(8,128)(2,1)S(1)} %get-tuple-element.64), channel_id=1, source_target_pairs={{0,4},{1,5},{2,6},{3,7},{4,0},{5,1},{6,2},{7,3},{8,12},{9,13},{10,... | collective-permute-start | bytes 393224 | tf_op jit(solution)/shard_map/ppermute | solution.py:267
  40.9 7.6 %collective-permute-start.10 = (bf16[16,4096]{1,0:T(8,128)(2,1)S(1)}, bf16[16,4096]{1,0:T(8,128)(2,1)S(1)}, u32[]{:S(2)}, u32[]{:S(2)}) collective-permute-start(bf16[16,4096]{1,0:T(8,128)(2,1)S(1)} %get-tuple-element.65), channel_id=1, source_target_pairs={{0,2},{1,3},{2,0},{3,1},{4,6},{5,7},{6,4},{7,5},{8,10},{9,11},{10,... | collective-permute-start | bytes 393224 | tf_op jit(solution)/shard_map/ppermute | solution.py:267
  42.0 6.5 %collective-permute-start.11 = (bf16[16,4096]{1,0:T(8,128)(2,1)S(1)}, bf16[16,4096]{1,0:T(8,128)(2,1)S(1)}, u32[]{:S(2)}, u32[]{:S(2)}) collective-permute-start(bf16[16,4096]{1,0:T(8,128)(2,1)S(1)} %get-tuple-element.66), channel_id=1, source_target_pairs={{0,6},{1,7},{2,4},{3,5},{4,2},{5,3},{6,0},{7,1},{8,14},{9,15},{10,... | collective-permute-start | bytes 393224 | tf_op jit(solution)/shard_map/ppermute | solution.py:267
  43.8 8.4 %collective-permute-start.15 = (bf16[192,4096]{1,0:T(8,128)(2,1)S(1)}, bf16[192,4096]{1,0:T(8,128)(2,1)S(1)}, u32[]{:S(2)}, u32[]{:S(2)}) collective-permute-start(bf16[192,4096]{1,0:T(8,128)(2,1)S(1)} %get-tuple-element.76.refs_4_), channel_id=1, source_target_pairs={{0,1},{1,0},{2,3},{3,2},{4,5},{5,4},{6,7},{7,6},{8,9},{9,8},{10,11... | collective-permute-start | bytes 4718600 | tf_op jit(solution)/shard_map/ppermute | solution.py:267
  48.6 6.2 %collective-permute-start.16 = (bf16[192,4096]{1,0:T(8,128)(2,1)S(1)}, bf16[192,4096]{1,0:T(8,128)(2,1)S(1)}, u32[]{:S(2)}, u32[]{:S(2)}) collective-permute-start(bf16[192,4096]{1,0:T(8,128)(2,1)S(1)} %get-tuple-element.78.refs_6_), channel_id=1, source_target_pairs={{0,1},{1,0},{2,3},{3,2},{4,5},{5,4},{6,7},{7,6},{8,9},{9,8},{10,11... | collective-permute-start | bytes 4718600 | tf_op jit(solution)/shard_map/ppermute | solution.py:267
  48.7 9.5 %collective-permute-start.12 = (bf16[16,4096]{1,0:T(8,128)(2,1)S(1)}, bf16[16,4096]{1,0:T(8,128)(2,1)S(1)}, u32[]{:S(2)}, u32[]{:S(2)}) collective-permute-start(bf16[16,4096]{1,0:T(8,128)(2,1)S(1)} %get-tuple-element.72), channel_id=1, source_target_pairs={{0,4},{1,5},{2,6},{3,7},{4,0},{5,1},{6,2},{7,3},{8,12},{9,13},{10,... | collective-permute-start | bytes 393224 | tf_op jit(solution)/shard_map/ppermute | solution.py:267
  50.4 9.9 %collective-permute-start.13 = (bf16[16,4096]{1,0:T(8,128)(2,1)S(1)}, bf16[16,4096]{1,0:T(8,128)(2,1)S(1)}, u32[]{:S(2)}, u32[]{:S(2)}) collective-permute-start(bf16[16,4096]{1,0:T(8,128)(2,1)S(1)} %get-tuple-element.73), channel_id=1, source_target_pairs={{0,6},{1,7},{2,4},{3,5},{4,2},{5,3},{6,0},{7,1},{8,14},{9,15},{10,... | collective-permute-start | bytes 393224 | tf_op jit(solution)/shard_map/ppermute | solution.py:267
  50.8 9.4 %collective-permute-start.14 = (bf16[16,4096]{1,0:T(8,128)(2,1)S(1)}, bf16[16,4096]{1,0:T(8,128)(2,1)S(1)}, u32[]{:S(2)}, u32[]{:S(2)}) collective-permute-start(bf16[16,4096]{1,0:T(8,128)(2,1)S(1)} %get-tuple-element.74), channel_id=1, source_target_pairs={{0,2},{1,3},{2,0},{3,1},{4,6},{5,7},{6,4},{7,5},{8,10},{9,11},{10,... | collective-permute-start | bytes 393224 | tf_op jit(solution)/shard_map/ppermute | solution.py:267
  52.2 8.1 %collective-permute-start.17 = (bf16[16,4096]{1,0:T(8,128)(2,1)S(1)}, bf16[16,4096]{1,0:T(8,128)(2,1)S(1)}, u32[]{:S(2)}, u32[]{:S(2)}) collective-permute-start(bf16[16,4096]{1,0:T(8,128)(2,1)S(1)} %shard_map.109), channel_id=1, source_target_pairs={{0,8},{1,9},{2,10},{3,11},{4,12},{5,13},{6,14},{7,15},{8,0},{9,1},... | collective-permute-start | bytes 393224 | tf_op jit(solution)/shard_map/ppermute | solution.py:270
  54.8 5.6 %copy-start.4 = (bf16[32,128]{1,0:T(8,128)(2,1)S(1)}, bf16[32,128]{1,0:T(8,128)(2,1)}, u32[]{:S(2)}) copy-start(bf16[32,128]{1,0:T(8,128)(2,1)} %get-tuple-element.45.select_ref) | copy-start | bytes 24580
